TPU v7x, 128 devices: a whole 4x4x4 slice. The times are simulated.
128 devices in a mesh: row: 16 (over y, x), col: 8 (over z, core).
Axes of the slice: x: 4, y: 4, z: 4, core: 2. Of those that a mesh axis runs over, the one named last changes fastest.
Arguments:
- source_points: bfloat16 [64, 262144], P(None, 'row'), may hold values from -3 to 3
- target_points: bfloat16 [64, 1048576], P(None, 'col'), may hold values from -4 to 4
- source_mass: float32 [262144], P('row'), may hold values from 0.5 to 4
- target_mass: float32 [1048576], P('col'), may hold values from 0.5 to 4
- tile_cols: int32 [2048, 8, 4], P('row', 'col'), may hold values from 0 to 1023, as said below
- tile_counts: int32 [2048, 8], P('row', 'col'), may hold values from 1 to 4
Outputs:
- source_potential: float32 [262144], P('row')
- target_potential: float32 [1048576], P('col')
Inputs may be any that keep to these rules, and one draw needn't show every extreme that they name: `tile_cols`: for each row block and target shard the 4 entries are distinct; only the first tile_counts entries are live; every target block of every shard is live for some row block.
All inputs are finite; a program needn't handle non-finite values.
Results may differ from a plain program's by a relative error of at most 0.0003.
Values sent between devices are 32-bit elements; how exact they have to be, the bound alone decides.
No kernel may reach another device: no remote copies, remote signals or barrier semaphores. Data moves between devices by JAX's collectives and lax.ppermute only.
A program may use at most 192 MiB of HBM per device.

v0:
```python
import math

import jax
import jax.numpy as jnp
from jax import lax
from jax.sharding import PartitionSpec as P

ITERS = 2


very_negative = -1e30
first_epsilon = 0.5


def body(source_points, target_points, source_mass, target_mass, tile_cols, tile_counts):
    width, rows = source_points.shape
    tile = 128
    row_blocks = rows // tile
    target_cells = target_points.shape[1]
    target_blocks = target_cells // tile
    slots = tile_cols.shape[2]
    group = math.gcd(row_blocks, 16)
    steps = row_blocks // group
    src_half = 0.5 * jnp.sum(jnp.square(source_points.astype(jnp.float32)), axis=0)
    tgt_half = (0.5 * jnp.sum(jnp.square(target_points.astype(jnp.float32)), axis=0)).reshape(
        target_blocks, tile
    )
    tgt_tiles = target_points.reshape(width, target_blocks, tile)
    columns = tile_cols.reshape(steps, group, slots)
    alive = (jnp.arange(slots, dtype=jnp.int32)[None, None, :] < tile_counts[:, :, None]).reshape(
        steps, group, slots
    )
    step_ids = jnp.arange(steps, dtype=jnp.int32)
    source_sum = lax.psum(jnp.sum(source_mass), "row")
    target_sum = lax.psum(jnp.sum(target_mass), "col")
    log_a = jnp.log(source_mass) - jnp.log(source_sum)
    log_b = jnp.log(target_mass) - jnp.log(target_sum)
    log_b_tiles = log_b.reshape(target_blocks, tile)

    def cost(index, cols):
        start = index * group * tile
        block = lax.dynamic_slice_in_dim(source_points, start, group * tile, 1).reshape(
            width, group, tile
        )
        half = lax.dynamic_slice_in_dim(src_half, start, group * tile, 0).reshape(group, tile)
        picked = tgt_tiles[:, cols, :]
        inner = jnp.einsum("dgi,dgsj->gisj", block, picked, preferred_element_type=jnp.float32)
        return half[:, :, None, None] + tgt_half[cols][:, None, :, :] - inner

    def column_scores(index, cols, source_pot, epsilon):
        local = lax.dynamic_slice_in_dim(source_pot, index * group * tile, group * tile, 0).reshape(
            group, tile
        )
        return (local[:, :, None, None] - cost(index, cols)) / epsilon

    def column_max(source_pot, epsilon):

        def visit(carry, args):
            index, cols, live = args
            scores = jnp.where(
                live[:, None, :, None],
                column_scores(index, cols, source_pot, epsilon),
                very_negative,
            )
            update = jnp.max(scores, axis=1).reshape(group * slots, tile)
            return (carry.at[cols.reshape(-1)].max(update), None)

        start_top = jnp.full((target_blocks, tile), very_negative, jnp.float32)
        result, _ = lax.scan(visit, start_top, (step_ids, columns, alive))
        return result

    def column_sum(source_pot, epsilon, col_top):

        def visit(carry, args):
            index, cols, live = args
            scores = column_scores(index, cols, source_pot, epsilon)
            terms = jnp.where(live[:, None, :, None], jnp.exp(scores - col_top[cols][:, None]), 0.0)
            update = jnp.sum(terms, axis=1).reshape(group * slots, tile)
            return (carry.at[cols.reshape(-1)].add(update), None)

        result, _ = lax.scan(
            visit, jnp.zeros((target_blocks, tile), jnp.float32), (step_ids, columns, alive)
        )
        return result

    target_pot = jnp.zeros((target_cells,), jnp.float32)
    source_pot = jnp.zeros((rows,), jnp.float32)
    for step in range(ITERS):
        epsilon = first_epsilon * 0.5**step
        pot_tiles = target_pot.reshape(target_blocks, tile)

        def row_visit(args):
            index, cols, live = args
            masked = live[:, None, :, None]
            scores = jnp.where(
                masked, (pot_tiles[cols][:, None] - cost(index, cols)) / epsilon, very_negative
            )
            highest = jnp.max(scores, axis=(2, 3))
            summed = jnp.sum(
                jnp.where(masked, jnp.exp(scores - highest[:, :, None, None]), 0.0), axis=(2, 3)
            )
            return (highest.reshape(-1), summed.reshape(-1))

        highest, summed = lax.map(row_visit, (step_ids, columns, alive))
        highest, summed = (highest.reshape(rows), summed.reshape(rows))
        overall = lax.pmax(highest, "col")
        summed = lax.psum(summed * jnp.exp(highest - overall), "col")
        highest = overall
        source_pot = epsilon * (log_a - (highest + jnp.log(summed)))
        local_top = column_max(source_pot, epsilon)
        col_top = lax.pmax(local_top, "row")
        local_sum = column_sum(source_pot, epsilon, col_top)
        col_sum = lax.psum(local_sum, "row")
        target_pot = (epsilon * (log_b_tiles - (col_top + jnp.log(col_sum)))).reshape(-1)
    return (source_pot, target_pot)


def solution(mesh):
    return jax.shard_map(
        body,
        mesh=mesh,
        in_specs=(
            P(None, "row"),
            P(None, "col"),
            P("row"),
            P("col"),
            P("row", "col", None),
            P("row", "col"),
        ),
        out_specs=(P("row"), P("col")),
        check_vma=False,
    )
```

profile of v0, /device:TPU:0, one launch (start us, length us, event | category | flops | bytes accessed | tf_op | source)
XLA Modules:
  0.0 1591.6 jit_solution(2242835315922902038)
XLA Ops:
  7.2 16.5 %copy_bitcast_fusion = bf16[64,1024,128]{2,0,1:T(8,128)(2,1)} fusion(bf16[64,131072]{1,0:T(8,128)(2,1)} %param.19), kind=kLoop, calls=%fused_computation.85 | loop fusion | bytes 33554432 | tf_op jit(solution)/shard_map/while | solution.py:104
  33.6 185.8 %while.76 = (s32[]{:T(128)}, f32[8,2048]{1,0:T(8,128)}, f32[8,2048]{1,0:T(8,128)}, pred[8,16,4]{1,2,0:T(4,128)(4,1)}, s32[8,16,4]{1,2,0:T(4,128)}, /*index=5*/s3...) while((s32[]{:T(128)}, f32[8,2048]{1,0:T(8,128)}, ...), condition=%wide.region_9.10_spmd, body=%wide.region_6.9_spmd.sunk | while | flops 148894912 | bytes 13728867 | solution.py:104
  36.4 7.4 gather_fusion.2
  59.7 7.4 gather_fusion.2
  82.8 7.4 gather_fusion.2
  106.0 7.4 gather_fusion.2
  129.3 7.4 gather_fusion.2
  152.4 7.4 gather_fusion.2
  175.7 7.4 gather_fusion.2
  198.9 7.4 gather_fusion.2
  221.8 60.6 %all-reduce.9.cloned.1.call-done = f32[16384]{0:T(1024)} async-done(((f32[16384]{0:T(1024)}), f32[16384]{0:T(1024)}) %all-reduce.9.cloned.1.call-update) | async-done | bytes 65552 | tf_op jit(solution)/shard_map/pmax | solution.py:106
  285.4 40.9 %psum.42 = f32[]{:T(128)} all-reduce(f32[]{:T(128)} %reduce_sum.84), channel_id=1, replica_groups=mesh['row'=16,'col'=8] {'row'}, use_global_device_ids=true, to_apply=%region_1.0 | all-reduce | flops 1 | bytes 8 | tf_op jit(solution)/shard_map/psum | solution.py:34
  327.1 16.1 %all-reduce.11.cloned.1.call-done = f32[16384]{0:T(1024)} async-done(((f32[16384]{0:T(1024)}), f32[16384]{0:T(1024)}) %all-reduce.11.cloned.1.call-update) | async-done | bytes 65552 | tf_op jit(solution)/shard_map/psum | solution.py:107
  345.3 134.2 %while.77 = (s32[]{:T(128)}, f32[1024,128]{1,0:T(8,128)S(1)}, s32[8,16,4]{1,2,0:T(4,128)}, pred[8,16,4]{1,2,0:T(4,128)(4,1)}, s32[8]{0:T(128)}, /*index=5*/f32[1...) while((s32[]{:T(128)}, f32[1024,128]{1,0:T(8,128)S(1)}, ...), condition=%wide.region_15.16_spmd, body=%wide.region_12.15_spmd.sunk | while | flops 140510592 | bytes 4743951 | solution.py:69
  349.4 7.4 gather_fusion.3
  366.3 7.4 gather_fusion.3
  383.0 7.4 gather_fusion.3
  399.7 7.4 gather_fusion.3
  416.5 7.4 gather_fusion.3
  433.3 7.4 gather_fusion.3
  450.1 7.4 gather_fusion.3
  466.9 7.4 gather_fusion.3
  480.4 84.4 %all-reduce.13.cloned.1.call-done = f32[1024,128]{1,0:T(8,128)} async-done(((f32[1024,128]{1,0:T(8,128)}), f32[1024,128]{1,0:T(8,128)}) %all-reduce.13.cloned.1.call-update) | async-done | bytes 524304 | tf_op jit(solution)/shard_map/pmax | solution.py:111
  565.4 155.2 %while.78 = (s32[]{:T(128)}, f32[1024,128]{1,0:T(8,128)S(1)}, s32[8,16,4]{1,2,0:T(4,128)}, pred[8,16,4]{1,2,0:T(4,128)(4,1)}, s32[8]{0:T(128)}, /*index=5*/f32[1...) while((s32[]{:T(128)}, f32[1024,128]{1,0:T(8,128)S(1)}, ...), condition=%wide.region_20.21_spmd, body=%wide.region_17.20_spmd.sunk | while | flops 141559168 | bytes 4842519 | solution.py:81
  569.5 7.4 gather_fusion.5
  588.9 7.4 gather_fusion.5
  608.3 7.4 gather_fusion.5
  627.7 7.4 gather_fusion.5
  647.1 7.4 gather_fusion.5
  685.9 7.4 gather_fusion.5
  705.3 7.4 gather_fusion.5
  723.3 14.3 psum.43
  738.3 67.7 %all-reduce.15.cloned.1.call-done = f32[1024,128]{1,0:T(8,128)} async-done(((f32[1024,128]{1,0:T(8,128)}), f32[1024,128]{1,0:T(8,128)}) %all-reduce.15.cloned.1.call-update) | async-done | bytes 524304 | tf_op jit(solution)/shard_map/psum | solution.py:113
  809.3 190.0 %while.79 = (s32[]{:T(128)}, f32[8,2048]{1,0:T(8,128)}, f32[8,2048]{1,0:T(8,128)}, pred[8,16,4]{1,2,0:T(4,128)(4,1)}, s32[8,16,4]{1,2,0:T(4,128)}, /*index=5*/f3...) while((s32[]{:T(128)}, f32[8,2048]{1,0:T(8,128)}, ...), condition=%wide.region_25.26_spmd, body=%wide.region_22.25_spmd.sunk | while | flops 148894912 | bytes 13237371 | solution.py:104
  837.0 7.4 gather_fusion.10
  860.7 7.4 gather_fusion.10
  884.5 7.4 gather_fusion.10
  908.2 7.4 gather_fusion.10
  931.9 7.4 gather_fusion.10
  955.7 7.4 gather_fusion.10
  979.5 7.4 gather_fusion.10
  1001.7 57.5 %all-reduce.17.cloned.1.call-done = f32[16384]{0:T(1024)} async-done(((f32[16384]{0:T(1024)}), f32[16384]{0:T(1024)}) %all-reduce.17.cloned.1.call-update) | async-done | bytes 65552 | tf_op jit(solution)/shard_map/pmax | solution.py:106
  1061.0 58.8 %all-reduce.19.cloned.1.call-done = f32[16384]{0:T(1024)} async-done(((f32[16384]{0:T(1024)}), f32[16384]{0:T(1024)}) %all-reduce.19.cloned.1.call-update) | async-done | bytes 65552 | tf_op jit(solution)/shard_map/psum | solution.py:107
  1121.9 134.2 %while.80 = (s32[]{:T(128)}, f32[1024,128]{1,0:T(8,128)S(1)}, s32[8,16,4]{1,2,0:T(4,128)}, pred[8,16,4]{1,2,0:T(4,128)(4,1)}, s32[8]{0:T(128)}, /*index=5*/f32[1...) while((s32[]{:T(128)}, f32[1024,128]{1,0:T(8,128)S(1)}, ...), condition=%wide.region_31.32_spmd, body=%wide.region_28.31_spmd.sunk | while | flops 140510592 | bytes 4743951 | solution.py:69
  1126.0 7.4 gather_fusion.11
  1257.0 84.4 %all-reduce.21.cloned.1.call-done = f32[1024,128]{1,0:T(8,128)} async-done(((f32[1024,128]{1,0:T(8,128)}), f32[1024,128]{1,0:T(8,128)}) %all-reduce.21.cloned.1.call-update) | async-done | bytes 524304 | tf_op jit(solution)/shard_map/pmax | solution.py:111
  1341.9 155.2 %while.81 = (s32[]{:T(128)}, f32[1024,128]{1,0:T(8,128)S(1)}, s32[8,16,4]{1,2,0:T(4,128)}, pred[8,16,4]{1,2,0:T(4,128)(4,1)}, s32[8]{0:T(128)}, /*index=5*/f32[1...) while((s32[]{:T(128)}, f32[1024,128]{1,0:T(8,128)S(1)}, ...), condition=%wide.region_36.37_spmd, body=%wide.region_33.36_spmd.sunk | while | flops 141559168 | bytes 4842519 | solution.py:81
  1498.0 84.5 %all-reduce.23.cloned.1.call-done = f32[1024,128]{1,0:T(8,128)} async-done(((f32[1024,128]{1,0:T(8,128)}), f32[1024,128]{1,0:T(8,128)}) %all-reduce.23.cloned.1.call-update) | async-done | bytes 524304 | tf_op jit(solution)/shard_map/psum | solution.py:113
  (893 shorter events, 726.0 us)
Async XLA Ops:
  7.2 275.2 %all-reduce.9.cloned.1.call-start = ((), (), s32[]{:S(2)}) async-start(), calls=%async_computation | async-start | bytes 131072 | tf_op jit(solution)/shard_map/pmax | solution.py:106
  7.2 16.5 %copy-start = (bf16[64,131072]{1,0:T(8,128)(2,1)S(1)}, bf16[64,131072]{1,0:T(8,128)(2,1)}, u32[]{:S(2)}) copy-start(bf16[64,131072]{1,0:T(8,128)(2,1)} %param.19) | copy-start | bytes 50331652
  23.7 5.6 copy-start.1
  23.7 6.1 copy-start.7
  23.7 7.3 copy-start.8
  220.9 122.3 %all-reduce.11.cloned.1.call-start = ((), (), s32[]{:S(2)}) async-start(), calls=%async_computation.1 | async-start | bytes 131072 | tf_op jit(solution)/shard_map/psum | solution.py:107
  283.9 280.9 %all-reduce.13.cloned.1.call-start = ((), (), s32[]{:S(2)}) async-start(), calls=%async_computation.2 | async-start | bytes 1048576 | tf_op jit(solution)/shard_map/pmax | solution.py:111
  479.6 0.8 copy-start.4
  480.4 325.6 %all-reduce.15.cloned.1.call-start = ((), (), s32[]{:S(2)}) async-start(), calls=%async_computation.3 | async-start | bytes 1048576 | tf_op jit(solution)/shard_map/psum | solution.py:113
  720.6 0.8 copy-start.5
  721.4 337.7 %all-reduce.17.cloned.1.call-start = ((), (), s32[]{:S(2)}) async-start(), calls=%async_computation.4 | async-start | bytes 131072 | tf_op jit(solution)/shard_map/pmax | solution.py:106
  827.4 2.7 copy-start.6
  851.1 2.7 copy-start.6
  874.8 2.7 copy-start.6
  898.6 2.7 copy-start.6
  922.3 2.7 copy-start.6
  946.1 2.7 copy-start.6
  969.9 2.7 copy-start.6
  993.6 2.7 copy-start.6
  1000.8 118.9 %all-reduce.19.cloned.1.call-start = ((), (), s32[]{:S(2)}) async-start(), calls=%async_computation.5 | async-start | bytes 131072 | tf_op jit(solution)/shard_map/psum | solution.py:107
  1060.7 280.6 %all-reduce.21.cloned.1.call-start = ((), (), s32[]{:S(2)}) async-start(), calls=%async_computation.6 | async-start | bytes 1048576 | tf_op jit(solution)/shard_map/pmax | solution.py:111
  1256.1 0.8 copy-start.2
  1257.0 325.5 %all-reduce.23.cloned.1.call-start = ((), (), s32[]{:S(2)}) async-start(), calls=%async_computation.7 | async-start | bytes 1048576 | tf_op jit(solution)/shard_map/psum | solution.py:113
  1497.2 0.8 copy-start.3
Sparse Core Ops, SparseCore 0:
  221.0 61.3 all-reduce.8
  285.4 57.7 all-reduce.10
  480.5 84.2 all-reduce.12
  721.6 84.3 all-reduce.14
  1000.9 58.2 all-reduce.16
  1061.9 57.7 all-reduce.18
  1257.1 84.2 all-reduce.20
  1498.1 84.2 all-reduce.22
where the time goes:
time: 1600 us; the launch traced here: 1590 us
  local copies, waits for them, and re-layouts  658 us (41%)
  waiting for transfers between devices  514 us (32%)
  matrix products  183 us (11%)
  other arithmetic  132 us (8%)
  blocking collectives  55.2 us (3%)
  loops' own time  33.6 us (2%)
    gather x48, local copies, waits for them, and re-layouts, cost(): picked = tgt_tiles[:, cols, :]  357 us
    dot_general x48, matrix products, cost(): jnp.einsum('dgi,dgsj->gisj', block, picked, preferred_element_type=jnp.fl...  183 us
    pmax x2, waiting for transfers between devices, body(): col_top = lax.pmax(local_top, 'row')  169 us
    psum x2, waiting for transfers between devices, body(): col_sum = lax.psum(local_sum, 'row')  152 us
    pmax x2, waiting for transfers between devices, body(): overall = lax.pmax(highest, 'col')  118 us
    psum x2, waiting for transfers between devices, body(): summed = lax.psum(summed * jnp.exp(highest - overall), 'col')  74.9 us
    dynamic_slice x80, local copies, waits for them, and re-layouts, body(): highest, summed = lax.map(row_visit, (step_ids, columns, alive))  56.1 us
    dynamic_update_slice x32, local copies, waits for them, and re-layouts, body(): highest, summed = lax.map(row_visit, (step_ids, columns, alive))  48 us
  transfers between devices with their start and end apart: 8, of which 8 were waited for; matrix products, arithmetic and copies ran while one was open for 0% of the time, Pallas kernels for 0%

commit v1 on v0

v1 whole, which is shorter than its diff:
```python
import functools
import math

import jax
import jax.numpy as jnp
from jax import lax
from jax.experimental import pallas as pl
from jax.experimental.pallas import tpu as pltpu
from jax.sharding import PartitionSpec as P

ITERS = 2
TILE = 128
very_negative = -1e30
first_epsilon = 0.5
LOG2E = 1.4426950408889634
LN2 = 0.6931471805599453
SMALLEST = 2.0**-100
LARGEST = 2.0**120
VMEM_LIMIT = 50 * 1024 * 1024


def split3(row):
    hi = row.astype(jnp.bfloat16).astype(jnp.float32)
    rest = row - hi
    mid = rest.astype(jnp.bfloat16).astype(jnp.float32)
    lo = (rest - mid).astype(jnp.bfloat16).astype(jnp.float32)
    return hi, mid, lo


def products(x_ref, y_ref, f_ref, r):
    xb = x_ref[:, pl.ds(pl.multiple_of(r * TILE, TILE), TILE)]
    yb = y_ref[r]
    if f_ref is not None:
        hi, mid, lo = split3(f_ref[pl.ds(r, 1), :])
        place = lax.broadcasted_iota(jnp.int32, (16, TILE), 0)
        extra = jnp.where(
            place == 0, hi, jnp.where(place == 1, mid, jnp.where(place == 2, lo, 0.0))
        )
        xb = jnp.concatenate([xb, extra.astype(jnp.bfloat16)], axis=0)
        yb = jnp.concatenate([yb, jnp.ones((16, yb.shape[1]), jnp.bfloat16)], axis=0)
    return jnp.dot(xb.T, yb, preferred_element_type=jnp.float32)


def row_pass_kernel(kappa, first, slots, *refs):
    if first:
        cols, counts, x_ref, y_hbm, out_ref, y_ref, g_out, hx_ref, total, sems = refs
        f_ref = None
    else:
        cols, counts, x_ref, y_ref, f_ref, g_ref, out_ref, total = refs
    blocks = out_ref.shape[0]
    lane = lax.broadcasted_iota(jnp.int32, (TILE, TILE), 1)

    if first:

        def copy(r, k):
            start = pl.multiple_of(cols[r * slots + k] * TILE, TILE)
            return pltpu.make_async_copy(
                y_hbm.at[:, pl.ds(start, TILE)],
                y_ref.at[r, :, pl.ds(k * TILE, TILE)],
                sems.at[r],
            )

        @pl.loop(0, blocks)
        def _(r):
            for k in range(slots):
                copy(r, k).start()

    def shifts(r):
        live = counts[r]
        rows = []
        for k in range(slots):
            if first:
                row = g_out[pl.ds(r * slots + k, 1), :]
            else:
                row = g_ref[pl.ds(cols[r * slots + k], 1), :]
            rows.append(jnp.where(k < live, row, very_negative))
        return rows

    @pl.loop(0, blocks)
    def _(r):
        if first:
            pltpu.make_async_copy(y_ref.at[r], y_ref.at[r], sems.at[r]).wait()
            yf = y_ref[r].astype(jnp.float32)
            half = -0.5 * jnp.sum(yf * yf, axis=0, keepdims=True)
            for k in range(slots):
                g_out[pl.ds(r * slots + k, 1), :] = half[:, k * TILE : (k + 1) * TILE]
            xf = x_ref[:, pl.ds(pl.multiple_of(r * TILE, TILE), TILE)].astype(jnp.float32)
            hx_ref[pl.ds(r, 1), :] = 0.5 * jnp.sum(xf * xf, axis=0, keepdims=True)
        scores = products(x_ref, y_ref, f_ref, r)
        terms = jnp.zeros((TILE, TILE), jnp.float32)
        for k, row in enumerate(shifts(r)):
            terms += jnp.exp2((scores[:, k * TILE : (k + 1) * TILE] + row) * kappa)
        summed = jnp.sum(terms, axis=1, keepdims=True)
        total[...] = jnp.where(lane == r, summed, total[...])

    sums = total[...]
    out_ref[...] = jnp.log2(sums).T
    fine = jnp.logical_and(jnp.min(sums) >= SMALLEST, jnp.max(sums) <= LARGEST)

    @pl.when(jnp.logical_not(fine))
    def _():
        @pl.loop(0, blocks)
        def _(r):
            scores = products(x_ref, y_ref, f_ref, r)
            scores = jnp.concatenate(
                [
                    scores[:, k * TILE : (k + 1) * TILE] + row
                    for k, row in enumerate(shifts(r))
                ],
                axis=1,
            )
            top = jnp.max(scores, axis=1, keepdims=True)
            summed = jnp.sum(jnp.exp2((scores - top) * kappa), axis=1, keepdims=True)
            total[...] = jnp.where(lane == r, top * kappa + jnp.log2(summed), total[...])

        out_ref[...] = total[...].T


def col_pass_kernel(kappa, first, slots, *refs):
    cols, counts, x_ref, y_ref, f_ref, g_ref, out_ref, total = refs
    blocks = f_ref.shape[0]

    def shifts(r):
        live = counts[r]
        rows = []
        for k in range(slots):
            if first:
                row = g_ref[pl.ds(r * slots + k, 1), :]
            else:
                row = g_ref[pl.ds(cols[r * slots + k], 1), :]
            rows.append(jnp.where(k < live, row, very_negative))
        return rows

    total[...] = jnp.zeros_like(total)

    def visit(r, carry):
        least, most = carry
        scores = products(x_ref, y_ref, f_ref, r)
        live = counts[r]
        for k, row in enumerate(shifts(r)):
            terms = jnp.exp2((scores[:, k * TILE : (k + 1) * TILE] + row) * kappa)
            summed = jnp.sum(terms, axis=0, keepdims=True)
            at = pl.ds(cols[r * slots + k], 1)
            total[at, :] += summed
            least = jnp.minimum(least, jnp.where(k < live, summed, 1.0))
            most = jnp.maximum(most, summed)
        return least, most

    ones = jnp.ones((1, TILE), jnp.float32)
    least, most = lax.fori_loop(0, blocks, visit, (ones, ones))
    sums = total[...]
    out_ref[...] = jnp.where(sums > 0.0, jnp.log2(sums), very_negative)
    fine = jnp.logical_and(jnp.min(least) >= SMALLEST, jnp.max(most) <= LARGEST / blocks)

    @pl.when(jnp.logical_not(fine))
    def _():
        out_ref[...] = jnp.full_like(out_ref, very_negative)

        @pl.loop(0, blocks)
        def _(r):
            scores = products(x_ref, y_ref, f_ref, r)
            live = counts[r]
            for k, row in enumerate(shifts(r)):

                @pl.when(k < live)
                def _():
                    part = scores[:, k * TILE : (k + 1) * TILE] + row
                    top = jnp.max(part, axis=0, keepdims=True)
                    summed = jnp.sum(jnp.exp2((part - top) * kappa), axis=0, keepdims=True)
                    mine = top * kappa + jnp.log2(summed)
                    at = pl.ds(cols[r * slots + k], 1)
                    old = out_ref[at, :]
                    peak = jnp.maximum(old, mine)
                    out_ref[at, :] = peak + jnp.log2(
                        jnp.exp2(old - peak) + jnp.exp2(mine - peak)
                    )


SMEM = functools.partial(pl.BlockSpec, memory_space=pltpu.SMEM)
VMEM = functools.partial(pl.BlockSpec, memory_space=pltpu.VMEM)
PARAMS = dict(compiler_params=pltpu.CompilerParams(vmem_limit_bytes=VMEM_LIMIT))


def lse(stack):
    top = jnp.max(stack, axis=0)
    return top + jnp.log2(jnp.sum(jnp.exp2(stack - top[None]), axis=0))


def shift_z(value, by, cols):
    return lax.ppermute(value, "col", [(i, (i + 2 * by) % cols) for i in range(cols)])


def over_cols(part, cols):
    half = part.shape[0] // 2
    core = lax.axis_index("col") % 2
    swap = [(i, i ^ 1) for i in range(cols)]
    away = lax.dynamic_slice_in_dim(part, (1 - core) * half, half, 0)
    mine = lax.dynamic_slice_in_dim(part, core * half, half, 0)
    mine = lse(jnp.stack([mine, lax.ppermute(away, "col", swap)]))
    chips = cols // 2
    mine = lse(jnp.stack([mine] + [shift_z(mine, by, cols) for by in range(1, chips)]))
    other = lax.ppermute(mine, "col", swap)
    low = jnp.where(core == 0, mine, other)
    high = jnp.where(core == 0, other, mine)
    return jnp.concatenate([low, high], axis=0)


def body(source_points, target_points, source_mass, target_mass, tile_cols, tile_counts):
    width, rows = source_points.shape
    row_blocks = rows // TILE
    target_cells = target_points.shape[1]
    target_blocks = target_cells // TILE
    slots = tile_cols.shape[2]
    row_devices = lax.axis_size("row")
    col_devices = lax.axis_size("col")
    own_blocks = target_blocks // row_devices
    me = lax.axis_index("row")
    f32 = jnp.float32

    cols = tile_cols.reshape(row_blocks * slots)
    counts = tile_counts.reshape(row_blocks)
    mass_a = source_mass.reshape(row_blocks, TILE)
    log_a = jnp.log2(mass_a)
    own_mass = lax.dynamic_slice_in_dim(target_mass, me * own_blocks * TILE, own_blocks * TILE, 0)
    log_b = jnp.log2(own_mass).reshape(own_blocks, TILE)
    own_points = lax.dynamic_slice_in_dim(
        target_points, me * own_blocks * TILE, own_blocks * TILE, 1
    ).astype(f32)
    own_half = (0.5 * jnp.sum(own_points * own_points, axis=0)).reshape(own_blocks, TILE)
    part_a = jnp.log2(jnp.sum(source_mass))
    part_b = jnp.log2(jnp.sum(target_mass))

    shape = jax.ShapeDtypeStruct
    epsilon = first_epsilon
    part, tiles, halves, half_x = pl.pallas_call(
        functools.partial(row_pass_kernel, LOG2E / epsilon, True, slots),
        out_shape=(
            shape((row_blocks, TILE), f32),
            pltpu.VMEM((row_blocks, width, slots * TILE), jnp.bfloat16),
            shape((row_blocks * slots, TILE), f32),
            shape((row_blocks, TILE), f32),
        ),
        in_specs=[SMEM(), SMEM(), VMEM(), pl.BlockSpec(memory_space=pl.ANY)],
        out_specs=(VMEM(), VMEM(), VMEM(), VMEM()),
        scratch_shapes=[
            pltpu.VMEM((TILE, row_blocks), f32),
            pltpu.SemaphoreType.DMA((row_blocks,)),
        ],
        name="row_pass_first",
        **PARAMS,
    )(cols, counts, source_points, target_points)
    tiles = pltpu.with_memory_space_constraint(tiles, pltpu.VMEM)

    f_pot = jnp.zeros((row_blocks, TILE), f32)
    g_own = -own_half
    g_pot = halves
    total_a = total_b = None
    for step in range(ITERS):
        epsilon = first_epsilon * 0.5**step
        kappa = LOG2E / epsilon
        if step > 0:
            part = pl.pallas_call(
                functools.partial(row_pass_kernel, kappa, False, slots),
                out_shape=shape((row_blocks, TILE), f32),
                in_specs=[SMEM(), SMEM(), VMEM(), VMEM(), VMEM(), VMEM()],
                out_specs=VMEM(),
                scratch_shapes=[pltpu.VMEM((TILE, row_blocks), f32)],
                name="row_pass",
                **PARAMS,
            )(cols, counts, source_points, tiles, f_pot, g_pot)
        if step == 0:
            extra = jnp.full((16, TILE), part_b, f32)
            both = over_cols(jnp.concatenate([part, extra], axis=0), col_devices)
            part, total_b = both[:row_blocks], both[row_blocks, 0]
        else:
            part = over_cols(part, col_devices)
        f_pot = f_pot + (epsilon * LN2) * (log_a - part)

        part = pl.pallas_call(
            functools.partial(col_pass_kernel, kappa, step == 0, slots),
            out_shape=shape((target_blocks, TILE), f32),
            in_specs=[SMEM(), SMEM(), VMEM(), VMEM(), VMEM(), VMEM()],
            out_specs=VMEM(),
            scratch_shapes=[pltpu.VMEM((target_blocks, TILE), f32)],
            name="col_pass",
            **PARAMS,
        )(cols, counts, source_points, tiles, f_pot, g_pot)
        part = part.reshape(row_devices, own_blocks, TILE)
        if step == 0:
            extra = jnp.full((row_devices, 8, TILE), part_a, f32)
            part = jnp.concatenate([part, extra], axis=1)
        part = lse(lax.all_to_all(part, "row", 0, 0))
        if step == 0:
            part, total_a = part[:own_blocks], part[own_blocks, 0]
        g_own = g_own + (epsilon * LN2) * (log_b - part)
        send = g_own
        if step == ITERS - 1:
            both_eps = first_epsilon * (2.0 - 0.5**step)
            send = g_own + own_half + (both_eps * LN2) * (total_a - total_b)
        g_pot = lax.all_to_all(
            jnp.broadcast_to(send[None], (row_devices, own_blocks, TILE)), "row", 0, 0
        ).reshape(target_blocks, TILE)

    earlier = first_epsilon * (2.0 - 0.5 ** (ITERS - 1)) - epsilon
    source = f_pot + half_x - LN2 * (epsilon * total_a + earlier * (total_a - total_b))
    return (source.reshape(rows), g_pot.reshape(target_cells))


def solution(mesh):
    return jax.shard_map(
        body,
        mesh=mesh,
        in_specs=(
            P(None, "row"),
            P(None, "col"),
            P("row"),
            P("col"),
            P("row", "col", None),
            P("row", "col"),
        ),
        out_specs=(P("row"), P("col")),
        check_vma=False,
    )
```

time: 1600 us -> 317 us (0.20)
  local copies, waits for them, and re-layouts: 658 us -> 18.6 us
  waiting for transfers between devices: 514 us -> 45.3 us
  matrix products: 183 us -> 0 us
  Pallas kernels: 0 us -> 152 us
  other arithmetic: 132 us -> 8.89 us
  starting transfers between devices: 0.51 us -> 72.9 us
  blocking collectives: 55.2 us -> 14.5 us
  loops' own time: 33.6 us -> 0 us
    gather x128 -> x0, local copies, waits for them, and re-layouts: 431 us -> none  [the longest x48 357 us: cost(): picked = tgt_tiles[:, cols, :]]
    pmax x4 -> x0, waiting for transfers between devices: 287 us -> none  [the longest x2 169 us: body(): col_top = lax.pmax(local_top, 'row')]
    psum x4 -> x0, waiting for transfers between devices: 227 us -> none  [the longest x2 152 us: body(): col_sum = lax.psum(local_sum, 'row')]
    dot_general x48 -> x0, matrix products: 183 us -> none  [cost(): jnp.einsum('dgi,dgsj->gisj', block, picked, preferred_element_type=jnp.fl...]
    pallas_call x0 -> x4, Pallas kernels: none -> 152 us  [the longest x2 66.8 us: body(): pl.pallas_call(functools.partial(col_pass_kernel, kappa, step == 0, slots...]
    ppermute x0 -> x10, starting transfers between devices: none -> 58.7 us  [the longest x6 58.5 us: shift_z(): lax.ppermute(value, 'col', [(i, (i + 2 * by) % cols) for i in range(cols)])]
    dynamic_slice x80 -> x0, local copies, waits for them, and re-layouts: 56.1 us -> none  [body(): highest, summed = lax.map(row_visit, (step_ids, columns, alive))]
    psum x2 -> x0, blocking collectives: 55.2 us -> none  [the longest x1 40.9 us: body(): source_sum = lax.psum(jnp.sum(source_mass), 'row')]
  transfers between devices with their start and end apart: 8 -> 13, of which waited for: 8 -> 10; matrix products, arithmetic and copies ran while one was open for 0% -> 1% of each run, Pallas kernels for 0% -> 0%
where the time goes in v1:
time: 317 us
  Pallas kernels  152 us (48%)
  starting transfers between devices  72.9 us (23%)
  waiting for transfers between devices  45.3 us (14%)
  local copies, waits for them, and re-layouts  18.6 us (6%)
  blocking collectives  14.5 us (5%)
  other arithmetic  8.89 us (3%)
  between operations  4.24 us (1%)
    pallas_call x2, Pallas kernels, body(): pl.pallas_call(functools.partial(col_pass_kernel, kappa, step == 0, slots...  66.8 us
    ppermute x6, starting transfers between devices, shift_z(): lax.ppermute(value, 'col', [(i, (i + 2 * by) % cols) for i in range(cols)])  58.5 us
    pallas_call x1, Pallas kernels, body(): pl.pallas_call(functools.partial(row_pass_kernel, LOG2E / epsilon, True,...  44.4 us
    pallas_call x1, Pallas kernels, body(): pl.pallas_call(functools.partial(row_pass_kernel, kappa, False, slots), o...  41.2 us
    all_to_all x2, waiting for transfers between devices, body(): part = lse(lax.all_to_all(part, 'row', 0, 0))  23.8 us
    all_to_all x1, blocking collectives, body(): lax.all_to_all(jnp.broadcast_to(send[None], (row_devices, own_blocks, TIL...  14.5 us
    unnamed x16, local copies, waits for them, and re-layouts  12.4 us
    all_to_all x1, waiting for transfers between devices, body(): lax.all_to_all(jnp.broadcast_to(send[None], (row_devices, own_blocks, TIL...  11 us
  transfers between devices with their start and end apart: 13, of which 10 were waited for; matrix products, arithmetic and copies ran while one was open for 1% of the time, Pallas kernels for 0%

profile of v1, /device:TPU:0, one launch (start us, length us, event | category | flops | bytes accessed | tf_op | source)
XLA Modules:
  0.0 316.8 jit_solution(13867859400773469352)
XLA Ops:
  0.6 1.8 reduce_sum.81
  3.1 0.8 copy.8
  3.9 0.7 reshape.83.refs_0_
  4.6 44.4 %row_pass_first.1 = (f32[128,128]{1,0:T(8,128)}, bf16[128,64,512]{2,1,0:T(8,128)(2,1)S(1)}, f32[512,128]{1,0:T(8,128)}, f32[128,128]{1,0:T(8,128)}) custom-call(s32[512]{0:T(512)} %reshape.83.refs_0_, s32[128]{0:T(128)} %bitcast.64, bf16[64,16384]{1,0:T(8,128)(2,1)} %refs_2_.7, bf16[64,131072]{1,0:T(8,128)(2,1)} %refs_3_.1), custom_call_target="tpu_custom_call" | custom-call | tf_op jit(solution)/shard_map/row_pass_first/pallas_call | solution.py:235
  49.0 3.2 %copy-done = bf16[128,64,512]{2,1,0:T(8,128)(2,1)} copy-done((bf16[128,64,512]{2,1,0:T(8,128)(2,1)}, bf16[128,64,512]{2,1,0:T(8,128)(2,1)S(1)}, u32[]{:S(2)}) %copy-start) | copy-done | bytes 8388632
  52.3 0.8 fusion.22
  53.0 1.2 collective-permute-done
  54.3 0.8 fusion.23
  55.1 4.2 %collective-permute-start.3 = (f32[72,128]{1,0:T(8,128)S(1)}, f32[72,128]{1,0:T(8,128)S(1)}, u32[]{:S(2)}, u32[]{:S(2)}) collective-permute-start(f32[72,128]{1,0:T(8,128)S(1)} %multiply_add_fusion.2), channel_id=1, source_target_pairs={{0,6},{1,7},{2,0},{3,1},{4,2},{5,3},{6,4},{7,5},{8,14},{9,15},{10,... | collective-permute-start | bytes 110600 | tf_op jit(solution)/shard_map/ppermute | solution.py:190
  59.3 1.3 collective-permute-start.1
  60.5 0.4 collective-permute-done.3
  60.9 3.9 %collective-permute-done.2 = f32[72,128]{1,0:T(8,128)S(1)} collective-permute-done((f32[72,128]{1,0:T(8,128)S(1)}, f32[72,128]{1,0:T(8,128)S(1)}, u32[]{:S(2)}, u32[]{:S(2)}) %collective-permute-start.2) | collective-permute-done | bytes 36896 | tf_op jit(solution)/shard_map/ppermute | solution.py:190
  64.9 0.1 collective-permute-start.4
  65.0 0.6 reduce_sum.85
  66.4 0.7 fusion.10.refs_4_
  67.0 3.4 %copy-done.1 = bf16[128,64,512]{2,1,0:T(8,128)(2,1)S(1)} copy-done((bf16[128,64,512]{2,1,0:T(8,128)(2,1)S(1)}, bf16[128,64,512]{2,1,0:T(8,128)(2,1)}, u32[]{:S(2)}) %copy-start.1) | copy-done | bytes 8388632
  70.4 33.4 %col_pass.2 = f32[1024,128]{1,0:T(8,128)} custom-call(s32[512]{0:T(512)} %reshape.83.refs_0_, s32[128]{0:T(128)} %bitcast.65, bf16[64,16384]{1,0:T(8,128)(2,1)} %refs_2_.7, bf16[128,64,512]{2,1,0:T(8,128)(2,1)S(1)} %copy-done.1, f32[128,128]{1,0:T(8,128)} %fusion.10.refs_4_, f32[512,128]{1,0:T(8,128)} %get-tuple-element.8.refs_5_), custom_call_target="tpu_custom_call" | custom-call | tf_op jit(solution)/shard_map/col_pass/pallas_call | solution.py:279
  103.8 1.9 concatenate.14
  105.8 7.0 %all-to-all-start = ((f32[16,72,128]{2,1,0:T(8,128)}), f32[16,72,128]{2,1,0:T(8,128)S(1)}, u32[]{:S(2)}, u32[]{:S(2)}) async-start(f32[16,72,128]{2,1,0:T(8,128)} %concatenate.14), calls=%async_computation | async-start | bytes 1179648 | tf_op jit(solution)/shard_map/all_to_all | solution.py:292
  112.8 1.5 multiply_reduce_fusion
  114.4 11.3 %all-to-all-done = f32[16,72,128]{2,1,0:T(8,128)S(1)} async-done(((f32[16,72,128]{2,1,0:T(8,128)}), f32[16,72,128]{2,1,0:T(8,128)S(1)}, u32[]{:S(2)}, u32[]{:S(2)}) %all-to-all-start) | async-done | bytes 589856 | tf_op jit(solution)/shard_map/all_to_all | solution.py:292
  125.7 0.1 exponential_reduce_fusion
  125.9 0.8 fusion.17
  126.7 0.8 broadcast_in_dim.4
  127.5 3.6 %all-to-all-start.1 = ((f32[16,64,128]{2,1,0:T(8,128)}), f32[16,64,128]{2,1,0:T(8,128)S(1)}, u32[]{:S(2)}, u32[]{:S(2)}) async-start(f32[16,64,128]{2,1,0:T(8,128)} %broadcast_in_dim.4), calls=%async_computation.1 | async-start | bytes 1048576 | tf_op jit(solution)/shard_map/all_to_all | solution.py:300
  131.1 11.0 %all-to-all-done.1 = f32[16,64,128]{2,1,0:T(8,128)S(1)} async-done(((f32[16,64,128]{2,1,0:T(8,128)}), f32[16,64,128]{2,1,0:T(8,128)S(1)}, u32[]{:S(2)}, u32[]{:S(2)}) %all-to-all-start.1) | async-done | bytes 524320 | tf_op jit(solution)/shard_map/all_to_all | solution.py:300
  142.1 0.8 copy-done.3
  142.9 3.4 %copy-done.2 = bf16[128,64,512]{2,1,0:T(8,128)(2,1)S(1)} copy-done((bf16[128,64,512]{2,1,0:T(8,128)(2,1)S(1)}, bf16[128,64,512]{2,1,0:T(8,128)(2,1)}, u32[]{:S(2)}) %copy-start.2) | copy-done | bytes 8388632
  146.3 41.2 %row_pass.1 = f32[128,128]{1,0:T(8,128)} custom-call(s32[512]{0:T(512)} %reshape.83.refs_0_, s32[128]{0:T(128)} %bitcast.66, bf16[64,16384]{1,0:T(8,128)(2,1)} %refs_2_.7, bf16[128,64,512]{2,1,0:T(8,128)(2,1)S(1)} %copy-done.2, f32[128,128]{1,0:T(8,128)} %fusion.10.refs_4_, f32[1024,128]{1,0:T(8,128)} %bitcast.49), custom_call_target="tpu_custom_call" | custom-call | tf_op jit(solution)/shard_map/row_pass/pallas_call | solution.py:262
  187.5 0.8 dynamic-slice_bitcast_fusion
  188.3 1.2 collective-permute-done.5
  189.5 0.8 dynamic-slice_maximum_fusion
  190.3 0.9 collective-permute-start.8
  191.2 50.8 %collective-permute-start.7 = (f32[64,128]{1,0:T(8,128)S(1)}, f32[64,128]{1,0:T(8,128)S(1)}, u32[]{:S(2)}, u32[]{:S(2)}) collective-permute-start(f32[64,128]{1,0:T(8,128)S(1)} %multiply_add_fusion.4), channel_id=1, source_target_pairs={{0,4},{1,5},{2,6},{3,7},{4,0},{5,1},{6,2},{7,3},{8,12},{9,13},{10,... | collective-permute-start | bytes 98312 | tf_op jit(solution)/shard_map/ppermute | solution.py:190
  242.1 1.3 collective-permute-start.6
  243.4 0.6 collective-permute-done.7
  244.0 3.2 %collective-permute-done.6 = f32[64,128]{1,0:T(8,128)S(1)} collective-permute-done((f32[64,128]{1,0:T(8,128)S(1)}, f32[64,128]{1,0:T(8,128)S(1)}, u32[]{:S(2)}, u32[]{:S(2)}) %collective-permute-start.6) | collective-permute-done | bytes 32800 | tf_op jit(solution)/shard_map/ppermute | solution.py:190
  247.3 0.1 collective-permute-start.9
  247.4 0.5 slice.18
  247.9 0.6 slice.17
  250.4 0.7 subtract_bitcast_fusion
  251.1 33.4 %col_pass.3 = f32[1024,128]{1,0:T(8,128)} custom-call(s32[512]{0:T(512)} %reshape.83.refs_0_, s32[128]{0:T(128)} %bitcast.67, bf16[64,16384]{1,0:T(8,128)(2,1)} %refs_2_.7, bf16[128,64,512]{2,1,0:T(8,128)(2,1)S(1)} %copy-done.2, f32[128,128]{1,0:T(8,128)} %get-tuple-element.11.refs_4_, f32[1024,128]{1,0:T(8,128)} %bitcast.50), custom_call_target="tpu_custom_call" | custom-call | tf_op jit(solution)/shard_map/col_pass/pallas_call | solution.py:279
  284.5 3.6 %all-to-all-start.2 = ((f32[16,64,128]{2,1,0:T(8,128)}), f32[16,64,128]{2,1,0:T(8,128)S(1)}, u32[]{:S(2)}, u32[]{:S(2)}) async-start(f32[16,64,128]{2,1,0:T(8,128)} %bitcast.51), calls=%async_computation.2 | async-start | bytes 1048576 | tf_op jit(solution)/shard_map/all_to_all | solution.py:292
  288.1 12.4 %all-to-all-done.2 = f32[16,64,128]{2,1,0:T(8,128)S(1)} async-done(((f32[16,64,128]{2,1,0:T(8,128)}), f32[16,64,128]{2,1,0:T(8,128)S(1)}, u32[]{:S(2)}, u32[]{:S(2)}) %all-to-all-start.2) | async-done | bytes 524320 | tf_op jit(solution)/shard_map/all_to_all | solution.py:292
  300.6 0.1 exponential_reduce_fusion.1
  300.7 0.8 fusion.21
  301.5 14.5 %all_to_all.20 = f32[16,64,128]{2,1,0:T(8,128)S(1)} all-to-all(f32[16,64,128]{2,1,0:T(8,128)S(1)} %broadcast_in_dim.5), channel_id=1, replica_groups=mesh['row'=16,'col'=8] {'row'}, dimensions={0} | all-to-all | bytes 1048576 | tf_op jit(solution)/shard_map/all_to_all | solution.py:300
  316.0 0.8 copy.10
  (33 shorter events, 0.5 us)
Async XLA Ops:
  4.6 60.4 %copy-start.5 = (f32[16384]{0:T(1024)S(1)}, f32[16384]{0:T(1024)}, u32[]{:S(2)}) copy-start(f32[16384]{0:T(1024)} %param.8) | copy-start | bytes 196612
  49.0 3.2 %copy-start = (bf16[128,64,512]{2,1,0:T(8,128)(2,1)}, bf16[128,64,512]{2,1,0:T(8,128)(2,1)S(1)}, u32[]{:S(2)}) copy-start(bf16[128,64,512]{2,1,0:T(8,128)(2,1)S(1)} %get-tuple-element.7.refs_3_) | copy-start | bytes 25165828
  53.0 1.2 collective-permute-start
  55.1 5.8 %collective-permute-start.3 = (f32[72,128]{1,0:T(8,128)S(1)}, f32[72,128]{1,0:T(8,128)S(1)}, u32[]{:S(2)}, u32[]{:S(2)}) collective-permute-start(f32[72,128]{1,0:T(8,128)S(1)} %multiply_add_fusion.2), channel_id=1, source_target_pairs={{0,6},{1,7},{2,0},{3,1},{4,2},{5,3},{6,4},{7,5},{8,14},{9,15},{10,... | collective-permute-start | bytes 110600 | tf_op jit(solution)/shard_map/ppermute | solution.py:190
  59.3 5.5 %collective-permute-start.2 = (f32[72,128]{1,0:T(8,128)S(1)}, f32[72,128]{1,0:T(8,128)S(1)}, u32[]{:S(2)}, u32[]{:S(2)}) collective-permute-start(f32[72,128]{1,0:T(8,128)S(1)} %multiply_add_fusion.2), channel_id=1, source_target_pairs={{0,4},{1,5},{2,6},{3,7},{4,0},{5,1},{6,2},{7,3},{8,12},{9,13},{10,... | collective-permute-start | bytes 110600 | tf_op jit(solution)/shard_map/ppermute | solution.py:190
  59.3 5.6 %collective-permute-start.1 = (f32[72,128]{1,0:T(8,128)S(1)}, f32[72,128]{1,0:T(8,128)S(1)}, u32[]{:S(2)}, u32[]{:S(2)}) collective-permute-start(f32[72,128]{1,0:T(8,128)S(1)} %multiply_add_fusion.2), channel_id=1, source_target_pairs={{0,2},{1,3},{2,4},{3,5},{4,6},{5,7},{6,0},{7,1},{8,10},{9,11},{10,... | collective-permute-start | bytes 110600 | tf_op jit(solution)/shard_map/ppermute | solution.py:190
  64.9 1.4 collective-permute-start.4
  67.0 3.4 %copy-start.1 = (bf16[128,64,512]{2,1,0:T(8,128)(2,1)S(1)}, bf16[128,64,512]{2,1,0:T(8,128)(2,1)}, u32[]{:S(2)}) copy-start(bf16[128,64,512]{2,1,0:T(8,128)(2,1)} %copy-done) | copy-start | bytes 25165828
  105.8 19.9 %all-to-all-start = ((f32[16,72,128]{2,1,0:T(8,128)}), f32[16,72,128]{2,1,0:T(8,128)S(1)}, u32[]{:S(2)}, u32[]{:S(2)}) async-start(f32[16,72,128]{2,1,0:T(8,128)} %concatenate.14), calls=%async_computation | async-start | bytes 1179648 | tf_op jit(solution)/shard_map/all_to_all | solution.py:292
  112.8 137.6 %copy-start.4 = (f32[128,128]{1,0:T(8,128)S(1)}, f32[128,128]{1,0:T(8,128)}, u32[]{:S(2)}) copy-start(f32[128,128]{1,0:T(8,128)} %fusion.10.refs_4_) | copy-start | bytes 196612
  112.8 137.6 %copy-start.6 = (f32[128,128]{1,0:T(8,128)S(1)}, f32[128,128]{1,0:T(8,128)}, u32[]{:S(2)}) copy-start(f32[128,128]{1,0:T(8,128)} %get-tuple-element.9) | copy-start | bytes 196612
  127.5 14.6 %all-to-all-start.1 = ((f32[16,64,128]{2,1,0:T(8,128)}), f32[16,64,128]{2,1,0:T(8,128)S(1)}, u32[]{:S(2)}, u32[]{:S(2)}) async-start(f32[16,64,128]{2,1,0:T(8,128)} %broadcast_in_dim.4), calls=%async_computation.1 | async-start | bytes 1048576 | tf_op jit(solution)/shard_map/all_to_all | solution.py:300
  142.1 0.8 copy-start.3
  142.9 3.4 %copy-start.2 = (bf16[128,64,512]{2,1,0:T(8,128)(2,1)S(1)}, bf16[128,64,512]{2,1,0:T(8,128)(2,1)}, u32[]{:S(2)}) copy-start(bf16[128,64,512]{2,1,0:T(8,128)(2,1)} %copy-done) | copy-start | bytes 25165828
  188.3 1.2 collective-permute-start.5
  190.3 53.1 %collective-permute-start.8 = (f32[64,128]{1,0:T(8,128)S(1)}, f32[64,128]{1,0:T(8,128)S(1)}, u32[]{:S(2)}, u32[]{:S(2)}) collective-permute-start(f32[64,128]{1,0:T(8,128)S(1)} %multiply_add_fusion.4), channel_id=1, source_target_pairs={{0,6},{1,7},{2,0},{3,1},{4,2},{5,3},{6,4},{7,5},{8,14},{9,15},{10,... | collective-permute-start | bytes 98312 | tf_op jit(solution)/shard_map/ppermute | solution.py:190
  191.2 52.7 %collective-permute-start.7 = (f32[64,128]{1,0:T(8,128)S(1)}, f32[64,128]{1,0:T(8,128)S(1)}, u32[]{:S(2)}, u32[]{:S(2)}) collective-permute-start(f32[64,128]{1,0:T(8,128)S(1)} %multiply_add_fusion.4), channel_id=1, source_target_pairs={{0,4},{1,5},{2,6},{3,7},{4,0},{5,1},{6,2},{7,3},{8,12},{9,13},{10,... | collective-permute-start | bytes 98312 | tf_op jit(solution)/shard_map/ppermute | solution.py:190
  242.1 5.1 %collective-permute-start.6 = (f32[64,128]{1,0:T(8,128)S(1)}, f32[64,128]{1,0:T(8,128)S(1)}, u32[]{:S(2)}, u32[]{:S(2)}) collective-permute-start(f32[64,128]{1,0:T(8,128)S(1)} %multiply_add_fusion.4), channel_id=1, source_target_pairs={{0,2},{1,3},{2,4},{3,5},{4,6},{5,7},{6,0},{7,1},{8,10},{9,11},{10,... | collective-permute-start | bytes 98312 | tf_op jit(solution)/shard_map/ppermute | solution.py:190
  247.3 3.1 collective-permute-start.9
  284.5 16.0 %all-to-all-start.2 = ((f32[16,64,128]{2,1,0:T(8,128)}), f32[16,64,128]{2,1,0:T(8,128)S(1)}, u32[]{:S(2)}, u32[]{:S(2)}) async-start(f32[16,64,128]{2,1,0:T(8,128)} %bitcast.51), calls=%async_computation.2 | async-start | bytes 1048576 | tf_op jit(solution)/shard_map/all_to_all | solution.py:292

commit v2 on v1

v2 whole, which is shorter than its diff:
```python
import functools
import math

import jax
import jax.numpy as jnp
from jax import lax
from jax.experimental import pallas as pl
from jax.experimental.pallas import tpu as pltpu
from jax.sharding import PartitionSpec as P

ITERS = 2
TILE = 128
very_negative = -1e30
first_epsilon = 0.5
LOG2E = 1.4426950408889634
LN2 = 0.6931471805599453
SMALLEST = 2.0**-100
LARGEST = 2.0**120
VMEM_LIMIT = 16 * 1024 * 1024
UNROLL = 16
CHUNK = 64


def split3(row):
    hi = row.astype(jnp.bfloat16).astype(jnp.float32)
    rest = row - hi
    mid = rest.astype(jnp.bfloat16).astype(jnp.float32)
    lo = (rest - mid).astype(jnp.bfloat16).astype(jnp.float32)
    return hi, mid, lo


def products(x_ref, y_ref, f_ref, cols, slots, r):
    lhs = x_ref[r]
    picked = [
        y_ref[:, pl.ds(pl.multiple_of(cols[r * slots + k] * TILE, TILE), TILE)]
        for k in range(slots)
    ]
    yb = jnp.concatenate(picked, axis=1)
    rhs = [yb, yb]
    if f_ref is not None:
        hi, mid, lo = split3(f_ref[pl.ds(r, 1), :])
        place = lax.broadcasted_iota(jnp.int32, (16, TILE), 0)
        extra = jnp.where(
            place == 0, hi, jnp.where(place == 1, mid, jnp.where(place == 2, lo, 0.0))
        )
        lhs = jnp.concatenate([lhs, extra.astype(jnp.bfloat16).T], axis=1)
        rhs.append(jnp.ones((16, yb.shape[1]), jnp.bfloat16))
    return jnp.dot(lhs, jnp.concatenate(rhs, axis=0), preferred_element_type=jnp.float32)


def shifts(cols, counts, g_ref, slots, r):
    live = counts[r]
    return [
        jnp.where(k < live, g_ref[pl.ds(cols[r * slots + k], 1), :], very_negative)
        for k in range(slots)
    ]


def prepare(kappa, x_hbm, y_hbm, x_ref, x2_ref, y_ref, g_ref, hx_ref, x_in, x_sem, y_sem):
    width = y_ref.shape[0]
    blocks = hx_ref.shape[0]
    target_blocks = g_ref.shape[0]
    chunks = target_blocks // CHUNK
    x_copy = pltpu.make_async_copy(x_hbm, x_in, x_sem)
    x_copy.start()

    def y_copy(c):
        at = pl.ds(pl.multiple_of(c * (CHUNK * TILE), CHUNK * TILE), CHUNK * TILE)
        return pltpu.make_async_copy(y_hbm.at[:, at], y_ref.at[:, at], y_sem.at[c])

    @pl.loop(0, chunks)
    def _(c):
        y_copy(c).start()

    x_copy.wait()

    @pl.loop(0, blocks, unroll=4)
    def _(r):
        xf = x_in[:, pl.ds(pl.multiple_of(r * TILE, TILE), TILE)].astype(jnp.float32)
        hx_ref[pl.ds(r, 1), :] = 0.5 * jnp.sum(xf * xf, axis=0, keepdims=True)
        scaled = xf * kappa
        hi = scaled.astype(jnp.bfloat16)
        lo = (scaled - hi.astype(jnp.float32)).astype(jnp.bfloat16)
        turned = jnp.concatenate([hi, lo], axis=0).T
        x_ref[r] = turned
        x2_ref[r] = turned + turned

    @pl.loop(0, chunks)
    def _(c):
        y_copy(c).wait()

        @pl.loop(0, CHUNK // 8, unroll=2)
        def _(q):
            first = c * CHUNK + q * 8
            at = pl.ds(pl.multiple_of(first * TILE, 8 * TILE), 8 * TILE)
            yf = y_ref[:, at].astype(jnp.float32)
            half = (-0.5 * kappa) * jnp.sum(yf * yf, axis=0, keepdims=True)
            for k in range(8):
                g_ref[pl.ds(first + k, 1), :] = half[:, k * TILE : (k + 1) * TILE]


def row_pass_kernel(kappa, slots, *refs):
    if kappa is not None:
        (cols, counts, x_hbm, y_hbm, out_ref, x_ref, x2_ref, y_ref, g_ref, hx_ref,
         total, x_in, x_sem, y_sem) = refs
        f_ref = None
        prepare(kappa, x_hbm, y_hbm, x_ref, x2_ref, y_ref, g_ref, hx_ref, x_in, x_sem, y_sem)
    else:
        cols, counts, x_ref, y_ref, f_ref, g_ref, out_ref, total = refs
    blocks = out_ref.shape[0]
    lane = lax.broadcasted_iota(jnp.int32, (TILE, TILE), 1)

    @pl.loop(0, blocks, unroll=UNROLL)
    def _(r):
        scores = products(x_ref, y_ref, f_ref, cols, slots, r)
        terms = None
        for k, row in enumerate(shifts(cols, counts, g_ref, slots, r)):
            term = jnp.exp2(scores[:, k * TILE : (k + 1) * TILE] + row)
            terms = term if terms is None else terms + term
        summed = jnp.sum(terms, axis=1, keepdims=True)
        total[...] = jnp.where(lane == r, summed, total[...])

    sums = total[...]
    out_ref[...] = jnp.log2(sums).T
    fine = jnp.logical_and(jnp.min(sums) >= SMALLEST, jnp.max(sums) <= LARGEST)

    @pl.when(jnp.logical_not(fine))
    def _():
        @pl.loop(0, blocks)
        def _(r):
            scores = products(x_ref, y_ref, f_ref, cols, slots, r)
            rows = shifts(cols, counts, g_ref, slots, r)
            parts = [scores[:, k * TILE : (k + 1) * TILE] + row for k, row in enumerate(rows)]
            top = functools.reduce(jnp.maximum, parts)
            top = jnp.max(top, axis=1, keepdims=True)
            terms = sum(jnp.exp2(part - top) for part in parts)
            summed = jnp.sum(terms, axis=1, keepdims=True)
            total[...] = jnp.where(lane == r, top + jnp.log2(summed), total[...])

        out_ref[...] = total[...].T


def col_pass_kernel(slots, with_mass, *refs):
    if with_mass:
        cols, counts, x_ref, y_ref, f_ref, g_ref, mass_ref, out_ref, total = refs
    else:
        cols, counts, x_ref, y_ref, f_ref, g_ref, out_ref, total = refs
    blocks = f_ref.shape[0]
    devices, height, _ = out_ref.shape
    own = total.shape[0] // devices
    total[...] = jnp.zeros_like(total)

    def visit(r, carry):
        least, most = carry
        scores = products(x_ref, y_ref, f_ref, cols, slots, r)
        live = counts[r]
        for k, row in enumerate(shifts(cols, counts, g_ref, slots, r)):
            terms = jnp.exp2(scores[:, k * TILE : (k + 1) * TILE] + row)
            summed = jnp.sum(terms, axis=0, keepdims=True)
            total[pl.ds(cols[r * slots + k], 1), :] += summed
            least = jnp.minimum(least, jnp.where(k < live, summed, 1.0))
            most = jnp.maximum(most, summed)
        return least, most

    ones = jnp.ones((1, TILE), jnp.float32)
    least, most = lax.fori_loop(0, blocks, visit, (ones, ones), unroll=UNROLL)
    fine = jnp.logical_and(jnp.min(least) >= SMALLEST, jnp.max(most) <= LARGEST / blocks)

    @pl.when(fine)
    def _():
        sums = total[...]
        total[...] = jnp.where(sums > 0.0, jnp.log2(sums), very_negative)

    @pl.when(jnp.logical_not(fine))
    def _():
        total[...] = jnp.full_like(total, very_negative)

        @pl.loop(0, blocks)
        def _(r):
            scores = products(x_ref, y_ref, f_ref, cols, slots, r)
            live = counts[r]
            for k, row in enumerate(shifts(cols, counts, g_ref, slots, r)):

                @pl.when(k < live)
                def _():
                    part = scores[:, k * TILE : (k + 1) * TILE] + row
                    top = jnp.max(part, axis=0, keepdims=True)
                    mine = top + jnp.log2(
                        jnp.sum(jnp.exp2(part - top), axis=0, keepdims=True)
                    )
                    at = pl.ds(cols[r * slots + k], 1)
                    old = total[at, :]
                    peak = jnp.maximum(old, mine)
                    total[at, :] = peak + jnp.log2(jnp.exp2(old - peak) + jnp.exp2(mine - peak))

    out_ref[:, :own, :] = total[...].reshape(devices, own, TILE)
    if with_mass:
        mass = mass_ref[...]
        mass = jnp.sum(jnp.sum(mass, axis=0, keepdims=True), axis=1, keepdims=True)
        out_ref[:, own:, :] = jnp.broadcast_to(
            jnp.log2(mass)[None], (devices, height - own, TILE)
        )


SMEM = functools.partial(pl.BlockSpec, memory_space=pltpu.SMEM)
VMEM = functools.partial(pl.BlockSpec, memory_space=pltpu.VMEM)
ANY = functools.partial(pl.BlockSpec, memory_space=pl.ANY)


def first_row_pass(cols, counts, source_points, target_points, slots):
    width, rows = source_points.shape
    blocks = rows // TILE
    target_blocks = target_points.shape[1] // TILE
    shape = jax.ShapeDtypeStruct
    bf16, f32 = jnp.bfloat16, jnp.float32
    return pl.pallas_call(
        functools.partial(row_pass_kernel, LOG2E / first_epsilon, slots),
        out_shape=(
            shape((blocks, TILE), f32),
            pltpu.VMEM((blocks, TILE, 2 * width), bf16),
            pltpu.VMEM((blocks, TILE, 2 * width), bf16),
            pltpu.VMEM(target_points.shape, bf16),
            shape((target_blocks, TILE), f32),
            shape((blocks, TILE), f32),
        ),
        in_specs=[SMEM(), SMEM(), ANY(), ANY()],
        out_specs=(VMEM(),) * 6,
        scratch_shapes=[
            pltpu.VMEM((TILE, blocks), f32),
            pltpu.VMEM(source_points.shape, bf16),
            pltpu.SemaphoreType.DMA,
            pltpu.SemaphoreType.DMA((target_blocks // CHUNK,)),
        ],
        name="row_pass_first",
        compiler_params=pltpu.CompilerParams(vmem_limit_bytes=VMEM_LIMIT),
    )(
        cols,
        counts,
        pltpu.with_memory_space_constraint(source_points, pltpu.HBM),
        pltpu.with_memory_space_constraint(target_points, pltpu.HBM),
    )


def row_pass(cols, counts, x, y, f_pot, g_pot, slots):
    return pl.pallas_call(
        functools.partial(row_pass_kernel, None, slots),
        out_shape=jax.ShapeDtypeStruct(f_pot.shape, jnp.float32),
        in_specs=[SMEM(), SMEM(), VMEM(), VMEM(), VMEM(), VMEM()],
        out_specs=VMEM(),
        scratch_shapes=[pltpu.VMEM((TILE, f_pot.shape[0]), jnp.float32)],
        name="row_pass",
        compiler_params=pltpu.CompilerParams(vmem_limit_bytes=VMEM_LIMIT),
    )(cols, counts, x, y, f_pot, g_pot)


def col_pass(cols, counts, x, y, f_pot, g_pot, mass, slots, devices):
    target_blocks = g_pot.shape[0]
    height = target_blocks // devices + (8 if mass is not None else 0)
    extra = () if mass is None else (mass,)
    return pl.pallas_call(
        functools.partial(col_pass_kernel, slots, mass is not None),
        out_shape=jax.ShapeDtypeStruct((devices, height, TILE), jnp.float32),
        in_specs=[SMEM(), SMEM()] + [VMEM()] * (4 + len(extra)),
        out_specs=VMEM(),
        scratch_shapes=[pltpu.VMEM((target_blocks, TILE), jnp.float32)],
        name="col_pass",
        compiler_params=pltpu.CompilerParams(vmem_limit_bytes=VMEM_LIMIT),
    )(cols, counts, x, y, f_pot, g_pot, *extra)


def lse(stack):
    top = jnp.max(stack, axis=0)
    return top + jnp.log2(jnp.sum(jnp.exp2(stack - top[None]), axis=0))


def shift_z(value, by, cols):
    return lax.ppermute(value, "col", [(i, (i + 2 * by) % cols) for i in range(cols)])


def over_cols(part, cols):
    half = part.shape[0] // 2
    core = lax.axis_index("col") % 2
    swap = [(i, i ^ 1) for i in range(cols)]
    away = lax.dynamic_slice_in_dim(part, (1 - core) * half, half, 0)
    mine = lax.dynamic_slice_in_dim(part, core * half, half, 0)
    mine = lse(jnp.stack([mine, lax.ppermute(away, "col", swap)]))
    chips = cols // 2
    mine = lse(jnp.stack([mine] + [shift_z(mine, by, cols) for by in range(1, chips)]))
    other = lax.ppermute(mine, "col", swap)
    low = jnp.where(core == 0, mine, other)
    high = jnp.where(core == 0, other, mine)
    return jnp.concatenate([low, high], axis=0)


def body(source_points, target_points, source_mass, target_mass, tile_cols, tile_counts):
    width, rows = source_points.shape
    row_blocks = rows // TILE
    target_cells = target_points.shape[1]
    target_blocks = target_cells // TILE
    slots = tile_cols.shape[2]
    row_devices = lax.axis_size("row")
    col_devices = lax.axis_size("col")
    own_blocks = target_blocks // row_devices
    me = lax.axis_index("row")
    f32 = jnp.float32

    cols = tile_cols.reshape(row_blocks * slots)
    counts = tile_counts.reshape(row_blocks)
    mass_a = source_mass.reshape(row_blocks, TILE)
    log_a = jnp.log2(mass_a)
    own_mass = lax.dynamic_slice_in_dim(target_mass, me * own_blocks * TILE, own_blocks * TILE, 0)
    log_b = jnp.log2(own_mass).reshape(own_blocks, TILE)
    part_b = jnp.log2(jnp.sum(target_mass))

    part, x1, x2, y, g_pot, half_x = first_row_pass(
        cols, counts, source_points, target_points, slots
    )
    x1, x2, y = (pltpu.with_memory_space_constraint(v, pltpu.VMEM) for v in (x1, x2, y))

    f_pot = jnp.zeros((row_blocks, TILE), f32)
    g_own = lax.dynamic_slice_in_dim(g_pot, me * own_blocks, own_blocks, 0)
    half_own = g_own * (-LN2 * first_epsilon)
    total_a = total_b = None
    for step in range(ITERS):
        epsilon = first_epsilon * 0.5**step
        x = x1 if step == 0 else x2
        if step > 0:
            part = row_pass(cols, counts, x, y, f_pot, g_pot, slots)
        if step == 0:
            extra = jnp.full((16, TILE), part_b, f32)
            both = over_cols(jnp.concatenate([part, extra], axis=0), col_devices)
            part, total_b = both[:row_blocks], both[row_blocks, 0]
        else:
            part = over_cols(part, col_devices)
        f_pot = f_pot + (log_a - part)

        part = col_pass(
            cols, counts, x, y, f_pot, g_pot, mass_a if step == 0 else None, slots, row_devices
        )
        part = lse(lax.all_to_all(part, "row", 0, 0))
        if step == 0:
            part, total_a = part[:own_blocks], part[own_blocks, 0]
        g_own = g_own + (log_b - part)
        if step < ITERS - 1:
            g_own, f_pot = 2.0 * g_own, 2.0 * f_pot
            send = g_own
        else:
            both_eps = first_epsilon * (2.0 - 0.5**step)
            send = LN2 * (epsilon * g_own + both_eps * (total_a - total_b)) + half_own
        g_pot = lax.all_to_all(
            jnp.broadcast_to(send[None], (row_devices, own_blocks, TILE)), "row", 0, 0
        ).reshape(target_blocks, TILE)

    earlier = first_epsilon * (2.0 - 0.5 ** (ITERS - 1)) - epsilon
    source = half_x + LN2 * (
        epsilon * f_pot - epsilon * total_a - earlier * (total_a - total_b)
    )
    return (source.reshape(rows), g_pot.reshape(target_cells))


def solution(mesh):
    return jax.shard_map(
        body,
        mesh=mesh,
        in_specs=(
            P(None, "row"),
            P(None, "col"),
            P("row"),
            P("col"),
            P("row", "col", None),
            P("row", "col"),
        ),
        out_specs=(P("row"), P("col")),
        check_vma=False,
    )
```

time: 317 us -> 215 us (0.68)
  Pallas kernels: 152 us -> 91 us
  starting transfers between devices: 72.9 us -> 23.5 us
  local copies, waits for them, and re-layouts: 18.6 us -> 29.9 us
  other arithmetic: 8.89 us -> 4.58 us
    pallas_call x4, Pallas kernels: 152 us -> 91 us  [the longest x1 59.2 us: row_pass(): pl.pallas_call(functools.partial(row_pass_kernel, None, slots), out_shape...]
    ppermute x6, starting transfers between devices: 58.5 us -> 8.98 us  [shift_z(): lax.ppermute(value, 'col', [(i, (i + 2 * by) % cols) for i in range(cols)])]
    unnamed x16 -> x22, local copies, waits for them, and re-layouts: 12.4 us -> 27.8 us
  transfers between devices with their start and end apart: 13 -> 13, of which waited for: 10 -> 12; matrix products, arithmetic and copies ran while one was open for 1% -> 0% of each run, Pallas kernels for 0% -> 0%
where the time goes in v2:
time: 215 us; the launch traced here: 214 us
  Pallas kernels  91 us (42%)
  waiting for transfers between devices  47.3 us (22%)
  local copies, waits for them, and re-layouts  29.9 us (14%)
  starting transfers between devices  23.5 us (11%)
  blocking collectives  14.5 us (7%)
  other arithmetic  4.58 us (2%)
  between operations  3.59 us (2%)
    pallas_call x1, Pallas kernels, row_pass(): pl.pallas_call(functools.partial(row_pass_kernel, None, slots), out_shape...  59.2 us
    unnamed x22, local copies, waits for them, and re-layouts  27.8 us
    all_to_all x2, waiting for transfers between devices, body(): part = lse(lax.all_to_all(part, 'row', 0, 0))  24.9 us
    pallas_call x2, Pallas kernels, col_pass(): pl.pallas_call(functools.partial(col_pass_kernel, slots, mass is not None...  17 us
    pallas_call x1, Pallas kernels, first_row_pass(): pl.pallas_call(functools.partial(row_pass_kernel, LOG2E / first_epsilon,...  14.9 us
    all_to_all x1, blocking collectives, body(): lax.all_to_all(jnp.broadcast_to(send[None], (row_devices, own_blocks, TIL...  14.5 us
    all_to_all x1, waiting for transfers between devices, body(): lax.all_to_all(jnp.broadcast_to(send[None], (row_devices, own_blocks, TIL...  10.7 us
    all_to_all x2, starting transfers between devices, body(): part = lse(lax.all_to_all(part, 'row', 0, 0))  10.6 us
  transfers between devices with their start and end apart: 13, of which 12 were waited for; matrix products, arithmetic and copies ran while one was open for 0% of the time, Pallas kernels for 0%

profile of v2, /device:TPU:0, one launch (start us, length us, event | category | flops | bytes accessed | tf_op | source)
XLA Modules:
  0.0 214.4 jit_solution(2715893300087359773)
XLA Ops:
  0.6 1.8 reduce_sum.63
  3.1 0.8 copy.8
  3.9 0.1 reshape.69.refs_0_
  4.0 0.6 copy-done.8
  4.7 14.9 %row_pass_first.1 = (f32[128,128]{1,0:T(8,128)S(1)}, bf16[128,128,128]{2,1,0:T(8,128)(2,1)S(1)}, bf16[128,128,128]{2,1,0:T(8,128)(2,1)S(1)}, bf16[64,131072]{1,0...) custom-call(s32[512]{0:T(512)S(1)} %reshape.69.refs_0_, s32[128]{0:T(128)S(1)} %bitcast.45, ...), custom_call_target="tpu_custom_call" | custom-call | tf_op jit(solution)/shard_map/row_pass_first/pallas_call | solution.py:216
  19.7 5.7 %copy-done = bf16[64,131072]{1,0:T(8,128)(2,1)} copy-done((bf16[64,131072]{1,0:T(8,128)(2,1)}, bf16[64,131072]{1,0:T(8,128)(2,1)S(1)}, u32[]{:S(2)}) %copy-start) | copy-done | bytes 16777240
  25.4 1.9 copy-done.3
  27.3 2.0 copy-done.5
  29.3 0.1 collective-permute-start
  29.4 1.2 collective-permute-done
  30.7 4.2 %collective-permute-start.3 = (f32[72,128]{1,0:T(8,128)S(1)}, f32[72,128]{1,0:T(8,128)S(1)}, u32[]{:S(2)}, u32[]{:S(2)}) collective-permute-start(f32[72,128]{1,0:T(8,128)S(1)} %multiply_add_fusion.2), channel_id=1, source_target_pairs={{0,6},{1,7},{2,0},{3,1},{4,2},{5,3},{6,4},{7,5},{8,14},{9,15},{10,... | collective-permute-start | bytes 110600 | tf_op jit(solution)/shard_map/ppermute | solution.py:277
  34.8 1.3 collective-permute-start.1
  36.1 0.3 collective-permute-done.3
  36.5 3.9 %collective-permute-done.2 = f32[72,128]{1,0:T(8,128)S(1)} collective-permute-done((f32[72,128]{1,0:T(8,128)S(1)}, f32[72,128]{1,0:T(8,128)S(1)}, u32[]{:S(2)}, u32[]{:S(2)}) %collective-permute-start.2) | collective-permute-done | bytes 36896 | tf_op jit(solution)/shard_map/ppermute | solution.py:277
  40.5 0.1 collective-permute-start.4
  40.6 1.2 collective-permute-done.4
  41.9 5.8 %copy-done.1 = bf16[64,131072]{1,0:T(8,128)(2,1)S(1)} copy-done((bf16[64,131072]{1,0:T(8,128)(2,1)S(1)}, bf16[64,131072]{1,0:T(8,128)(2,1)}, u32[]{:S(2)}) %copy-start.1) | copy-done | bytes 16777240
  47.6 2.2 %copy-done.6 = bf16[128,128,128]{2,1,0:T(8,128)(2,1)S(1)} copy-done((bf16[128,128,128]{2,1,0:T(8,128)(2,1)S(1)}, bf16[128,128,128]{2,1,0:T(8,128)(2,1)}, u32[]{:S(2)}) %copy-start.6) | copy-done | bytes 4194328
  49.8 8.5 %col_pass.2 = f32[16,72,128]{2,1,0:T(8,128)} custom-call(s32[512]{0:T(512)S(1)} %reshape.69.refs_0_, s32[128]{0:T(128)S(1)} %bitcast.46, bf16[128,128,128]{2,1,0:T(8,128)(2,1)S(1)} %copy-done.6, bf16[64,131072]{1,0:T(8,128)(2,1)S(1)} %copy-done.1, f32[128,128]{1,0:T(8,128)S(1)} %get-tuple-element.17.refs_4_, f32[1024,128]{1,0:T(8,128)S(1)} %get-tuple-element.12.refs_5_, ...), custom_call_target="tpu_custom_call" | custom-call | tf_op jit(solution)/shard_map/col_pass/pallas_call | solution.py:260
  58.3 7.1 %all-to-all-start = ((f32[16,72,128]{2,1,0:T(8,128)}), f32[16,72,128]{2,1,0:T(8,128)S(1)}, u32[]{:S(2)}, u32[]{:S(2)}) async-start(f32[16,72,128]{2,1,0:T(8,128)} %col_pass.2), calls=%async_computation | async-start | bytes 1179648 | tf_op jit(solution)/shard_map/all_to_all | solution.py:340
  65.4 12.5 %all-to-all-done = f32[16,72,128]{2,1,0:T(8,128)S(1)} async-done(((f32[16,72,128]{2,1,0:T(8,128)}), f32[16,72,128]{2,1,0:T(8,128)S(1)}, u32[]{:S(2)}, u32[]{:S(2)}) %all-to-all-start) | async-done | bytes 589856 | tf_op jit(solution)/shard_map/all_to_all | solution.py:340
  78.0 0.1 exponential_reduce_fusion
  78.1 0.8 fusion.15
  78.9 0.8 broadcast_in_dim.4
  79.8 3.6 %all-to-all-start.1 = ((f32[16,64,128]{2,1,0:T(8,128)}), f32[16,64,128]{2,1,0:T(8,128)S(1)}, u32[]{:S(2)}, u32[]{:S(2)}) async-start(f32[16,64,128]{2,1,0:T(8,128)} %broadcast_in_dim.4), calls=%async_computation.1 | async-start | bytes 1048576 | tf_op jit(solution)/shard_map/all_to_all | solution.py:350
  83.4 10.7 %all-to-all-done.1 = f32[16,64,128]{2,1,0:T(8,128)S(1)} async-done(((f32[16,64,128]{2,1,0:T(8,128)}), f32[16,64,128]{2,1,0:T(8,128)S(1)}, u32[]{:S(2)}, u32[]{:S(2)}) %all-to-all-start.1) | async-done | bytes 524320 | tf_op jit(solution)/shard_map/all_to_all | solution.py:350
  94.0 5.8 %copy-done.2 = bf16[64,131072]{1,0:T(8,128)(2,1)S(1)} copy-done((bf16[64,131072]{1,0:T(8,128)(2,1)S(1)}, bf16[64,131072]{1,0:T(8,128)(2,1)}, u32[]{:S(2)}) %copy-start.2) | copy-done | bytes 16777240
  99.8 2.2 %copy-done.4 = bf16[128,128,128]{2,1,0:T(8,128)(2,1)S(1)} copy-done((bf16[128,128,128]{2,1,0:T(8,128)(2,1)S(1)}, bf16[128,128,128]{2,1,0:T(8,128)(2,1)}, u32[]{:S(2)}) %copy-start.4) | copy-done | bytes 4194328
  102.0 59.2 %row_pass.1 = f32[128,128]{1,0:T(8,128)S(1)} custom-call(s32[512]{0:T(512)S(1)} %reshape.69.refs_0_, s32[128]{0:T(128)S(1)} %bitcast.47, bf16[128,128,128]{2,1,0:T(8,128)(2,1)S(1)} %copy-done.4, bf16[64,131072]{1,0:T(8,128)(2,1)S(1)} %copy-done.2, f32[128,128]{1,0:T(8,128)S(1)} %get-tuple-element.16.refs_4_, f32[1024,128]{1,0:T(8,128)S(1)} %bitcast.42), custom_call_target="tpu_custom_call" | custom-call | tf_op jit(solution)/shard_map/row_pass/pallas_call | solution.py:245
  161.2 0.1 collective-permute-start.5
  161.3 1.2 collective-permute-done.5
  162.5 0.1 collective-permute-start.8
  162.6 2.1 collective-permute-start.7
  164.7 1.3 collective-permute-start.6
  166.0 0.5 collective-permute-done.8
  166.5 1.6 collective-permute-done.7
  168.1 1.7 collective-permute-done.6
  169.9 0.1 collective-permute-start.9
  170.0 0.5 slice.18
  170.5 0.5 slice.17
  173.0 0.7 add_bitcast_fusion
  173.7 8.4 %col_pass.3 = f32[16,64,128]{2,1,0:T(8,128)} custom-call(s32[512]{0:T(512)S(1)} %reshape.69.refs_0_, s32[128]{0:T(128)S(1)} %bitcast.48, bf16[128,128,128]{2,1,0:T(8,128)(2,1)S(1)} %copy-done.4, bf16[64,131072]{1,0:T(8,128)(2,1)S(1)} %copy-done.2, f32[128,128]{1,0:T(8,128)S(1)} %get-tuple-element.15.refs_4_, f32[1024,128]{1,0:T(8,128)S(1)} %bitcast.43), custom_call_target="tpu_custom_call" | custom-call | tf_op jit(solution)/shard_map/col_pass/pallas_call | solution.py:260
  182.1 3.6 %all-to-all-start.2 = ((f32[16,64,128]{2,1,0:T(8,128)}), f32[16,64,128]{2,1,0:T(8,128)S(1)}, u32[]{:S(2)}, u32[]{:S(2)}) async-start(f32[16,64,128]{2,1,0:T(8,128)} %col_pass.3), calls=%async_computation.2 | async-start | bytes 1048576 | tf_op jit(solution)/shard_map/all_to_all | solution.py:340
  185.7 12.4 %all-to-all-done.2 = f32[16,64,128]{2,1,0:T(8,128)S(1)} async-done(((f32[16,64,128]{2,1,0:T(8,128)}), f32[16,64,128]{2,1,0:T(8,128)S(1)}, u32[]{:S(2)}, u32[]{:S(2)}) %all-to-all-start.2) | async-done | bytes 524320 | tf_op jit(solution)/shard_map/all_to_all | solution.py:340
  198.1 0.1 exponential_reduce_fusion.1
  198.2 0.8 fusion.20
  199.1 14.5 %all_to_all.20 = f32[16,64,128]{2,1,0:T(8,128)S(1)} all-to-all(f32[16,64,128]{2,1,0:T(8,128)S(1)} %broadcast_in_dim.5), channel_id=1, replica_groups=mesh['row'=16,'col'=8] {'row'}, dimensions={0} | all-to-all | bytes 1048576 | tf_op jit(solution)/shard_map/all_to_all | solution.py:350
  213.6 0.8 copy.10
  (36 shorter events, 0.5 us)
Async XLA Ops:
  4.0 0.7 copy-start.8
  4.7 37.1 %copy-start.7 = (f32[16384]{0:T(1024)S(1)}, f32[16384]{0:T(1024)}, u32[]{:S(2)}) copy-start(f32[16384]{0:T(1024)} %param.8) | copy-start | bytes 196612
  4.7 37.1 %copy-start.9 = (s32[128,1]{0,1:T(1,128)S(1)}, s32[128,1]{0,1:T(1,128)}, u32[]{:S(2)}) copy-start(s32[128,1]{0,1:T(1,128)} %param.11) | copy-start | bytes 1540
  19.6 5.7 %copy-start = (bf16[64,131072]{1,0:T(8,128)(2,1)}, bf16[64,131072]{1,0:T(8,128)(2,1)S(1)}, u32[]{:S(2)}) copy-start(bf16[64,131072]{1,0:T(8,128)(2,1)S(1)} %get-tuple-element.11.refs_3_) | copy-start | bytes 50331652
  25.4 1.9 copy-start.3
  27.3 2.0 copy-start.5
  29.3 1.3 collective-permute-start
  30.7 5.8 %collective-permute-start.3 = (f32[72,128]{1,0:T(8,128)S(1)}, f32[72,128]{1,0:T(8,128)S(1)}, u32[]{:S(2)}, u32[]{:S(2)}) collective-permute-start(f32[72,128]{1,0:T(8,128)S(1)} %multiply_add_fusion.2), channel_id=1, source_target_pairs={{0,6},{1,7},{2,0},{3,1},{4,2},{5,3},{6,4},{7,5},{8,14},{9,15},{10,... | collective-permute-start | bytes 110600 | tf_op jit(solution)/shard_map/ppermute | solution.py:277
  34.8 5.5 %collective-permute-start.2 = (f32[72,128]{1,0:T(8,128)S(1)}, f32[72,128]{1,0:T(8,128)S(1)}, u32[]{:S(2)}, u32[]{:S(2)}) collective-permute-start(f32[72,128]{1,0:T(8,128)S(1)} %multiply_add_fusion.2), channel_id=1, source_target_pairs={{0,4},{1,5},{2,6},{3,7},{4,0},{5,1},{6,2},{7,3},{8,12},{9,13},{10,... | collective-permute-start | bytes 110600 | tf_op jit(solution)/shard_map/ppermute | solution.py:277
  34.8 5.6 %collective-permute-start.1 = (f32[72,128]{1,0:T(8,128)S(1)}, f32[72,128]{1,0:T(8,128)S(1)}, u32[]{:S(2)}, u32[]{:S(2)}) collective-permute-start(f32[72,128]{1,0:T(8,128)S(1)} %multiply_add_fusion.2), channel_id=1, source_target_pairs={{0,2},{1,3},{2,4},{3,5},{4,6},{5,7},{6,0},{7,1},{8,10},{9,11},{10,... | collective-permute-start | bytes 110600 | tf_op jit(solution)/shard_map/ppermute | solution.py:277
  40.5 1.3 collective-permute-start.4
  41.8 5.8 %copy-start.1 = (bf16[64,131072]{1,0:T(8,128)(2,1)S(1)}, bf16[64,131072]{1,0:T(8,128)(2,1)}, u32[]{:S(2)}) copy-start(bf16[64,131072]{1,0:T(8,128)(2,1)} %copy-done) | copy-start | bytes 50331652
  47.6 2.2 %copy-start.6 = (bf16[128,128,128]{2,1,0:T(8,128)(2,1)S(1)}, bf16[128,128,128]{2,1,0:T(8,128)(2,1)}, u32[]{:S(2)}) copy-start(bf16[128,128,128]{2,1,0:T(8,128)(2,1)} %copy-done.5) | copy-start | bytes 12582916
  58.3 19.6 %all-to-all-start = ((f32[16,72,128]{2,1,0:T(8,128)}), f32[16,72,128]{2,1,0:T(8,128)S(1)}, u32[]{:S(2)}, u32[]{:S(2)}) async-start(f32[16,72,128]{2,1,0:T(8,128)} %col_pass.2), calls=%async_computation | async-start | bytes 1179648 | tf_op jit(solution)/shard_map/all_to_all | solution.py:340
  79.8 14.3 %all-to-all-start.1 = ((f32[16,64,128]{2,1,0:T(8,128)}), f32[16,64,128]{2,1,0:T(8,128)S(1)}, u32[]{:S(2)}, u32[]{:S(2)}) async-start(f32[16,64,128]{2,1,0:T(8,128)} %broadcast_in_dim.4), calls=%async_computation.1 | async-start | bytes 1048576 | tf_op jit(solution)/shard_map/all_to_all | solution.py:350
  94.0 5.8 %copy-start.2 = (bf16[64,131072]{1,0:T(8,128)(2,1)S(1)}, bf16[64,131072]{1,0:T(8,128)(2,1)}, u32[]{:S(2)}) copy-start(bf16[64,131072]{1,0:T(8,128)(2,1)} %copy-done) | copy-start | bytes 50331652
  99.8 2.2 %copy-start.4 = (bf16[128,128,128]{2,1,0:T(8,128)(2,1)S(1)}, bf16[128,128,128]{2,1,0:T(8,128)(2,1)}, u32[]{:S(2)}) copy-start(bf16[128,128,128]{2,1,0:T(8,128)(2,1)} %copy-done.3) | copy-start | bytes 12582916
  161.2 1.3 collective-permute-start.5
  162.5 4.0 %collective-permute-start.8 = (f32[64,128]{1,0:T(8,128)S(1)}, f32[64,128]{1,0:T(8,128)S(1)}, u32[]{:S(2)}, u32[]{:S(2)}) collective-permute-start(f32[64,128]{1,0:T(8,128)S(1)} %multiply_add_fusion.4), channel_id=1, source_target_pairs={{0,6},{1,7},{2,0},{3,1},{4,2},{5,3},{6,4},{7,5},{8,14},{9,15},{10,... | collective-permute-start | bytes 98312 | tf_op jit(solution)/shard_map/ppermute | solution.py:277
  162.6 5.5 %collective-permute-start.7 = (f32[64,128]{1,0:T(8,128)S(1)}, f32[64,128]{1,0:T(8,128)S(1)}, u32[]{:S(2)}, u32[]{:S(2)}) collective-permute-start(f32[64,128]{1,0:T(8,128)S(1)} %multiply_add_fusion.4), channel_id=1, source_target_pairs={{0,4},{1,5},{2,6},{3,7},{4,0},{5,1},{6,2},{7,3},{8,12},{9,13},{10,... | collective-permute-start | bytes 98312 | tf_op jit(solution)/shard_map/ppermute | solution.py:277
  164.7 5.1 %collective-permute-start.6 = (f32[64,128]{1,0:T(8,128)S(1)}, f32[64,128]{1,0:T(8,128)S(1)}, u32[]{:S(2)}, u32[]{:S(2)}) collective-permute-start(f32[64,128]{1,0:T(8,128)S(1)} %multiply_add_fusion.4), channel_id=1, source_target_pairs={{0,2},{1,3},{2,4},{3,5},{4,6},{5,7},{6,0},{7,1},{8,10},{9,11},{10,... | collective-permute-start | bytes 98312 | tf_op jit(solution)/shard_map/ppermute | solution.py:277
  169.9 3.1 %collective-permute-start.9 = (f32[64,128]{1,0:T(8,128)S(1)}, f32[64,128]{1,0:T(8,128)S(1)}, u32[]{:S(2)}, u32[]{:S(2)}) collective-permute-start(f32[64,128]{1,0:T(8,128)S(1)} %multiply_add_fusion.3), channel_id=1, source_target_pairs={{0,1},{1,0},{2,3},{3,2},{4,5},{5,4},{6,7},{7,6},{8,9},{9,8},{10,11... | collective-permute-start | bytes 98312 | tf_op jit(solution)/shard_map/ppermute | solution.py:289
  182.1 16.0 %all-to-all-start.2 = ((f32[16,64,128]{2,1,0:T(8,128)}), f32[16,64,128]{2,1,0:T(8,128)S(1)}, u32[]{:S(2)}, u32[]{:S(2)}) async-start(f32[16,64,128]{2,1,0:T(8,128)} %col_pass.3), calls=%async_computation.2 | async-start | bytes 1048576 | tf_op jit(solution)/shard_map/all_to_all | solution.py:340

commit v3 on v2

--- a/solution.py
+++ b/solution.py
@@ -19,6 +19,8 @@
 VMEM_LIMIT = 16 * 1024 * 1024
 UNROLL = 16
 CHUNK = 64
+ROW_OFFSET = 64.0
+COL_OFFSET = 80.0
 
 
 def split3(row):
@@ -29,16 +31,16 @@
     return hi, mid, lo
 
 
-def products(x_ref, y_ref, f_ref, cols, slots, r):
+def products(x_ref, y_ref, f_ref, cols, slots, r, offset):
     lhs = x_ref[r]
     picked = [
-        y_ref[:, pl.ds(pl.multiple_of(cols[r * slots + k] * TILE, TILE), TILE)]
+        y_ref[:, pl.ds(pl.multiple_of(cols[k, r] * TILE, TILE), TILE)]
         for k in range(slots)
     ]
     yb = jnp.concatenate(picked, axis=1)
     rhs = [yb, yb]
     if f_ref is not None:
-        hi, mid, lo = split3(f_ref[pl.ds(r, 1), :])
+        hi, mid, lo = split3(f_ref[pl.ds(r, 1), :] + offset)
         place = lax.broadcasted_iota(jnp.int32, (16, TILE), 0)
         extra = jnp.where(
             place == 0, hi, jnp.where(place == 1, mid, jnp.where(place == 2, lo, 0.0))
@@ -51,12 +53,12 @@
 def shifts(cols, counts, g_ref, slots, r):
     live = counts[r]
     return [
-        jnp.where(k < live, g_ref[pl.ds(cols[r * slots + k], 1), :], very_negative)
+        jnp.where(k < live, g_ref[pl.ds(cols[k, r], 1), :], very_negative)
         for k in range(slots)
     ]
 
 
-def prepare(kappa, x_hbm, y_hbm, x_ref, x2_ref, y_ref, g_ref, hx_ref, x_in, x_sem, y_sem):
+def prepare(kappa, x_hbm, y_hbm, x_ref, x2_ref, y_ref, g_ref, hx_ref, x_in, x_sem, y_sem, others):
     width = y_ref.shape[0]
     blocks = hx_ref.shape[0]
     target_blocks = g_ref.shape[0]
@@ -67,6 +69,9 @@
     def y_copy(c):
         at = pl.ds(pl.multiple_of(c * (CHUNK * TILE), CHUNK * TILE), CHUNK * TILE)
         return pltpu.make_async_copy(y_hbm.at[:, at], y_ref.at[:, at], y_sem.at[c])
+
+    for other in others:
+        other.start()
 
     @pl.loop(0, chunks)
     def _(c):
@@ -98,21 +103,32 @@
             for k in range(8):
                 g_ref[pl.ds(first + k, 1), :] = half[:, k * TILE : (k + 1) * TILE]
 
+    for other in others:
+        other.wait()
+
 
 def row_pass_kernel(kappa, slots, *refs):
     if kappa is not None:
-        (cols, counts, x_hbm, y_hbm, out_ref, x_ref, x2_ref, y_ref, g_ref, hx_ref,
-         total, x_in, x_sem, y_sem) = refs
+        (cols, counts, first_own, a_hbm, b_hbm, x_hbm, y_hbm, out_ref, x_ref, x2_ref, y_ref,
+         g_ref, hx_ref, a_ref, b_ref, own_ref, total, x_in, b_in, sems, y_sem) = refs
         f_ref = None
-        prepare(kappa, x_hbm, y_hbm, x_ref, x2_ref, y_ref, g_ref, hx_ref, x_in, x_sem, y_sem)
+        a_copy = pltpu.make_async_copy(a_hbm, a_ref, sems.at[1])
+        b_copy = pltpu.make_async_copy(b_hbm, b_in, sems.at[2])
+        prepare(kappa, x_hbm, y_hbm, x_ref, x2_ref, y_ref, g_ref, hx_ref, x_in, sems.at[0],
+                y_sem, (a_copy, b_copy))
+        own = pl.ds(pl.multiple_of(first_own[0], own_ref.shape[0]), own_ref.shape[0])
+        own_ref[...] = g_ref[own, :]
+        b_ref[...] = jnp.log2(b_in[own, :])
+        offset = 0.0
     else:
         cols, counts, x_ref, y_ref, f_ref, g_ref, out_ref, total = refs
-    blocks = out_ref.shape[0]
+        offset = ROW_OFFSET
+    blocks = total.shape[1]
     lane = lax.broadcasted_iota(jnp.int32, (TILE, TILE), 1)
 
     @pl.loop(0, blocks, unroll=UNROLL)
     def _(r):
-        scores = products(x_ref, y_ref, f_ref, cols, slots, r)
+        scores = products(x_ref, y_ref, f_ref, cols, slots, r, offset)
         terms = None
         for k, row in enumerate(shifts(cols, counts, g_ref, slots, r)):
             term = jnp.exp2(scores[:, k * TILE : (k + 1) * TILE] + row)
@@ -121,14 +137,18 @@
         total[...] = jnp.where(lane == r, summed, total[...])
 
     sums = total[...]
-    out_ref[...] = jnp.log2(sums).T
+    out_ref[:blocks, :] = (jnp.log2(sums) - offset).T
+    if kappa is not None:
+        mass = jnp.sum(jnp.sum(b_in[...], axis=0, keepdims=True), axis=1, keepdims=True)
+        out_ref[blocks:, :] = jnp.broadcast_to(jnp.log2(mass), (8, TILE))
+        a_ref[...] = jnp.log2(a_ref[...])
     fine = jnp.logical_and(jnp.min(sums) >= SMALLEST, jnp.max(sums) <= LARGEST)
 
     @pl.when(jnp.logical_not(fine))
     def _():
         @pl.loop(0, blocks)
         def _(r):
-            scores = products(x_ref, y_ref, f_ref, cols, slots, r)
+            scores = products(x_ref, y_ref, f_ref, cols, slots, r, offset)
             rows = shifts(cols, counts, g_ref, slots, r)
             parts = [scores[:, k * TILE : (k + 1) * TILE] + row for k, row in enumerate(rows)]
             top = functools.reduce(jnp.maximum, parts)
@@ -137,7 +157,7 @@
             summed = jnp.sum(terms, axis=1, keepdims=True)
             total[...] = jnp.where(lane == r, top + jnp.log2(summed), total[...])
 
-        out_ref[...] = total[...].T
+        out_ref[:blocks, :] = (total[...] - offset).T
 
 
 def col_pass_kernel(slots, with_mass, *refs):
@@ -152,12 +172,12 @@
 
     def visit(r, carry):
         least, most = carry
-        scores = products(x_ref, y_ref, f_ref, cols, slots, r)
+        scores = products(x_ref, y_ref, f_ref, cols, slots, r, COL_OFFSET)
         live = counts[r]
         for k, row in enumerate(shifts(cols, counts, g_ref, slots, r)):
             terms = jnp.exp2(scores[:, k * TILE : (k + 1) * TILE] + row)
             summed = jnp.sum(terms, axis=0, keepdims=True)
-            total[pl.ds(cols[r * slots + k], 1), :] += summed
+            total[pl.ds(cols[k, r], 1), :] += summed
             least = jnp.minimum(least, jnp.where(k < live, summed, 1.0))
             most = jnp.maximum(most, summed)
         return least, most
@@ -169,7 +189,7 @@
     @pl.when(fine)
     def _():
         sums = total[...]
-        total[...] = jnp.where(sums > 0.0, jnp.log2(sums), very_negative)
+        total[...] = jnp.where(sums > 0.0, jnp.log2(sums) - COL_OFFSET, very_negative)
 
     @pl.when(jnp.logical_not(fine))
     def _():
@@ -177,7 +197,7 @@
 
         @pl.loop(0, blocks)
         def _(r):
-            scores = products(x_ref, y_ref, f_ref, cols, slots, r)
+            scores = products(x_ref, y_ref, f_ref, cols, slots, r, COL_OFFSET)
             live = counts[r]
             for k, row in enumerate(shifts(cols, counts, g_ref, slots, r)):
 
@@ -185,10 +205,9 @@
                 def _():
                     part = scores[:, k * TILE : (k + 1) * TILE] + row
                     top = jnp.max(part, axis=0, keepdims=True)
-                    mine = top + jnp.log2(
-                        jnp.sum(jnp.exp2(part - top), axis=0, keepdims=True)
-                    )
-                    at = pl.ds(cols[r * slots + k], 1)
+                    summed = jnp.sum(jnp.exp2(part - top), axis=0, keepdims=True)
+                    mine = top - COL_OFFSET + jnp.log2(summed)
+                    at = pl.ds(cols[k, r], 1)
                     old = total[at, :]
                     peak = jnp.maximum(old, mine)
                     total[at, :] = peak + jnp.log2(jnp.exp2(old - peak) + jnp.exp2(mine - peak))
@@ -207,38 +226,42 @@
 ANY = functools.partial(pl.BlockSpec, memory_space=pl.ANY)
 
 
-def first_row_pass(cols, counts, source_points, target_points, slots):
+def first_row_pass(cols, counts, own, source_mass, target_mass, source_points, target_points, slots):
     width, rows = source_points.shape
     blocks = rows // TILE
     target_blocks = target_points.shape[1] // TILE
+    devices = lax.axis_size("row")
     shape = jax.ShapeDtypeStruct
     bf16, f32 = jnp.bfloat16, jnp.float32
+    in_hbm = [
+        pltpu.with_memory_space_constraint(v, pltpu.HBM)
+        for v in (source_mass, target_mass, source_points, target_points)
+    ]
     return pl.pallas_call(
         functools.partial(row_pass_kernel, LOG2E / first_epsilon, slots),
         out_shape=(
-            shape((blocks, TILE), f32),
+            shape((blocks + 8, TILE), f32),
             pltpu.VMEM((blocks, TILE, 2 * width), bf16),
             pltpu.VMEM((blocks, TILE, 2 * width), bf16),
             pltpu.VMEM(target_points.shape, bf16),
             shape((target_blocks, TILE), f32),
             shape((blocks, TILE), f32),
+            shape((blocks, TILE), f32),
+            shape((target_blocks // devices, TILE), f32),
+            shape((target_blocks // devices, TILE), f32),
         ),
-        in_specs=[SMEM(), SMEM(), ANY(), ANY()],
-        out_specs=(VMEM(),) * 6,
+        in_specs=[SMEM(), SMEM(), SMEM(), ANY(), ANY(), ANY(), ANY()],
+        out_specs=(VMEM(),) * 9,
         scratch_shapes=[
             pltpu.VMEM((TILE, blocks), f32),
             pltpu.VMEM(source_points.shape, bf16),
-            pltpu.SemaphoreType.DMA,
+            pltpu.VMEM((target_blocks, TILE), f32),
+            pltpu.SemaphoreType.DMA((3,)),
             pltpu.SemaphoreType.DMA((target_blocks // CHUNK,)),
         ],
         name="row_pass_first",
         compiler_params=pltpu.CompilerParams(vmem_limit_bytes=VMEM_LIMIT),
-    )(
-        cols,
-        counts,
-        pltpu.with_memory_space_constraint(source_points, pltpu.HBM),
-        pltpu.with_memory_space_constraint(target_points, pltpu.HBM),
-    )
+    )(cols, counts, own, *in_hbm)
 
 
 def row_pass(cols, counts, x, y, f_pot, g_pot, slots):
@@ -273,23 +296,21 @@
     return top + jnp.log2(jnp.sum(jnp.exp2(stack - top[None]), axis=0))
 
 
-def shift_z(value, by, cols):
-    return lax.ppermute(value, "col", [(i, (i + 2 * by) % cols) for i in range(cols)])
+def lse_two(one, two):
+    top = jnp.maximum(one, two)
+    return top + jnp.log2(1.0 + jnp.exp2(jnp.minimum(one, two) - top))
 
 
 def over_cols(part, cols):
-    half = part.shape[0] // 2
-    core = lax.axis_index("col") % 2
-    swap = [(i, i ^ 1) for i in range(cols)]
-    away = lax.dynamic_slice_in_dim(part, (1 - core) * half, half, 0)
-    mine = lax.dynamic_slice_in_dim(part, core * half, half, 0)
-    mine = lse(jnp.stack([mine, lax.ppermute(away, "col", swap)]))
-    chips = cols // 2
-    mine = lse(jnp.stack([mine] + [shift_z(mine, by, cols) for by in range(1, chips)]))
-    other = lax.ppermute(mine, "col", swap)
-    low = jnp.where(core == 0, mine, other)
-    high = jnp.where(core == 0, other, mine)
-    return jnp.concatenate([low, high], axis=0)
+    for mask in (1, 2, 6):
+        pairs = [(i, i ^ mask) for i in range(cols)]
+        part = lse_two(part, lax.ppermute(part, "col", pairs))
+    return part
+
+
+def exchange(blocks, rest):
+    blocks, rest = lax.optimization_barrier((blocks, rest))
+    return lax.optimization_barrier((lax.all_to_all(blocks, "row", 0, 0), rest))
 
 
 def body(source_points, target_points, source_mass, target_mass, tile_cols, tile_counts):
@@ -301,61 +322,70 @@
     row_devices = lax.axis_size("row")
     col_devices = lax.axis_size("col")
     own_blocks = target_blocks // row_devices
-    me = lax.axis_index("row")
-    f32 = jnp.float32
-
-    cols = tile_cols.reshape(row_blocks * slots)
+
+    cols = tile_cols.transpose(1, 2, 0).reshape(slots, row_blocks)
     counts = tile_counts.reshape(row_blocks)
     mass_a = source_mass.reshape(row_blocks, TILE)
-    log_a = jnp.log2(mass_a)
-    own_mass = lax.dynamic_slice_in_dim(target_mass, me * own_blocks * TILE, own_blocks * TILE, 0)
-    log_b = jnp.log2(own_mass).reshape(own_blocks, TILE)
-    part_b = jnp.log2(jnp.sum(target_mass))
-
-    part, x1, x2, y, g_pot, half_x = first_row_pass(
-        cols, counts, source_points, target_points, slots
+    first_own = (lax.axis_index("row") * own_blocks).reshape(1)
+
+    part, x1, x2, y, g_pot, half_x, log_a, log_b, g_own = first_row_pass(
+        cols,
+        counts,
+        first_own,
+        mass_a,
+        target_mass.reshape(target_blocks, TILE),
+        source_points,
+        target_points,
+        slots,
     )
     x1, x2, y = (pltpu.with_memory_space_constraint(v, pltpu.VMEM) for v in (x1, x2, y))
 
-    f_pot = jnp.zeros((row_blocks, TILE), f32)
-    g_own = lax.dynamic_slice_in_dim(g_pot, me * own_blocks, own_blocks, 0)
     half_own = g_own * (-LN2 * first_epsilon)
-    total_a = total_b = None
+    f_pot = total_a = total_b = None
     for step in range(ITERS):
         epsilon = first_epsilon * 0.5**step
         x = x1 if step == 0 else x2
-        if step > 0:
-            part = row_pass(cols, counts, x, y, f_pot, g_pot, slots)
         if step == 0:
-            extra = jnp.full((16, TILE), part_b, f32)
-            both = over_cols(jnp.concatenate([part, extra], axis=0), col_devices)
+            both = over_cols(part, col_devices)
             part, total_b = both[:row_blocks], both[row_blocks, 0]
+            f_pot = log_a - part
         else:
-            part = over_cols(part, col_devices)
-        f_pot = f_pot + (log_a - part)
+            part = over_cols(row_pass(cols, counts, x, y, f_pot, g_pot, slots), col_devices)
+            f_pot = f_pot + (log_a - part)
 
         part = col_pass(
             cols, counts, x, y, f_pot, g_pot, mass_a if step == 0 else None, slots, row_devices
         )
-        part = lse(lax.all_to_all(part, "row", 0, 0))
+        if step == ITERS - 1:
+            earlier = first_epsilon * (2.0 - 0.5**step) - epsilon
+            source = half_x + LN2 * (
+                epsilon * f_pot - epsilon * total_a - earlier * (total_a - total_b)
+            )
+            rest = (source, log_b, g_own, half_own, total_a - total_b)
+        else:
+            rest = (f_pot, half_x, log_a, log_b, g_own, half_own, total_b)
+        stack, rest = exchange(part, rest)
+        part = lse(stack)
         if step == 0:
+            f_pot, half_x, log_a, log_b, g_own, half_own, total_b = rest
             part, total_a = part[:own_blocks], part[own_blocks, 0]
+        else:
+            source, log_b, g_own, half_own, totals = rest
         g_own = g_own + (log_b - part)
         if step < ITERS - 1:
             g_own, f_pot = 2.0 * g_own, 2.0 * f_pot
             send = g_own
+            rest = (f_pot, half_x, log_a, log_b, g_own, half_own, total_a, total_b)
         else:
             both_eps = first_epsilon * (2.0 - 0.5**step)
-            send = LN2 * (epsilon * g_own + both_eps * (total_a - total_b)) + half_own
-        g_pot = lax.all_to_all(
-            jnp.broadcast_to(send[None], (row_devices, own_blocks, TILE)), "row", 0, 0
-        ).reshape(target_blocks, TILE)
-
-    earlier = first_epsilon * (2.0 - 0.5 ** (ITERS - 1)) - epsilon
-    source = half_x + LN2 * (
-        epsilon * f_pot - epsilon * total_a - earlier * (total_a - total_b)
-    )
-    return (source.reshape(rows), g_pot.reshape(target_cells))
+            send = LN2 * (epsilon * g_own + both_eps * totals) + half_own
+            rest = (source,)
+        send = jnp.broadcast_to(send[None], (row_devices, own_blocks, TILE))
+        g_pot, rest = exchange(send, rest)
+        g_pot = g_pot.reshape(target_blocks, TILE)
+        if step < ITERS - 1:
+            f_pot, half_x, log_a, log_b, g_own, half_own, total_a, total_b = rest
+    return (rest[0].reshape(rows), g_pot.reshape(target_cells))
 
 
 def solution(mesh):

time: 215 us -> 141 us (0.66)
  Pallas kernels: 91 us -> 38.8 us
  blocking collectives: 14.5 us -> 56.9 us
  waiting for transfers between devices: 47.3 us -> 11.9 us
  starting transfers between devices: 23.5 us -> 9.58 us
  local copies, waits for them, and re-layouts: 29.9 us -> 19.2 us
  other arithmetic: 4.58 us -> 1.23 us
    pallas_call x1, Pallas kernels: 59.2 us -> 8.35 us  [row_pass(): pl.pallas_call(functools.partial(row_pass_kernel, None, slots), out_shape...]
    all_to_all x1 -> x4, blocking collectives: 14.5 us -> 56.9 us  [exchange(): return lax.optimization_barrier((lax.all_to_all(blocks, 'row', 0, 0), rest))]
    all_to_all x3 -> x0, waiting for transfers between devices: 35.6 us -> none  [the longest x2 24.9 us: body(): part = lse(lax.all_to_all(part, 'row', 0, 0))]
    all_to_all x3 -> x0, starting transfers between devices: 14.2 us -> none  [the longest x2 10.6 us: body(): part = lse(lax.all_to_all(part, 'row', 0, 0))]
    unnamed x22 -> x23, local copies, waits for them, and re-layouts: 27.8 us -> 18.1 us
    ppermute x10 -> x6, starting transfers between devices: 9.32 us -> 9.58 us  [over_cols(): part = lse_two(part, lax.ppermute(part, 'col', pairs))]
    ppermute x10 -> x6, waiting for transfers between devices: 11.7 us -> 11.9 us  [over_cols(): part = lse_two(part, lax.ppermute(part, 'col', pairs))]
  transfers between devices with their start and end apart: 13 -> 6, of which waited for: 12 -> 6; matrix products, arithmetic and copies ran while one was open for 0% -> 0% of each run, Pallas kernels for 0% -> 0%
where the time goes in v3:
time: 141 us; the launch traced here: 140 us
  blocking collectives  56.9 us (40%)
  Pallas kernels  38.8 us (28%)
  local copies, waits for them, and re-layouts  19.2 us (14%)
  waiting for transfers between devices  11.9 us (8%)
  starting transfers between devices  9.58 us (7%)
  between operations  2.77 us (2%)
    all_to_all x4, blocking collectives, exchange(): return lax.optimization_barrier((lax.all_to_all(blocks, 'row', 0, 0), rest))  56.9 us
    unnamed x23, local copies, waits for them, and re-layouts  18.1 us
    pallas_call x2, Pallas kernels, col_pass(): pl.pallas_call(functools.partial(col_pass_kernel, slots, mass is not None...  15.5 us
    pallas_call x1, Pallas kernels, first_row_pass(): pl.pallas_call(functools.partial(row_pass_kernel, LOG2E / first_epsilon,...  15 us
    ppermute x6, waiting for transfers between devices, over_cols(): part = lse_two(part, lax.ppermute(part, 'col', pairs))  11.9 us
    ppermute x6, starting transfers between devices, over_cols(): part = lse_two(part, lax.ppermute(part, 'col', pairs))  9.58 us
    pallas_call x1, Pallas kernels, row_pass(): pl.pallas_call(functools.partial(row_pass_kernel, None, slots), out_shape...  8.35 us
  transfers between devices with their start and end apart: 6, of which 6 were waited for; matrix products, arithmetic and copies ran while one was open for 0% of the time, Pallas kernels for 0%

profile of v3, /device:TPU:0, one launch (start us, length us, event | category | flops | bytes accessed | tf_op | source)
XLA Modules:
  0.0 140.4 jit_solution(9558728193726147586)
XLA Ops:
  0.6 0.0 copy-start.7
  0.6 0.7 copy-done.7
  1.3 0.0 copy-start.9
  1.3 0.7 copy-done.9
  2.0 0.0 copy-start.6
  2.0 15.0 %row_pass_first.1 = (f32[136,128]{1,0:T(8,128)S(1)}, bf16[128,128,128]{2,1,0:T(8,128)(2,1)S(1)}, bf16[128,128,128]{2,1,0:T(8,128)(2,1)S(1)}, bf16[64,131072]{1,0...) custom-call(s32[4,128]{1,0:T(4,128)S(1)} %bitcast.16, ...), custom_call_target="tpu_custom_call" | custom-call | tf_op jit(solution)/shard_map/row_pass_first/pallas_call | solution.py:240
  16.9 0.0 copy-start
  16.9 0.0 copy-start.3
  17.0 0.1 collective-permute-start
  17.1 1.2 collective-permute-done
  18.3 2.1 %collective-permute-start.1 = (f32[136,128]{1,0:T(8,128)S(1)}, f32[136,128]{1,0:T(8,128)S(1)}, u32[]{:S(2)}, u32[]{:S(2)}) collective-permute-start(f32[136,128]{1,0:T(8,128)S(1)} %multiply_add_fusion.2), channel_id=1, source_target_pairs={{0,2},{1,3},{2,0},{3,1},{4,6},{5,7},{6,4},{7,5},{8,10},{9,11},{10,... | collective-permute-start | bytes 208904 | tf_op jit(solution)/shard_map/ppermute | solution.py:307
  20.4 2.5 %collective-permute-done.1 = f32[136,128]{1,0:T(8,128)S(1)} collective-permute-done((f32[136,128]{1,0:T(8,128)S(1)}, f32[136,128]{1,0:T(8,128)S(1)}, u32[]{:S(2)}, u32[]{:S(2)}) %collective-permute-start.1) | collective-permute-done | bytes 69664 | tf_op jit(solution)/shard_map/ppermute | solution.py:307
  23.0 4.0 %collective-permute-start.2 = (f32[136,128]{1,0:T(8,128)S(1)}, f32[136,128]{1,0:T(8,128)S(1)}, u32[]{:S(2)}, u32[]{:S(2)}) collective-permute-start(f32[136,128]{1,0:T(8,128)S(1)} %multiply_add_fusion.1), channel_id=1, source_target_pairs={{0,6},{1,7},{2,4},{3,5},{4,2},{5,3},{6,0},{7,1},{8,14},{9,15},{10,... | collective-permute-start | bytes 208904 | tf_op jit(solution)/shard_map/ppermute | solution.py:307
  27.0 2.3 %collective-permute-done.2 = f32[136,128]{1,0:T(8,128)S(1)} collective-permute-done((f32[136,128]{1,0:T(8,128)S(1)}, f32[136,128]{1,0:T(8,128)S(1)}, u32[]{:S(2)}, u32[]{:S(2)}) %collective-permute-start.2) | collective-permute-done | bytes 69664 | tf_op jit(solution)/shard_map/ppermute | solution.py:307
  29.3 0.5 slice.17
  29.9 0.0 copy-done.6
  29.9 7.8 %col_pass.2 = f32[16,72,128]{2,1,0:T(8,128)S(1)} custom-call(s32[4,128]{1,0:T(4,128)S(1)} %bitcast.17, s32[128]{0:T(128)S(1)} %bitcast.21, bf16[128,128,128]{2,1,0:T(8,128)(2,1)S(1)} %get-tuple-element.63.refs_2_, bf16[64,131072]{1,0:T(8,128)(2,1)S(1)} %get-tuple-element.62.refs_3_, f32[128,128]{1,0:T(8,128)S(1)} %slice_subtract_fusion.refs_4_, ...), custom_call_target="tpu_custom_call" | custom-call | tf_op jit(solution)/shard_map/col_pass/pallas_call | solution.py:283
  37.7 0.0 copy-done
  37.7 0.0 copy-done.3
  37.7 0.0 copy-start.8
  37.7 0.0 copy-start.10
  37.7 17.4 %all_to_all.20 = f32[16,72,128]{2,1,0:T(8,128)S(1)} all-to-all(f32[16,72,128]{2,1,0:T(8,128)S(1)} %col_pass.2), channel_id=1, replica_groups=mesh['row'=16,'col'=8] {'row'}, dimensions={0} | all-to-all | bytes 1179648 | tf_op jit(solution)/shard_map/all_to_all | solution.py:313
  55.1 0.1 exponential_reduce_fusion
  55.3 0.5 slice.19
  55.9 13.3 %all_to_all.21 = f32[16,64,128]{2,1,0:T(8,128)S(1)} all-to-all(f32[16,64,128]{2,1,0:T(8,128)S(1)} %broadcast_in_dim.4), channel_id=1, replica_groups=mesh['row'=16,'col'=8] {'row'}, dimensions={0} | all-to-all | bytes 1048576 | tf_op jit(solution)/shard_map/all_to_all | solution.py:313
  69.1 0.0 copy-done.8
  69.1 0.0 copy-done.10
  69.1 0.0 copy-start.1
  69.1 5.8 %copy-done.1 = bf16[64,131072]{1,0:T(8,128)(2,1)S(1)} copy-done((bf16[64,131072]{1,0:T(8,128)(2,1)S(1)}, bf16[64,131072]{1,0:T(8,128)(2,1)}, u32[]{:S(2)}) %copy-start.1) | copy-done | bytes 16777240
  74.9 0.0 copy-start.4
  74.9 2.2 %copy-done.4 = bf16[128,128,128]{2,1,0:T(8,128)(2,1)S(1)} copy-done((bf16[128,128,128]{2,1,0:T(8,128)(2,1)S(1)}, bf16[128,128,128]{2,1,0:T(8,128)(2,1)}, u32[]{:S(2)}) %copy-start.4) | copy-done | bytes 4194328
  77.1 8.4 %row_pass.1 = f32[128,128]{1,0:T(8,128)S(1)} custom-call(s32[4,128]{1,0:T(4,128)S(1)} %bitcast.18, s32[128]{0:T(128)S(1)} %bitcast.22, bf16[128,128,128]{2,1,0:T(8,128)(2,1)S(1)} %copy-done.4, bf16[64,131072]{1,0:T(8,128)(2,1)S(1)} %copy-done.1, f32[128,128]{1,0:T(8,128)S(1)} %broadcast_multiply_fusion.refs_4_, f32[1024,128]{1,0:T(8,128)S(1)} %bitcast.12), custom_call_target="tpu_custom_call" | custom-call | tf_op jit(solution)/shard_map/row_pass/pallas_call | solution.py:268
  85.5 0.1 collective-permute-start.3
  85.6 1.2 collective-permute-done.3
  86.8 0.1 collective-permute-start.4
  86.9 4.3 %collective-permute-done.4 = f32[128,128]{1,0:T(8,128)S(1)} collective-permute-done((f32[128,128]{1,0:T(8,128)S(1)}, f32[128,128]{1,0:T(8,128)S(1)}, u32[]{:S(2)}, u32[]{:S(2)}) %collective-permute-start.4) | collective-permute-done | bytes 65568 | tf_op jit(solution)/shard_map/ppermute | solution.py:307
  91.2 3.2 %collective-permute-start.5 = (f32[128,128]{1,0:T(8,128)S(1)}, f32[128,128]{1,0:T(8,128)S(1)}, u32[]{:S(2)}, u32[]{:S(2)}) collective-permute-start(f32[128,128]{1,0:T(8,128)S(1)} %multiply_add_fusion.4), channel_id=1, source_target_pairs={{0,6},{1,7},{2,4},{3,5},{4,2},{5,3},{6,0},{7,1},{8,14},{9,15},{10,... | collective-permute-start | bytes 196616 | tf_op jit(solution)/shard_map/ppermute | solution.py:307
  96.4 0.4 collective-permute-done.5
  96.8 0.7 multiply_add_fusion.3
  97.5 0.0 copy-start.2
  97.5 5.8 %copy-done.2 = bf16[64,131072]{1,0:T(8,128)(2,1)S(1)} copy-done((bf16[64,131072]{1,0:T(8,128)(2,1)S(1)}, bf16[64,131072]{1,0:T(8,128)(2,1)}, u32[]{:S(2)}) %copy-start.2) | copy-done | bytes 16777240
  103.2 0.0 copy-start.5
  103.2 2.2 %copy-done.5 = bf16[128,128,128]{2,1,0:T(8,128)(2,1)S(1)} copy-done((bf16[128,128,128]{2,1,0:T(8,128)(2,1)S(1)}, bf16[128,128,128]{2,1,0:T(8,128)(2,1)}, u32[]{:S(2)}) %copy-start.5) | copy-done | bytes 4194328
  105.4 7.7 %col_pass.3 = f32[16,64,128]{2,1,0:T(8,128)S(1)} custom-call(s32[4,128]{1,0:T(4,128)S(1)} %bitcast.19, s32[128]{0:T(128)S(1)} %bitcast.23, bf16[128,128,128]{2,1,0:T(8,128)(2,1)S(1)} %copy-done.5, bf16[64,131072]{1,0:T(8,128)(2,1)S(1)} %copy-done.2, f32[128,128]{1,0:T(8,128)S(1)} %get-tuple-element.121.refs_4_, f32[1024,128]{1,0:T(8,128)S(1)} %bitcast.13), custom_call_target="tpu_custom_call" | custom-call | tf_op jit(solution)/shard_map/col_pass/pallas_call | solution.py:283
  113.1 13.1 %all_to_all.22 = f32[16,64,128]{2,1,0:T(8,128)S(1)} all-to-all(f32[16,64,128]{2,1,0:T(8,128)S(1)} %col_pass.3), channel_id=1, replica_groups=mesh['row'=16,'col'=8] {'row'}, dimensions={0} | all-to-all | bytes 1048576 | tf_op jit(solution)/shard_map/all_to_all | solution.py:313
  126.2 0.1 exponential_reduce_fusion.1
  126.4 13.1 %all_to_all.23 = f32[16,64,128]{2,1,0:T(8,128)S(1)} all-to-all(f32[16,64,128]{2,1,0:T(8,128)S(1)} %broadcast_in_dim.5), channel_id=1, replica_groups=mesh['row'=16,'col'=8] {'row'}, dimensions={0} | all-to-all | bytes 1048576 | tf_op jit(solution)/shard_map/all_to_all | solution.py:313
  139.5 0.8 copy.9
  (15 shorter events, 0.4 us)
Async XLA Ops:
  0.6 0.7 copy-start.7
  1.3 0.7 copy-start.9
  2.0 27.9 %copy-start.6 = (f32[16384]{0:T(1024)S(1)}, f32[16384]{0:T(1024)}, u32[]{:S(2)}) copy-start(f32[16384]{0:T(1024)} %param.8) | copy-start | bytes 196612
  16.9 20.7 %copy-start = (bf16[64,131072]{1,0:T(8,128)(2,1)}, bf16[64,131072]{1,0:T(8,128)(2,1)S(1)}, u32[]{:S(2)}) copy-start(bf16[64,131072]{1,0:T(8,128)(2,1)S(1)} %get-tuple-element.62.refs_3_) | copy-start | bytes 50331652
  16.9 20.7 %copy-start.3 = (bf16[128,128,128]{2,1,0:T(8,128)(2,1)}, bf16[128,128,128]{2,1,0:T(8,128)(2,1)S(1)}, u32[]{:S(2)}) copy-start(bf16[128,128,128]{2,1,0:T(8,128)(2,1)S(1)} %get-tuple-element.61.refs_2_) | copy-start | bytes 12582916
  17.0 1.3 collective-permute-start
  18.3 4.6 %collective-permute-start.1 = (f32[136,128]{1,0:T(8,128)S(1)}, f32[136,128]{1,0:T(8,128)S(1)}, u32[]{:S(2)}, u32[]{:S(2)}) collective-permute-start(f32[136,128]{1,0:T(8,128)S(1)} %multiply_add_fusion.2), channel_id=1, source_target_pairs={{0,2},{1,3},{2,0},{3,1},{4,6},{5,7},{6,4},{7,5},{8,10},{9,11},{10,... | collective-permute-start | bytes 208904 | tf_op jit(solution)/shard_map/ppermute | solution.py:307
  23.0 6.3 %collective-permute-start.2 = (f32[136,128]{1,0:T(8,128)S(1)}, f32[136,128]{1,0:T(8,128)S(1)}, u32[]{:S(2)}, u32[]{:S(2)}) collective-permute-start(f32[136,128]{1,0:T(8,128)S(1)} %multiply_add_fusion.1), channel_id=1, source_target_pairs={{0,6},{1,7},{2,4},{3,5},{4,2},{5,3},{6,0},{7,1},{8,14},{9,15},{10,... | collective-permute-start | bytes 208904 | tf_op jit(solution)/shard_map/ppermute | solution.py:307
  37.7 31.5 %copy-start.8 = (s32[128,1,4]{0,2,1:T(4,128)S(1)}, s32[128,1,4]{0,2,1:T(4,128)}, u32[]{:S(2)}) copy-start(s32[128,1,4]{0,2,1:T(4,128)} %param.10) | copy-start | bytes 6148
  37.7 31.5 %copy-start.10 = (s32[128,1]{0,1:T(1,128)S(1)}, s32[128,1]{0,1:T(1,128)}, u32[]{:S(2)}) copy-start(s32[128,1]{0,1:T(1,128)} %param.11) | copy-start | bytes 1540
  69.1 5.8 %copy-start.1 = (bf16[64,131072]{1,0:T(8,128)(2,1)S(1)}, bf16[64,131072]{1,0:T(8,128)(2,1)}, u32[]{:S(2)}) copy-start(bf16[64,131072]{1,0:T(8,128)(2,1)} %copy-done) | copy-start | bytes 50331652
  74.9 2.2 %copy-start.4 = (bf16[128,128,128]{2,1,0:T(8,128)(2,1)S(1)}, bf16[128,128,128]{2,1,0:T(8,128)(2,1)}, u32[]{:S(2)}) copy-start(bf16[128,128,128]{2,1,0:T(8,128)(2,1)} %copy-done.3) | copy-start | bytes 12582916
  85.5 1.3 collective-permute-start.3
  86.8 4.3 %collective-permute-start.4 = (f32[128,128]{1,0:T(8,128)S(1)}, f32[128,128]{1,0:T(8,128)S(1)}, u32[]{:S(2)}, u32[]{:S(2)}) collective-permute-start(f32[128,128]{1,0:T(8,128)S(1)} %multiply_add_fusion.5), channel_id=1, source_target_pairs={{0,2},{1,3},{2,0},{3,1},{4,6},{5,7},{6,4},{7,5},{8,10},{9,11},{10,... | collective-permute-start | bytes 196616 | tf_op jit(solution)/shard_map/ppermute | solution.py:307
  91.2 5.6 %collective-permute-start.5 = (f32[128,128]{1,0:T(8,128)S(1)}, f32[128,128]{1,0:T(8,128)S(1)}, u32[]{:S(2)}, u32[]{:S(2)}) collective-permute-start(f32[128,128]{1,0:T(8,128)S(1)} %multiply_add_fusion.4), channel_id=1, source_target_pairs={{0,6},{1,7},{2,4},{3,5},{4,2},{5,3},{6,0},{7,1},{8,14},{9,15},{10,... | collective-permute-start | bytes 196616 | tf_op jit(solution)/shard_map/ppermute | solution.py:307
  97.5 5.8 %copy-start.2 = (bf16[64,131072]{1,0:T(8,128)(2,1)S(1)}, bf16[64,131072]{1,0:T(8,128)(2,1)}, u32[]{:S(2)}) copy-start(bf16[64,131072]{1,0:T(8,128)(2,1)} %copy-done) | copy-start | bytes 50331652
  103.2 2.2 %copy-start.5 = (bf16[128,128,128]{2,1,0:T(8,128)(2,1)S(1)}, bf16[128,128,128]{2,1,0:T(8,128)(2,1)}, u32[]{:S(2)}) copy-start(bf16[128,128,128]{2,1,0:T(8,128)(2,1)} %copy-done.3) | copy-start | bytes 12582916

commit v4 on v3

--- a/solution.py
+++ b/solution.py
@@ -109,13 +109,17 @@
 
 def row_pass_kernel(kappa, slots, *refs):
     if kappa is not None:
-        (cols, counts, first_own, a_hbm, b_hbm, x_hbm, y_hbm, out_ref, x_ref, x2_ref, y_ref,
-         g_ref, hx_ref, a_ref, b_ref, own_ref, total, x_in, b_in, sems, y_sem) = refs
+        (first_own, cols_hbm, counts_hbm, a_hbm, b_hbm, x_hbm, y_hbm, out_ref, x_ref, x2_ref,
+         y_ref, g_ref, hx_ref, a_ref, b_ref, own_ref, total, x_in, b_in, cols, counts, sems,
+         y_sem) = refs
         f_ref = None
-        a_copy = pltpu.make_async_copy(a_hbm, a_ref, sems.at[1])
-        b_copy = pltpu.make_async_copy(b_hbm, b_in, sems.at[2])
+        small = ((a_hbm, a_ref), (b_hbm, b_in), (cols_hbm, cols), (counts_hbm, counts))
+        others = [
+            pltpu.make_async_copy(source, target, sems.at[1 + i])
+            for i, (source, target) in enumerate(small)
+        ]
         prepare(kappa, x_hbm, y_hbm, x_ref, x2_ref, y_ref, g_ref, hx_ref, x_in, sems.at[0],
-                y_sem, (a_copy, b_copy))
+                y_sem, others)
         own = pl.ds(pl.multiple_of(first_own[0], own_ref.shape[0]), own_ref.shape[0])
         own_ref[...] = g_ref[own, :]
         b_ref[...] = jnp.log2(b_in[own, :])
@@ -235,7 +239,7 @@
     bf16, f32 = jnp.bfloat16, jnp.float32
     in_hbm = [
         pltpu.with_memory_space_constraint(v, pltpu.HBM)
-        for v in (source_mass, target_mass, source_points, target_points)
+        for v in (cols, counts, source_mass, target_mass, source_points, target_points)
     ]
     return pl.pallas_call(
         functools.partial(row_pass_kernel, LOG2E / first_epsilon, slots),
@@ -250,18 +254,20 @@
             shape((target_blocks // devices, TILE), f32),
             shape((target_blocks // devices, TILE), f32),
         ),
-        in_specs=[SMEM(), SMEM(), SMEM(), ANY(), ANY(), ANY(), ANY()],
+        in_specs=[SMEM()] + [ANY()] * 6,
         out_specs=(VMEM(),) * 9,
         scratch_shapes=[
             pltpu.VMEM((TILE, blocks), f32),
             pltpu.VMEM(source_points.shape, bf16),
             pltpu.VMEM((target_blocks, TILE), f32),
-            pltpu.SemaphoreType.DMA((3,)),
+            pltpu.SMEM(cols.shape, jnp.int32),
+            pltpu.SMEM(counts.shape, jnp.int32),
+            pltpu.SemaphoreType.DMA((5,)),
             pltpu.SemaphoreType.DMA((target_blocks // CHUNK,)),
         ],
         name="row_pass_first",
         compiler_params=pltpu.CompilerParams(vmem_limit_bytes=VMEM_LIMIT),
-    )(cols, counts, own, *in_hbm)
+    )(own, *in_hbm)
 
 
 def row_pass(cols, counts, x, y, f_pot, g_pot, slots):
@@ -291,9 +297,51 @@
     )(cols, counts, x, y, f_pot, g_pot, *extra)
 
 
-def lse(stack):
-    top = jnp.max(stack, axis=0)
-    return top + jnp.log2(jnp.sum(jnp.exp2(stack - top[None]), axis=0))
+def combine_kernel(epsilon, both_eps, *refs):
+    if both_eps is None:
+        stack_ref, mass_ref, g_ref, send_ref, new_ref, total_ref = refs
+    else:
+        stack_ref, mass_ref, g_ref, first_ref, a_ref, b_ref, send_ref = refs
+    devices = stack_ref.shape[0]
+    own = mass_ref.shape[0]
+    top = stack_ref[0]
+    for d in range(1, devices):
+        top = jnp.maximum(top, stack_ref[d])
+    summed = jnp.exp2(stack_ref[0] - top)
+    for d in range(1, devices):
+        summed += jnp.exp2(stack_ref[d] - top)
+    whole = top + jnp.log2(summed)
+    new = g_ref[...] + (mass_ref[...] - whole[:own])
+    if both_eps is None:
+        new = 2.0 * new
+        new_ref[...] = new
+        total_ref[...] = whole[own:]
+    else:
+        totals = a_ref[:1, :] - b_ref[:1, :]
+        half = first_ref[...] * first_epsilon
+        new = LN2 * (epsilon * new + both_eps * totals - half)
+    for d in range(devices):
+        send_ref[d] = new
+
+
+def combine(stack, log_b, g_own, last):
+    shape = jax.ShapeDtypeStruct
+    own = log_b.shape[0]
+    send = shape((stack.shape[0], own, TILE), jnp.float32)
+    if last is None:
+        more, scales = (), (None, None)
+        out = (send, shape(log_b.shape, jnp.float32), shape((8, TILE), jnp.float32))
+    else:
+        more, scales = last[:3], last[3:]
+        out = send
+    return pl.pallas_call(
+        functools.partial(combine_kernel, *scales),
+        out_shape=out,
+        in_specs=[VMEM()] * (3 + len(more)),
+        out_specs=jax.tree.map(lambda _: VMEM(), out),
+        name="combine",
+        compiler_params=pltpu.CompilerParams(vmem_limit_bytes=VMEM_LIMIT // 2),
+    )(stack, log_b, g_own, *more)
 
 
 def lse_two(one, two):
@@ -340,14 +388,14 @@
     )
     x1, x2, y = (pltpu.with_memory_space_constraint(v, pltpu.VMEM) for v in (x1, x2, y))
 
-    half_own = g_own * (-LN2 * first_epsilon)
-    f_pot = total_a = total_b = None
+    g_first = g_own
+    f_pot = total_a = total_b = source = None
     for step in range(ITERS):
         epsilon = first_epsilon * 0.5**step
         x = x1 if step == 0 else x2
         if step == 0:
             both = over_cols(part, col_devices)
-            part, total_b = both[:row_blocks], both[row_blocks, 0]
+            part, total_b = both[:row_blocks], both[row_blocks:]
             f_pot = log_a - part
         else:
             part = over_cols(row_pass(cols, counts, x, y, f_pot, g_pot, slots), col_devices)
@@ -356,36 +404,25 @@
         part = col_pass(
             cols, counts, x, y, f_pot, g_pot, mass_a if step == 0 else None, slots, row_devices
         )
-        if step == ITERS - 1:
+        if step < ITERS - 1:
+            f_pot = 2.0 * f_pot
+            stack, rest = exchange(part, (f_pot, total_b))
+            f_pot, total_b = rest
+            send, g_own, total_a = combine(stack, log_b, g_own, None)
+            g_pot, rest = exchange(send, (f_pot, total_b))
+            f_pot, total_b = rest
+        else:
             earlier = first_epsilon * (2.0 - 0.5**step) - epsilon
-            source = half_x + LN2 * (
-                epsilon * f_pot - epsilon * total_a - earlier * (total_a - total_b)
+            totals = epsilon * total_a[:1] + earlier * (total_a[:1] - total_b[:1])
+            source = half_x + LN2 * (epsilon * f_pot - totals)
+            stack, source = exchange(part, source)
+            both_eps = first_epsilon * (2.0 - 0.5**step)
+            send = combine(
+                stack, log_b, g_own, (g_first, total_a, total_b, epsilon, both_eps)
             )
-            rest = (source, log_b, g_own, half_own, total_a - total_b)
-        else:
-            rest = (f_pot, half_x, log_a, log_b, g_own, half_own, total_b)
-        stack, rest = exchange(part, rest)
-        part = lse(stack)
-        if step == 0:
-            f_pot, half_x, log_a, log_b, g_own, half_own, total_b = rest
-            part, total_a = part[:own_blocks], part[own_blocks, 0]
-        else:
-            source, log_b, g_own, half_own, totals = rest
-        g_own = g_own + (log_b - part)
-        if step < ITERS - 1:
-            g_own, f_pot = 2.0 * g_own, 2.0 * f_pot
-            send = g_own
-            rest = (f_pot, half_x, log_a, log_b, g_own, half_own, total_a, total_b)
-        else:
-            both_eps = first_epsilon * (2.0 - 0.5**step)
-            send = LN2 * (epsilon * g_own + both_eps * totals) + half_own
-            rest = (source,)
-        send = jnp.broadcast_to(send[None], (row_devices, own_blocks, TILE))
-        g_pot, rest = exchange(send, rest)
+            g_pot, source = exchange(send, source)
         g_pot = g_pot.reshape(target_blocks, TILE)
-        if step < ITERS - 1:
-            f_pot, half_x, log_a, log_b, g_own, half_own, total_a, total_b = rest
-    return (rest[0].reshape(rows), g_pot.reshape(target_cells))
+    return (source.reshape(rows), g_pot.reshape(target_cells))
 
 
 def solution(mesh):

time: 141 us -> 122 us (0.87)
  local copies, waits for them, and re-layouts: 19.2 us -> 0.84 us
  waiting for transfers between devices: 11.9 us -> 13.9 us
  between operations: 2.77 us -> 0.79 us
    unnamed x23 -> x7, local copies, waits for them, and re-layouts: 18.1 us -> 0.84 us
    ppermute x6, waiting for transfers between devices: 11.9 us -> 13.9 us  [over_cols(): part = lse_two(part, lax.ppermute(part, 'col', pairs))]
where the time goes in v4:
time: 122 us; the launch traced here: 121 us
  blocking collectives  57 us (47%)
  Pallas kernels  38.6 us (32%)
  waiting for transfers between devices  13.9 us (11%)
  starting transfers between devices  9.5 us (8%)
    all_to_all x4, blocking collectives, exchange(): return lax.optimization_barrier((lax.all_to_all(blocks, 'row', 0, 0), rest))  57 us
    pallas_call x2, Pallas kernels, col_pass(): pl.pallas_call(functools.partial(col_pass_kernel, slots, mass is not None...  15.5 us
    pallas_call x1, Pallas kernels, first_row_pass(): pl.pallas_call(functools.partial(row_pass_kernel, LOG2E / first_epsilon,...  14.5 us
    ppermute x6, waiting for transfers between devices, over_cols(): part = lse_two(part, lax.ppermute(part, 'col', pairs))  13.9 us
    ppermute x6, starting transfers between devices, over_cols(): part = lse_two(part, lax.ppermute(part, 'col', pairs))  9.5 us
    pallas_call x1, Pallas kernels, row_pass(): pl.pallas_call(functools.partial(row_pass_kernel, None, slots), out_shape...  8.31 us
  transfers between devices with their start and end apart: 6, of which 6 were waited for; matrix products, arithmetic and copies ran while one was open for 0% of the time, Pallas kernels for 0%

profile of v4, /device:TPU:0, one launch (start us, length us, event | category | flops | bytes accessed | tf_op | source)
XLA Modules:
  0.0 121.5 jit_solution(3302120850422486745)
XLA Ops:
  0.6 0.0 copy-start
  0.6 0.0 copy-start.1
  0.7 0.0 copy-start.2
  0.7 14.5 %row_pass_first.1 = (f32[136,128]{1,0:T(8,128)S(1)}, bf16[128,128,128]{2,1,0:T(8,128)(2,1)S(1)}, bf16[128,128,128]{2,1,0:T(8,128)(2,1)S(1)}, bf16[64,131072]{1,0...) custom-call(s32[1]{0:T(128)} %bitcast.3.refs_0_, ...), custom_call_target="tpu_custom_call" | custom-call | tf_op jit(solution)/shard_map/row_pass_first/pallas_call | solution.py:244
  15.2 0.1 collective-permute-start
  15.3 1.2 %collective-permute-done = f32[136,128]{1,0:T(8,128)S(1)} collective-permute-done((f32[136,128]{1,0:T(8,128)S(1)}, f32[136,128]{1,0:T(8,128)S(1)}, u32[]{:S(2)}, u32[]{:S(2)}) %collective-permute-start) | collective-permute-done | bytes 69664 | tf_op jit(solution)/shard_map/ppermute | solution.py:355
  16.6 2.1 %collective-permute-start.1 = (f32[136,128]{1,0:T(8,128)S(1)}, f32[136,128]{1,0:T(8,128)S(1)}, u32[]{:S(2)}, u32[]{:S(2)}) collective-permute-start(f32[136,128]{1,0:T(8,128)S(1)} %multiply_add_fusion.2), channel_id=1, source_target_pairs={{0,2},{1,3},{2,0},{3,1},{4,6},{5,7},{6,4},{7,5},{8,10},{9,11},{10,... | collective-permute-start | bytes 208904 | tf_op jit(solution)/shard_map/ppermute | solution.py:355
  18.7 2.5 %collective-permute-done.1 = f32[136,128]{1,0:T(8,128)S(1)} collective-permute-done((f32[136,128]{1,0:T(8,128)S(1)}, f32[136,128]{1,0:T(8,128)S(1)}, u32[]{:S(2)}, u32[]{:S(2)}) %collective-permute-start.1) | collective-permute-done | bytes 69664 | tf_op jit(solution)/shard_map/ppermute | solution.py:355
  21.2 4.0 %collective-permute-start.2 = (f32[136,128]{1,0:T(8,128)S(1)}, f32[136,128]{1,0:T(8,128)S(1)}, u32[]{:S(2)}, u32[]{:S(2)}) collective-permute-start(f32[136,128]{1,0:T(8,128)S(1)} %multiply_add_fusion.1), channel_id=1, source_target_pairs={{0,6},{1,7},{2,4},{3,5},{4,2},{5,3},{6,0},{7,1},{8,14},{9,15},{10,... | collective-permute-start | bytes 208904 | tf_op jit(solution)/shard_map/ppermute | solution.py:355
  25.2 2.3 %collective-permute-done.2 = f32[136,128]{1,0:T(8,128)S(1)} collective-permute-done((f32[136,128]{1,0:T(8,128)S(1)}, f32[136,128]{1,0:T(8,128)S(1)}, u32[]{:S(2)}, u32[]{:S(2)}) %collective-permute-start.2) | collective-permute-done | bytes 69664 | tf_op jit(solution)/shard_map/ppermute | solution.py:355
  27.6 0.0 copy-done
  27.6 0.0 copy-done.1
  27.6 0.0 copy-done.2
  27.6 7.8 %col_pass.2 = f32[16,72,128]{2,1,0:T(8,128)S(1)} custom-call(s32[4,128]{1,0:T(4,128)S(1)} %bitcast.17, s32[128]{0:T(128)S(1)} %bitcast.21, bf16[128,128,128]{2,1,0:T(8,128)(2,1)S(1)} %get-tuple-element.36.refs_2_, bf16[64,131072]{1,0:T(8,128)(2,1)S(1)} %get-tuple-element.35.refs_3_, f32[128,128]{1,0:T(8,128)S(1)} %get-tuple-element.69.refs_4_, ...), custom_call_target="tpu_custom_call" | custom-call | tf_op jit(solution)/shard_map/col_pass/pallas_call | solution.py:289
  35.4 17.4 %all_to_all.20.refs_0_ = f32[16,72,128]{2,1,0:T(8,128)S(1)} all-to-all(f32[16,72,128]{2,1,0:T(8,128)S(1)} %col_pass.2), channel_id=1, replica_groups=mesh['row'=16,'col'=8] {'row'}, dimensions={0} | all-to-all | bytes 1179648 | tf_op jit(solution)/shard_map/all_to_all | solution.py:361
  52.8 0.1 combine.2
  52.9 13.3 %all_to_all.21 = f32[16,64,128]{2,1,0:T(8,128)S(1)} all-to-all(f32[16,64,128]{2,1,0:T(8,128)S(1)} %get-tuple-element.49), channel_id=1, replica_groups=mesh['row'=16,'col'=8] {'row'}, dimensions={0} | all-to-all | bytes 1048576 | tf_op jit(solution)/shard_map/all_to_all | solution.py:361
  66.2 8.3 %row_pass.1 = f32[128,128]{1,0:T(8,128)S(1)} custom-call(s32[4,128]{1,0:T(4,128)S(1)} %bitcast.18, s32[128]{0:T(128)S(1)} %bitcast.22, bf16[128,128,128]{2,1,0:T(8,128)(2,1)S(1)} %get-tuple-element.34.refs_2_, bf16[64,131072]{1,0:T(8,128)(2,1)S(1)} %get-tuple-element.35.refs_3_, f32[128,128]{1,0:T(8,128)S(1)} %get-tuple-element.52.refs_4_, ...), custom_call_target="tpu_custom_call" | custom-call | tf_op jit(solution)/shard_map/row_pass/pallas_call | solution.py:274
  74.5 0.1 collective-permute-start.3
  74.6 1.2 %collective-permute-done.3 = f32[128,128]{1,0:T(8,128)S(1)} collective-permute-done((f32[128,128]{1,0:T(8,128)S(1)}, f32[128,128]{1,0:T(8,128)S(1)}, u32[]{:S(2)}, u32[]{:S(2)}) %collective-permute-start.3) | collective-permute-done | bytes 65568 | tf_op jit(solution)/shard_map/ppermute | solution.py:355
  75.9 0.1 collective-permute-start.4
  76.0 4.3 %collective-permute-done.4 = f32[128,128]{1,0:T(8,128)S(1)} collective-permute-done((f32[128,128]{1,0:T(8,128)S(1)}, f32[128,128]{1,0:T(8,128)S(1)}, u32[]{:S(2)}, u32[]{:S(2)}) %collective-permute-start.4) | collective-permute-done | bytes 65568 | tf_op jit(solution)/shard_map/ppermute | solution.py:355
  80.3 3.2 %collective-permute-start.5 = (f32[128,128]{1,0:T(8,128)S(1)}, f32[128,128]{1,0:T(8,128)S(1)}, u32[]{:S(2)}, u32[]{:S(2)}) collective-permute-start(f32[128,128]{1,0:T(8,128)S(1)} %multiply_add_fusion.4), channel_id=1, source_target_pairs={{0,6},{1,7},{2,4},{3,5},{4,2},{5,3},{6,0},{7,1},{8,14},{9,15},{10,... | collective-permute-start | bytes 196616 | tf_op jit(solution)/shard_map/ppermute | solution.py:355
  83.5 2.4 %collective-permute-done.5 = f32[128,128]{1,0:T(8,128)S(1)} collective-permute-done((f32[128,128]{1,0:T(8,128)S(1)}, f32[128,128]{1,0:T(8,128)S(1)}, u32[]{:S(2)}, u32[]{:S(2)}) %collective-permute-start.5) | collective-permute-done | bytes 65568 | tf_op jit(solution)/shard_map/ppermute | solution.py:355
  85.8 0.7 multiply_add_fusion.3
  86.5 7.7 %col_pass.3 = f32[16,64,128]{2,1,0:T(8,128)S(1)} custom-call(s32[4,128]{1,0:T(4,128)S(1)} %bitcast.19, s32[128]{0:T(128)S(1)} %bitcast.23, bf16[128,128,128]{2,1,0:T(8,128)(2,1)S(1)} %get-tuple-element.34.refs_2_, bf16[64,131072]{1,0:T(8,128)(2,1)S(1)} %get-tuple-element.35.refs_3_, f32[128,128]{1,0:T(8,128)S(1)} %get-tuple-element.67.refs_4_, ...), custom_call_target="tpu_custom_call" | custom-call | tf_op jit(solution)/shard_map/col_pass/pallas_call | solution.py:289
  94.2 13.2 %all_to_all.22.refs_0_ = f32[16,64,128]{2,1,0:T(8,128)S(1)} all-to-all(f32[16,64,128]{2,1,0:T(8,128)S(1)} %col_pass.3), channel_id=1, replica_groups=mesh['row'=16,'col'=8] {'row'}, dimensions={0} | all-to-all | bytes 1048576 | tf_op jit(solution)/shard_map/all_to_all | solution.py:361
  107.4 0.1 combine.3
  107.5 13.1 %all_to_all.23 = f32[16,64,128]{2,1,0:T(8,128)S(1)} all-to-all(f32[16,64,128]{2,1,0:T(8,128)S(1)} %combine.3), channel_id=1, replica_groups=mesh['row'=16,'col'=8] {'row'}, dimensions={0} | all-to-all | bytes 1048576 | tf_op jit(solution)/shard_map/all_to_all | solution.py:361
  120.7 0.8 copy.9
  (8 shorter events, 0.2 us)
Async XLA Ops:
  0.6 26.9 %copy-start = (f32[16384]{0:T(1024)S(1)}, f32[16384]{0:T(1024)}, u32[]{:S(2)}) copy-start(f32[16384]{0:T(1024)} %param.8) | copy-start | bytes 196612
  0.6 26.9 %copy-start.1 = (s32[128,1,4]{0,2,1:T(4,128)S(1)}, s32[128,1,4]{0,2,1:T(4,128)}, u32[]{:S(2)}) copy-start(s32[128,1,4]{0,2,1:T(4,128)} %param.10) | copy-start | bytes 6148
  0.7 26.9 %copy-start.2 = (s32[128,1]{0,1:T(1,128)S(1)}, s32[128,1]{0,1:T(1,128)}, u32[]{:S(2)}) copy-start(s32[128,1]{0,1:T(1,128)} %param.11) | copy-start | bytes 1540
  15.2 1.3 %collective-permute-start = (f32[136,128]{1,0:T(8,128)S(1)}, f32[136,128]{1,0:T(8,128)S(1)}, u32[]{:S(2)}, u32[]{:S(2)}) collective-permute-start(f32[136,128]{1,0:T(8,128)S(1)} %get-tuple-element.38), channel_id=1, source_target_pairs={{0,1},{1,0},{2,3},{3,2},{4,5},{5,4},{6,7},{7,6},{8,9},{9,8},{10,11... | collective-permute-start | bytes 208904 | tf_op jit(solution)/shard_map/ppermute | solution.py:355
  16.6 4.6 %collective-permute-start.1 = (f32[136,128]{1,0:T(8,128)S(1)}, f32[136,128]{1,0:T(8,128)S(1)}, u32[]{:S(2)}, u32[]{:S(2)}) collective-permute-start(f32[136,128]{1,0:T(8,128)S(1)} %multiply_add_fusion.2), channel_id=1, source_target_pairs={{0,2},{1,3},{2,0},{3,1},{4,6},{5,7},{6,4},{7,5},{8,10},{9,11},{10,... | collective-permute-start | bytes 208904 | tf_op jit(solution)/shard_map/ppermute | solution.py:355
  21.2 6.3 %collective-permute-start.2 = (f32[136,128]{1,0:T(8,128)S(1)}, f32[136,128]{1,0:T(8,128)S(1)}, u32[]{:S(2)}, u32[]{:S(2)}) collective-permute-start(f32[136,128]{1,0:T(8,128)S(1)} %multiply_add_fusion.1), channel_id=1, source_target_pairs={{0,6},{1,7},{2,4},{3,5},{4,2},{5,3},{6,0},{7,1},{8,14},{9,15},{10,... | collective-permute-start | bytes 208904 | tf_op jit(solution)/shard_map/ppermute | solution.py:355
  74.5 1.3 %collective-permute-start.3 = (f32[128,128]{1,0:T(8,128)S(1)}, f32[128,128]{1,0:T(8,128)S(1)}, u32[]{:S(2)}, u32[]{:S(2)}) collective-permute-start(f32[128,128]{1,0:T(8,128)S(1)} %row_pass.1), channel_id=1, source_target_pairs={{0,1},{1,0},{2,3},{3,2},{4,5},{5,4},{6,7},{7,6},{8,9},{9,8},{10,11... | collective-permute-start | bytes 196616 | tf_op jit(solution)/shard_map/ppermute | solution.py:355
  75.9 4.3 %collective-permute-start.4 = (f32[128,128]{1,0:T(8,128)S(1)}, f32[128,128]{1,0:T(8,128)S(1)}, u32[]{:S(2)}, u32[]{:S(2)}) collective-permute-start(f32[128,128]{1,0:T(8,128)S(1)} %multiply_add_fusion.5), channel_id=1, source_target_pairs={{0,2},{1,3},{2,0},{3,1},{4,6},{5,7},{6,4},{7,5},{8,10},{9,11},{10,... | collective-permute-start | bytes 196616 | tf_op jit(solution)/shard_map/ppermute | solution.py:355
  80.3 5.6 %collective-permute-start.5 = (f32[128,128]{1,0:T(8,128)S(1)}, f32[128,128]{1,0:T(8,128)S(1)}, u32[]{:S(2)}, u32[]{:S(2)}) collective-permute-start(f32[128,128]{1,0:T(8,128)S(1)} %multiply_add_fusion.4), channel_id=1, source_target_pairs={{0,6},{1,7},{2,4},{3,5},{4,2},{5,3},{6,0},{7,1},{8,14},{9,15},{10,... | collective-permute-start | bytes 196616 | tf_op jit(solution)/shard_map/ppermute | solution.py:355

commit v5 on v4

--- a/solution.py
+++ b/solution.py
@@ -1,5 +1,4 @@
 import functools
-import math
 
 import jax
 import jax.numpy as jnp
@@ -8,7 +7,6 @@
 from jax.experimental.pallas import tpu as pltpu
 from jax.sharding import PartitionSpec as P
 
-ITERS = 2
 TILE = 128
 very_negative = -1e30
 first_epsilon = 0.5
@@ -58,6 +56,11 @@
     ]
 
 
+def log2_sum(values):
+    summed = jnp.sum(jnp.sum(values, axis=0, keepdims=True), axis=1, keepdims=True)
+    return jnp.broadcast_to(jnp.log2(summed), (8, TILE))
+
+
 def prepare(kappa, x_hbm, y_hbm, x_ref, x2_ref, y_ref, g_ref, hx_ref, x_in, x_sem, y_sem, others):
     width = y_ref.shape[0]
     blocks = hx_ref.shape[0]
@@ -109,23 +112,20 @@
 
 def row_pass_kernel(kappa, slots, *refs):
     if kappa is not None:
-        (first_own, cols_hbm, counts_hbm, a_hbm, b_hbm, x_hbm, y_hbm, out_ref, x_ref, x2_ref,
-         y_ref, g_ref, hx_ref, a_ref, b_ref, own_ref, total, x_in, b_in, cols, counts, sems,
-         y_sem) = refs
+        (cols_hbm, counts_hbm, a_hbm, b_hbm, x_hbm, y_hbm, out_ref, x_ref, x2_ref,
+         y_ref, g_ref, hx_ref, a_ref, b_ref, mass_ref, total, x_in, cols, counts, sems, y_sem) = refs
         f_ref = None
-        small = ((a_hbm, a_ref), (b_hbm, b_in), (cols_hbm, cols), (counts_hbm, counts))
+        small = ((a_hbm, a_ref), (b_hbm, b_ref), (cols_hbm, cols), (counts_hbm, counts))
         others = [
             pltpu.make_async_copy(source, target, sems.at[1 + i])
             for i, (source, target) in enumerate(small)
         ]
         prepare(kappa, x_hbm, y_hbm, x_ref, x2_ref, y_ref, g_ref, hx_ref, x_in, sems.at[0],
                 y_sem, others)
-        own = pl.ds(pl.multiple_of(first_own[0], own_ref.shape[0]), own_ref.shape[0])
-        own_ref[...] = g_ref[own, :]
-        b_ref[...] = jnp.log2(b_in[own, :])
         offset = 0.0
     else:
-        cols, counts, x_ref, y_ref, f_ref, g_ref, out_ref, total = refs
+        (cols, counts, x_ref, y_ref, f_ref, g_ref, g_first_ref, b_ref, mass_ref, out_ref,
+         total) = refs
         offset = ROW_OFFSET
     blocks = total.shape[1]
     lane = lax.broadcasted_iota(jnp.int32, (TILE, TILE), 1)
@@ -143,9 +143,13 @@
     sums = total[...]
     out_ref[:blocks, :] = (jnp.log2(sums) - offset).T
     if kappa is not None:
-        mass = jnp.sum(jnp.sum(b_in[...], axis=0, keepdims=True), axis=1, keepdims=True)
-        out_ref[blocks:, :] = jnp.broadcast_to(jnp.log2(mass), (8, TILE))
+        mass_ref[...] = log2_sum(b_ref[...])
         a_ref[...] = jnp.log2(a_ref[...])
+        b_ref[...] = jnp.log2(b_ref[...])
+    else:
+        out_ref[blocks : blocks + 8, :] = mass_ref[...]
+        last = g_first_ref[...] + b_ref[...] - 0.5 * g_ref[...]
+        out_ref[blocks + 8 :, :] = log2_sum(jnp.exp2(last))
     fine = jnp.logical_and(jnp.min(sums) >= SMALLEST, jnp.max(sums) <= LARGEST)
 
     @pl.when(jnp.logical_not(fine))
@@ -164,14 +168,9 @@
         out_ref[:blocks, :] = (total[...] - offset).T
 
 
-def col_pass_kernel(slots, with_mass, *refs):
-    if with_mass:
-        cols, counts, x_ref, y_ref, f_ref, g_ref, mass_ref, out_ref, total = refs
-    else:
-        cols, counts, x_ref, y_ref, f_ref, g_ref, out_ref, total = refs
+def col_pass_kernel(slots, *refs):
+    cols, counts, x_ref, y_ref, f_ref, g_ref, out_ref, total = refs
     blocks = f_ref.shape[0]
-    devices, height, _ = out_ref.shape
-    own = total.shape[0] // devices
     total[...] = jnp.zeros_like(total)
 
     def visit(r, carry):
@@ -216,13 +215,7 @@
                     peak = jnp.maximum(old, mine)
                     total[at, :] = peak + jnp.log2(jnp.exp2(old - peak) + jnp.exp2(mine - peak))
 
-    out_ref[:, :own, :] = total[...].reshape(devices, own, TILE)
-    if with_mass:
-        mass = mass_ref[...]
-        mass = jnp.sum(jnp.sum(mass, axis=0, keepdims=True), axis=1, keepdims=True)
-        out_ref[:, own:, :] = jnp.broadcast_to(
-            jnp.log2(mass)[None], (devices, height - own, TILE)
-        )
+    out_ref[...] = total[...].reshape(out_ref.shape)
 
 
 SMEM = functools.partial(pl.BlockSpec, memory_space=pltpu.SMEM)
@@ -230,11 +223,10 @@
 ANY = functools.partial(pl.BlockSpec, memory_space=pl.ANY)
 
 
-def first_row_pass(cols, counts, own, source_mass, target_mass, source_points, target_points, slots):
+def first_row_pass(cols, counts, source_mass, target_mass, source_points, target_points, slots):
     width, rows = source_points.shape
     blocks = rows // TILE
     target_blocks = target_points.shape[1] // TILE
-    devices = lax.axis_size("row")
     shape = jax.ShapeDtypeStruct
     bf16, f32 = jnp.bfloat16, jnp.float32
     in_hbm = [
@@ -244,22 +236,21 @@
     return pl.pallas_call(
         functools.partial(row_pass_kernel, LOG2E / first_epsilon, slots),
         out_shape=(
-            shape((blocks + 8, TILE), f32),
+            shape((blocks, TILE), f32),
             pltpu.VMEM((blocks, TILE, 2 * width), bf16),
             pltpu.VMEM((blocks, TILE, 2 * width), bf16),
             pltpu.VMEM(target_points.shape, bf16),
             shape((target_blocks, TILE), f32),
             shape((blocks, TILE), f32),
             shape((blocks, TILE), f32),
-            shape((target_blocks // devices, TILE), f32),
-            shape((target_blocks // devices, TILE), f32),
+            shape((target_blocks, TILE), f32),
+            shape((8, TILE), f32),
         ),
-        in_specs=[SMEM()] + [ANY()] * 6,
+        in_specs=[ANY()] * 6,
         out_specs=(VMEM(),) * 9,
         scratch_shapes=[
             pltpu.VMEM((TILE, blocks), f32),
             pltpu.VMEM(source_points.shape, bf16),
-            pltpu.VMEM((target_blocks, TILE), f32),
             pltpu.SMEM(cols.shape, jnp.int32),
             pltpu.SMEM(counts.shape, jnp.int32),
             pltpu.SemaphoreType.DMA((5,)),
@@ -267,93 +258,92 @@
         ],
         name="row_pass_first",
         compiler_params=pltpu.CompilerParams(vmem_limit_bytes=VMEM_LIMIT),
-    )(own, *in_hbm)
-
-
-def row_pass(cols, counts, x, y, f_pot, g_pot, slots):
+    )(*in_hbm)
+
+
+def row_pass(cols, counts, x, y, f_pot, g_pot, g_first, log_b, mass, slots):
     return pl.pallas_call(
         functools.partial(row_pass_kernel, None, slots),
-        out_shape=jax.ShapeDtypeStruct(f_pot.shape, jnp.float32),
-        in_specs=[SMEM(), SMEM(), VMEM(), VMEM(), VMEM(), VMEM()],
+        out_shape=jax.ShapeDtypeStruct((f_pot.shape[0] + 16, TILE), jnp.float32),
+        in_specs=[SMEM(), SMEM()] + [VMEM()] * 7,
         out_specs=VMEM(),
         scratch_shapes=[pltpu.VMEM((TILE, f_pot.shape[0]), jnp.float32)],
         name="row_pass",
         compiler_params=pltpu.CompilerParams(vmem_limit_bytes=VMEM_LIMIT),
-    )(cols, counts, x, y, f_pot, g_pot)
-
-
-def col_pass(cols, counts, x, y, f_pot, g_pot, mass, slots, devices):
+    )(cols, counts, x, y, f_pot, g_pot, g_first, log_b, mass)
+
+
+def col_pass(cols, counts, x, y, f_pot, g_pot, slots, devices):
     target_blocks = g_pot.shape[0]
-    height = target_blocks // devices + (8 if mass is not None else 0)
-    extra = () if mass is None else (mass,)
     return pl.pallas_call(
-        functools.partial(col_pass_kernel, slots, mass is not None),
-        out_shape=jax.ShapeDtypeStruct((devices, height, TILE), jnp.float32),
-        in_specs=[SMEM(), SMEM()] + [VMEM()] * (4 + len(extra)),
+        functools.partial(col_pass_kernel, slots),
+        out_shape=jax.ShapeDtypeStruct(
+            (devices, target_blocks // devices, TILE), jnp.float32
+        ),
+        in_specs=[SMEM(), SMEM()] + [VMEM()] * 4,
         out_specs=VMEM(),
         scratch_shapes=[pltpu.VMEM((target_blocks, TILE), jnp.float32)],
         name="col_pass",
         compiler_params=pltpu.CompilerParams(vmem_limit_bytes=VMEM_LIMIT),
-    )(cols, counts, x, y, f_pot, g_pot, *extra)
+    )(cols, counts, x, y, f_pot, g_pot)
 
 
 def combine_kernel(epsilon, both_eps, *refs):
     if both_eps is None:
-        stack_ref, mass_ref, g_ref, send_ref, new_ref, total_ref = refs
+        first_own, stack_ref, b_ref, g_ref, send_ref, new_ref = refs
     else:
-        stack_ref, mass_ref, g_ref, first_ref, a_ref, b_ref, send_ref = refs
-    devices = stack_ref.shape[0]
-    own = mass_ref.shape[0]
+        first_own, stack_ref, b_ref, g_ref, first_ref, totals_ref, send_ref = refs
+    devices, own, _ = stack_ref.shape
+    here = pl.ds(pl.multiple_of(first_own[0], own), own)
     top = stack_ref[0]
     for d in range(1, devices):
         top = jnp.maximum(top, stack_ref[d])
     summed = jnp.exp2(stack_ref[0] - top)
     for d in range(1, devices):
         summed += jnp.exp2(stack_ref[d] - top)
-    whole = top + jnp.log2(summed)
-    new = g_ref[...] + (mass_ref[...] - whole[:own])
+    gain = b_ref[here, :] - (top + jnp.log2(summed))
     if both_eps is None:
-        new = 2.0 * new
+        new = 2.0 * (g_ref[here, :] + gain)
         new_ref[...] = new
-        total_ref[...] = whole[own:]
     else:
-        totals = a_ref[:1, :] - b_ref[:1, :]
-        half = first_ref[...] * first_epsilon
-        new = LN2 * (epsilon * new + both_eps * totals - half)
+        difference = totals_ref[8:9, :] - totals_ref[:1, :]
+        half = first_ref[here, :] * first_epsilon
+        new = LN2 * (epsilon * (g_ref[...] + gain) + both_eps * difference - half)
     for d in range(devices):
         send_ref[d] = new
 
 
-def combine(stack, log_b, g_own, last):
+def combine(first_own, stack, log_b, g_pot, last):
     shape = jax.ShapeDtypeStruct
-    own = log_b.shape[0]
-    send = shape((stack.shape[0], own, TILE), jnp.float32)
+    send = shape(stack.shape, jnp.float32)
     if last is None:
         more, scales = (), (None, None)
-        out = (send, shape(log_b.shape, jnp.float32), shape((8, TILE), jnp.float32))
+        out = (send, shape(stack.shape[1:], jnp.float32))
     else:
-        more, scales = last[:3], last[3:]
+        more, scales = last[:2], last[2:]
         out = send
     return pl.pallas_call(
         functools.partial(combine_kernel, *scales),
         out_shape=out,
-        in_specs=[VMEM()] * (3 + len(more)),
+        in_specs=[SMEM()] + [VMEM()] * (3 + len(more)),
         out_specs=jax.tree.map(lambda _: VMEM(), out),
         name="combine",
         compiler_params=pltpu.CompilerParams(vmem_limit_bytes=VMEM_LIMIT // 2),
-    )(stack, log_b, g_own, *more)
-
-
-def lse_two(one, two):
-    top = jnp.maximum(one, two)
-    return top + jnp.log2(1.0 + jnp.exp2(jnp.minimum(one, two) - top))
+    )(first_own, stack, log_b, g_pot, *more)
+
+
+def lse_of(parts):
+    top = functools.reduce(jnp.maximum, parts)
+    return top + jnp.log2(sum(jnp.exp2(part - top) for part in parts))
 
 
 def over_cols(part, cols):
-    for mask in (1, 2, 6):
-        pairs = [(i, i ^ mask) for i in range(cols)]
-        part = lse_two(part, lax.ppermute(part, "col", pairs))
-    return part
+    def moved(value, pairs):
+        return lax.ppermute(value, "col", pairs)
+
+    part = lse_of([part, moved(part, [(i, i ^ 1) for i in range(cols)])])
+    away = sorted(range(2, cols, 2), key=lambda by: -min(by, cols - by))
+    return lse_of([part] + [moved(part, [(i, (i + by) % cols) for i in range(cols)]) for by in away])
 
 
 def exchange(blocks, rest):
@@ -375,11 +365,11 @@
     counts = tile_counts.reshape(row_blocks)
     mass_a = source_mass.reshape(row_blocks, TILE)
     first_own = (lax.axis_index("row") * own_blocks).reshape(1)
-
-    part, x1, x2, y, g_pot, half_x, log_a, log_b, g_own = first_row_pass(
+    counts, first_own = lax.optimization_barrier((counts, first_own))
+
+    part, x1, x2, y, g_first, half_x, log_a, log_b, mass = first_row_pass(
         cols,
         counts,
-        first_own,
         mass_a,
         target_mass.reshape(target_blocks, TILE),
         source_points,
@@ -388,41 +378,27 @@
     )
     x1, x2, y = (pltpu.with_memory_space_constraint(v, pltpu.VMEM) for v in (x1, x2, y))
 
-    g_first = g_own
-    f_pot = total_a = total_b = source = None
-    for step in range(ITERS):
-        epsilon = first_epsilon * 0.5**step
-        x = x1 if step == 0 else x2
-        if step == 0:
-            both = over_cols(part, col_devices)
-            part, total_b = both[:row_blocks], both[row_blocks:]
-            f_pot = log_a - part
-        else:
-            part = over_cols(row_pass(cols, counts, x, y, f_pot, g_pot, slots), col_devices)
-            f_pot = f_pot + (log_a - part)
-
-        part = col_pass(
-            cols, counts, x, y, f_pot, g_pot, mass_a if step == 0 else None, slots, row_devices
-        )
-        if step < ITERS - 1:
-            f_pot = 2.0 * f_pot
-            stack, rest = exchange(part, (f_pot, total_b))
-            f_pot, total_b = rest
-            send, g_own, total_a = combine(stack, log_b, g_own, None)
-            g_pot, rest = exchange(send, (f_pot, total_b))
-            f_pot, total_b = rest
-        else:
-            earlier = first_epsilon * (2.0 - 0.5**step) - epsilon
-            totals = epsilon * total_a[:1] + earlier * (total_a[:1] - total_b[:1])
-            source = half_x + LN2 * (epsilon * f_pot - totals)
-            stack, source = exchange(part, source)
-            both_eps = first_epsilon * (2.0 - 0.5**step)
-            send = combine(
-                stack, log_b, g_own, (g_first, total_a, total_b, epsilon, both_eps)
-            )
-            g_pot, source = exchange(send, source)
-        g_pot = g_pot.reshape(target_blocks, TILE)
-    return (source.reshape(rows), g_pot.reshape(target_cells))
+    f_pot = log_a - over_cols(part, col_devices)
+    part = col_pass(cols, counts, x1, y, f_pot, g_first, slots, row_devices)
+    stack, (f_pot, first_own) = exchange(part, (2.0 * f_pot, first_own))
+    send, g_own = combine(first_own, stack, log_b, g_first, None)
+    g_pot, (f_pot, first_own) = exchange(send, (f_pot, first_own))
+    g_pot = g_pot.reshape(target_blocks, TILE)
+
+    first, second = first_epsilon, 0.5 * first_epsilon
+    part = row_pass(cols, counts, x2, y, f_pot, g_pot, g_first, log_b, mass, slots)
+    both = over_cols(part, col_devices)
+    part, totals = both[:row_blocks], both[row_blocks:]
+    f_pot = f_pot + (log_a - part)
+    total_b, total_a = totals[:1], totals[8:9]
+    source = half_x + LN2 * (
+        second * f_pot - (second + first) * total_a + first * total_b
+    )
+    part = col_pass(cols, counts, x2, y, f_pot, g_pot, slots, row_devices)
+    stack, (source, totals, first_own) = exchange(part, (source, totals, first_own))
+    send = combine(first_own, stack, log_b, g_own, (g_first, totals, second, first + second))
+    target, source = exchange(send, source)
+    return (source.reshape(rows), target.reshape(target_cells))
 
 
 def solution(mesh):

time: 122 us -> 121 us (level)
    ppermute x6 -> x8, waiting for transfers between devices: 13.9 us -> 12.7 us  [moved(): return lax.ppermute(value, 'col', pairs)]
    ppermute x6 -> x8, starting transfers between devices: 9.5 us -> 8.7 us  [moved(): return lax.ppermute(value, 'col', pairs)]
  transfers between devices with their start and end apart: 6 -> 8, of which waited for: 6 -> 6; matrix products, arithmetic and copies ran while one was open for 0% -> 0% of each run, Pallas kernels for 0% -> 0%
where the time goes in v5:
time: 121 us; the launch traced here: 120 us
  blocking collectives  57.8 us (48%)
  Pallas kernels  38.7 us (32%)
  waiting for transfers between devices  12.7 us (10%)
  starting transfers between devices  8.7 us (7%)
    all_to_all x4, blocking collectives, exchange(): return lax.optimization_barrier((lax.all_to_all(blocks, 'row', 0, 0), rest))  57.8 us
    pallas_call x2, Pallas kernels, col_pass(): pl.pallas_call(functools.partial(col_pass_kernel, slots), out_shape=jax.S...  15.4 us
    pallas_call x1, Pallas kernels, first_row_pass(): pl.pallas_call(functools.partial(row_pass_kernel, LOG2E / first_epsilon,...  14.5 us
    ppermute x8, waiting for transfers between devices, moved(): return lax.ppermute(value, 'col', pairs)  12.7 us
    ppermute x8, starting transfers between devices, moved(): return lax.ppermute(value, 'col', pairs)  8.7 us
    pallas_call x1, Pallas kernels, row_pass(): pl.pallas_call(functools.partial(row_pass_kernel, None, slots), out_shape...  8.51 us
  transfers between devices with their start and end apart: 8, of which 6 were waited for; matrix products, arithmetic and copies ran while one was open for 0% of the time, Pallas kernels for 0%

profile of v5, /device:TPU:0, one launch (start us, length us, event | category | flops | bytes accessed | tf_op | source)
XLA Modules:
  0.0 120.4 jit_solution(18286881295197939158)
XLA Ops:
  0.6 0.0 copy-start
  0.6 0.0 copy-start.1
  0.7 14.5 %row_pass_first.1 = (f32[128,128]{1,0:T(8,128)S(1)}, bf16[128,128,128]{2,1,0:T(8,128)(2,1)S(1)}, bf16[128,128,128]{2,1,0:T(8,128)(2,1)S(1)}, bf16[64,131072]{1,0...) custom-call(s32[4,128]{1,0:T(4,128)} %bitcast.16, ...), custom_call_target="tpu_custom_call" | custom-call | tf_op jit(solution)/shard_map/row_pass_first/pallas_call | solution.py:236
  15.2 0.1 collective-permute-start
  15.2 1.2 %collective-permute-done = f32[128,128]{1,0:T(8,128)S(1)} collective-permute-done((f32[128,128]{1,0:T(8,128)S(1)}, f32[128,128]{1,0:T(8,128)S(1)}, u32[]{:S(2)}, u32[]{:S(2)}) %collective-permute-start) | collective-permute-done | bytes 65568 | tf_op jit(solution)/shard_map/ppermute | solution.py:342
  16.5 4.2 %collective-permute-start.3 = (f32[128,128]{1,0:T(8,128)S(1)}, f32[128,128]{1,0:T(8,128)S(1)}, u32[]{:S(2)}, u32[]{:S(2)}) collective-permute-start(f32[128,128]{1,0:T(8,128)S(1)} %multiply_add_fusion.3), channel_id=1, source_target_pairs={{0,6},{1,7},{2,0},{3,1},{4,2},{5,3},{6,4},{7,5},{8,14},{9,15},{10,... | collective-permute-start | bytes 196616 | tf_op jit(solution)/shard_map/ppermute | solution.py:342
  20.7 0.0 collective-permute-start.2
  20.7 1.8 %collective-permute-start.1 = (f32[128,128]{1,0:T(8,128)S(1)}, f32[128,128]{1,0:T(8,128)S(1)}, u32[]{:S(2)}, u32[]{:S(2)}) collective-permute-start(f32[128,128]{1,0:T(8,128)S(1)} %multiply_add_fusion.3), channel_id=1, source_target_pairs={{0,4},{1,5},{2,6},{3,7},{4,0},{5,1},{6,2},{7,3},{8,12},{9,13},{10,... | collective-permute-start | bytes 196616 | tf_op jit(solution)/shard_map/ppermute | solution.py:342
  22.6 0.1 collective-permute-done.3
  22.6 4.6 %collective-permute-done.2 = f32[128,128]{1,0:T(8,128)S(1)} collective-permute-done((f32[128,128]{1,0:T(8,128)S(1)}, f32[128,128]{1,0:T(8,128)S(1)}, u32[]{:S(2)}, u32[]{:S(2)}) %collective-permute-start.2) | collective-permute-done | bytes 65568 | tf_op jit(solution)/shard_map/ppermute | solution.py:342
  27.2 0.0 collective-permute-done.1
  27.2 0.1 broadcast_multiply_fusion
  27.3 0.0 copy-done
  27.3 0.0 copy-done.1
  27.3 7.7 %col_pass.2 = f32[16,64,128]{2,1,0:T(8,128)S(1)} custom-call(s32[4,128]{1,0:T(4,128)S(1)} %bitcast.17, s32[128]{0:T(128)S(1)} %bitcast.21, bf16[128,128,128]{2,1,0:T(8,128)(2,1)S(1)} %get-tuple-element.42.refs_2_, bf16[64,131072]{1,0:T(8,128)(2,1)S(1)} %get-tuple-element.41.refs_3_, f32[128,128]{1,0:T(8,128)S(1)} %get-tuple-element.79.refs_4_, ...), custom_call_target="tpu_custom_call" | custom-call | tf_op jit(solution)/shard_map/col_pass/pallas_call | solution.py:278
  35.0 18.2 %all_to_all.20.refs_1_ = f32[16,64,128]{2,1,0:T(8,128)S(1)} all-to-all(f32[16,64,128]{2,1,0:T(8,128)S(1)} %col_pass.2), channel_id=1, replica_groups=mesh['row'=16,'col'=8] {'row'}, dimensions={0} | all-to-all | bytes 1048576 | tf_op jit(solution)/shard_map/all_to_all | solution.py:351
  53.2 0.1 combine.2
  53.4 13.4 %all_to_all.21 = f32[16,64,128]{2,1,0:T(8,128)S(1)} all-to-all(f32[16,64,128]{2,1,0:T(8,128)S(1)} %get-tuple-element.55), channel_id=1, replica_groups=mesh['row'=16,'col'=8] {'row'}, dimensions={0} | all-to-all | bytes 1048576 | tf_op jit(solution)/shard_map/all_to_all | solution.py:351
  66.8 8.5 %row_pass.1 = f32[144,128]{1,0:T(8,128)S(1)} custom-call(s32[4,128]{1,0:T(4,128)S(1)} %bitcast.18, s32[128]{0:T(128)S(1)} %bitcast.22, bf16[128,128,128]{2,1,0:T(8,128)(2,1)S(1)} %get-tuple-element.40.refs_2_, bf16[64,131072]{1,0:T(8,128)(2,1)S(1)} %get-tuple-element.41.refs_3_, f32[128,128]{1,0:T(8,128)S(1)} %get-tuple-element.58.refs_4_, ...), custom_call_target="tpu_custom_call" | custom-call | tf_op jit(solution)/shard_map/row_pass/pallas_call | solution.py:265
  75.3 0.1 collective-permute-start.4
  75.4 1.3 %collective-permute-done.4 = f32[144,128]{1,0:T(8,128)S(1)} collective-permute-done((f32[144,128]{1,0:T(8,128)S(1)}, f32[144,128]{1,0:T(8,128)S(1)}, u32[]{:S(2)}, u32[]{:S(2)}) %collective-permute-start.4) | collective-permute-done | bytes 73760 | tf_op jit(solution)/shard_map/ppermute | solution.py:342
  76.7 1.0 collective-permute-start.7
  77.7 1.1 collective-permute-start.6
  78.8 0.4 collective-permute-start.5
  79.2 1.9 %collective-permute-done.7 = f32[144,128]{1,0:T(8,128)S(1)} collective-permute-done((f32[144,128]{1,0:T(8,128)S(1)}, f32[144,128]{1,0:T(8,128)S(1)}, u32[]{:S(2)}, u32[]{:S(2)}) %collective-permute-start.7) | collective-permute-done | bytes 73760 | tf_op jit(solution)/shard_map/ppermute | solution.py:342
  81.1 3.7 %collective-permute-done.6 = f32[144,128]{1,0:T(8,128)S(1)} collective-permute-done((f32[144,128]{1,0:T(8,128)S(1)}, f32[144,128]{1,0:T(8,128)S(1)}, u32[]{:S(2)}, u32[]{:S(2)}) %collective-permute-start.6) | collective-permute-done | bytes 73760 | tf_op jit(solution)/shard_map/ppermute | solution.py:342
  84.8 0.0 collective-permute-done.5
  84.8 0.1 multiply_add_fusion
  84.9 0.7 multiply_add_fusion.2
  85.6 7.7 %col_pass.3 = f32[16,64,128]{2,1,0:T(8,128)S(1)} custom-call(s32[4,128]{1,0:T(4,128)S(1)} %bitcast.19, s32[128]{0:T(128)S(1)} %bitcast.23, bf16[128,128,128]{2,1,0:T(8,128)(2,1)S(1)} %get-tuple-element.40.refs_2_, bf16[64,131072]{1,0:T(8,128)(2,1)S(1)} %get-tuple-element.41.refs_3_, f32[128,128]{1,0:T(8,128)S(1)} %get-tuple-element.77.refs_4_, ...), custom_call_target="tpu_custom_call" | custom-call | tf_op jit(solution)/shard_map/col_pass/pallas_call | solution.py:278
  93.3 13.0 %all_to_all.22.refs_1_ = f32[16,64,128]{2,1,0:T(8,128)S(1)} all-to-all(f32[16,64,128]{2,1,0:T(8,128)S(1)} %col_pass.3), channel_id=1, replica_groups=mesh['row'=16,'col'=8] {'row'}, dimensions={0} | all-to-all | bytes 1048576 | tf_op jit(solution)/shard_map/all_to_all | solution.py:351
  106.3 0.1 combine.3
  106.4 13.1 %all_to_all.23 = f32[16,64,128]{2,1,0:T(8,128)S(1)} all-to-all(f32[16,64,128]{2,1,0:T(8,128)S(1)} %combine.3), channel_id=1, replica_groups=mesh['row'=16,'col'=8] {'row'}, dimensions={0} | all-to-all | bytes 1048576 | tf_op jit(solution)/shard_map/all_to_all | solution.py:351
  119.6 0.8 copy.9
  (4 shorter events, 0.1 us)
Async XLA Ops:
  0.6 26.7 %copy-start = (s32[128,1,4]{0,2,1:T(4,128)S(1)}, s32[128,1,4]{0,2,1:T(4,128)}, u32[]{:S(2)}) copy-start(s32[128,1,4]{0,2,1:T(4,128)} %param.10) | copy-start | bytes 6148
  0.6 26.7 %copy-start.1 = (s32[128,1]{0,1:T(1,128)S(1)}, s32[128,1]{0,1:T(1,128)}, u32[]{:S(2)}) copy-start(s32[128,1]{0,1:T(1,128)} %param.11) | copy-start | bytes 1540
  15.2 1.3 %collective-permute-start = (f32[128,128]{1,0:T(8,128)S(1)}, f32[128,128]{1,0:T(8,128)S(1)}, u32[]{:S(2)}, u32[]{:S(2)}) collective-permute-start(f32[128,128]{1,0:T(8,128)S(1)} %get-tuple-element.44), channel_id=1, source_target_pairs={{0,1},{1,0},{2,3},{3,2},{4,5},{5,4},{6,7},{7,6},{8,9},{9,8},{10,11... | collective-permute-start | bytes 196616 | tf_op jit(solution)/shard_map/ppermute | solution.py:342
  16.5 6.1 %collective-permute-start.3 = (f32[128,128]{1,0:T(8,128)S(1)}, f32[128,128]{1,0:T(8,128)S(1)}, u32[]{:S(2)}, u32[]{:S(2)}) collective-permute-start(f32[128,128]{1,0:T(8,128)S(1)} %multiply_add_fusion.3), channel_id=1, source_target_pairs={{0,6},{1,7},{2,0},{3,1},{4,2},{5,3},{6,4},{7,5},{8,14},{9,15},{10,... | collective-permute-start | bytes 196616 | tf_op jit(solution)/shard_map/ppermute | solution.py:342
  20.7 6.5 %collective-permute-start.2 = (f32[128,128]{1,0:T(8,128)S(1)}, f32[128,128]{1,0:T(8,128)S(1)}, u32[]{:S(2)}, u32[]{:S(2)}) collective-permute-start(f32[128,128]{1,0:T(8,128)S(1)} %multiply_add_fusion.3), channel_id=1, source_target_pairs={{0,2},{1,3},{2,4},{3,5},{4,6},{5,7},{6,0},{7,1},{8,10},{9,11},{10,... | collective-permute-start | bytes 196616 | tf_op jit(solution)/shard_map/ppermute | solution.py:342
  20.7 6.5 %collective-permute-start.1 = (f32[128,128]{1,0:T(8,128)S(1)}, f32[128,128]{1,0:T(8,128)S(1)}, u32[]{:S(2)}, u32[]{:S(2)}) collective-permute-start(f32[128,128]{1,0:T(8,128)S(1)} %multiply_add_fusion.3), channel_id=1, source_target_pairs={{0,4},{1,5},{2,6},{3,7},{4,0},{5,1},{6,2},{7,3},{8,12},{9,13},{10,... | collective-permute-start | bytes 196616 | tf_op jit(solution)/shard_map/ppermute | solution.py:342
  75.3 1.3 %collective-permute-start.4 = (f32[144,128]{1,0:T(8,128)S(1)}, f32[144,128]{1,0:T(8,128)S(1)}, u32[]{:S(2)}, u32[]{:S(2)}) collective-permute-start(f32[144,128]{1,0:T(8,128)S(1)} %row_pass.1), channel_id=1, source_target_pairs={{0,1},{1,0},{2,3},{3,2},{4,5},{5,4},{6,7},{7,6},{8,9},{9,8},{10,11... | collective-permute-start | bytes 221192 | tf_op jit(solution)/shard_map/ppermute | solution.py:342
  76.7 4.4 %collective-permute-start.7 = (f32[144,128]{1,0:T(8,128)S(1)}, f32[144,128]{1,0:T(8,128)S(1)}, u32[]{:S(2)}, u32[]{:S(2)}) collective-permute-start(f32[144,128]{1,0:T(8,128)S(1)} %multiply_add_fusion.1), channel_id=1, source_target_pairs={{0,6},{1,7},{2,0},{3,1},{4,2},{5,3},{6,4},{7,5},{8,14},{9,15},{10,... | collective-permute-start | bytes 221192 | tf_op jit(solution)/shard_map/ppermute | solution.py:342
  77.7 7.1 %collective-permute-start.6 = (f32[144,128]{1,0:T(8,128)S(1)}, f32[144,128]{1,0:T(8,128)S(1)}, u32[]{:S(2)}, u32[]{:S(2)}) collective-permute-start(f32[144,128]{1,0:T(8,128)S(1)} %multiply_add_fusion.1), channel_id=1, source_target_pairs={{0,2},{1,3},{2,4},{3,5},{4,6},{5,7},{6,0},{7,1},{8,10},{9,11},{10,... | collective-permute-start | bytes 221192 | tf_op jit(solution)/shard_map/ppermute | solution.py:342
  78.8 6.0 %collective-permute-start.5 = (f32[144,128]{1,0:T(8,128)S(1)}, f32[144,128]{1,0:T(8,128)S(1)}, u32[]{:S(2)}, u32[]{:S(2)}) collective-permute-start(f32[144,128]{1,0:T(8,128)S(1)} %multiply_add_fusion.1), channel_id=1, source_target_pairs={{0,4},{1,5},{2,6},{3,7},{4,0},{5,1},{6,2},{7,3},{8,12},{9,13},{10,... | collective-permute-start | bytes 221192 | tf_op jit(solution)/shard_map/ppermute | solution.py:342

commit v6 on v5

--- a/solution.py
+++ b/solution.py
@@ -15,7 +15,7 @@
 SMALLEST = 2.0**-100
 LARGEST = 2.0**120
 VMEM_LIMIT = 16 * 1024 * 1024
-UNROLL = 16
+UNROLL = 32
 CHUNK = 64
 ROW_OFFSET = 64.0
 COL_OFFSET = 80.0

time: 121 us -> 117 us (0.967)
  Pallas kernels: 38.7 us -> 35.3 us
    pallas_call x1, Pallas kernels: 8.51 us -> 7.29 us  [row_pass(): pl.pallas_call(functools.partial(row_pass_kernel, None, slots), out_shape...]
  transfers between devices with their start and end apart: 8 -> 8, of which waited for: 6 -> 5; matrix products, arithmetic and copies ran while one was open for 0% -> 0% of each run, Pallas kernels for 0% -> 0%
where the time goes in v6:
time: 117 us
  blocking collectives  57.7 us (49%)
  Pallas kernels  35.3 us (30%)
  waiting for transfers between devices  12.6 us (11%)
  starting transfers between devices  8.91 us (8%)
    all_to_all x4, blocking collectives, exchange(): return lax.optimization_barrier((lax.all_to_all(blocks, 'row', 0, 0), rest))  57.7 us
    pallas_call x2, Pallas kernels, col_pass(): pl.pallas_call(functools.partial(col_pass_kernel, slots), out_shape=jax.S...  14.2 us
    pallas_call x1, Pallas kernels, first_row_pass(): pl.pallas_call(functools.partial(row_pass_kernel, LOG2E / first_epsilon,...  13.5 us
    ppermute x8, waiting for transfers between devices, moved(): return lax.ppermute(value, 'col', pairs)  12.6 us
    ppermute x8, starting transfers between devices, moved(): return lax.ppermute(value, 'col', pairs)  8.91 us
    pallas_call x1, Pallas kernels, row_pass(): pl.pallas_call(functools.partial(row_pass_kernel, None, slots), out_shape...  7.29 us
  transfers between devices with their start and end apart: 8, of which 5 were waited for; matrix products, arithmetic and copies ran while one was open for 0% of the time, Pallas kernels for 0%

profile of v6, /device:TPU:0, one launch (start us, length us, event | category | flops | bytes accessed | tf_op | source)
XLA Modules:
  0.0 117.0 jit_solution(9658924506290259024)
XLA Ops:
  0.6 0.0 copy-start
  0.6 0.0 copy-start.1
  0.7 13.5 %row_pass_first.1 = (f32[128,128]{1,0:T(8,128)S(1)}, bf16[128,128,128]{2,1,0:T(8,128)(2,1)S(1)}, bf16[128,128,128]{2,1,0:T(8,128)(2,1)S(1)}, bf16[64,131072]{1,0...) custom-call(s32[4,128]{1,0:T(4,128)} %bitcast.16, ...), custom_call_target="tpu_custom_call" | custom-call | tf_op jit(solution)/shard_map/row_pass_first/pallas_call | solution.py:236
  14.2 0.1 collective-permute-start
  14.3 1.2 %collective-permute-done = f32[128,128]{1,0:T(8,128)S(1)} collective-permute-done((f32[128,128]{1,0:T(8,128)S(1)}, f32[128,128]{1,0:T(8,128)S(1)}, u32[]{:S(2)}, u32[]{:S(2)}) %collective-permute-start) | collective-permute-done | bytes 65568 | tf_op jit(solution)/shard_map/ppermute | solution.py:342
  15.5 4.2 %collective-permute-start.3 = (f32[128,128]{1,0:T(8,128)S(1)}, f32[128,128]{1,0:T(8,128)S(1)}, u32[]{:S(2)}, u32[]{:S(2)}) collective-permute-start(f32[128,128]{1,0:T(8,128)S(1)} %multiply_add_fusion.3), channel_id=1, source_target_pairs={{0,6},{1,7},{2,0},{3,1},{4,2},{5,3},{6,4},{7,5},{8,14},{9,15},{10,... | collective-permute-start | bytes 196616 | tf_op jit(solution)/shard_map/ppermute | solution.py:342
  19.7 0.0 collective-permute-start.2
  19.7 1.9 %collective-permute-start.1 = (f32[128,128]{1,0:T(8,128)S(1)}, f32[128,128]{1,0:T(8,128)S(1)}, u32[]{:S(2)}, u32[]{:S(2)}) collective-permute-start(f32[128,128]{1,0:T(8,128)S(1)} %multiply_add_fusion.3), channel_id=1, source_target_pairs={{0,4},{1,5},{2,6},{3,7},{4,0},{5,1},{6,2},{7,3},{8,12},{9,13},{10,... | collective-permute-start | bytes 196616 | tf_op jit(solution)/shard_map/ppermute | solution.py:342
  21.6 0.0 collective-permute-done.3
  21.7 4.6 %collective-permute-done.2 = f32[128,128]{1,0:T(8,128)S(1)} collective-permute-done((f32[128,128]{1,0:T(8,128)S(1)}, f32[128,128]{1,0:T(8,128)S(1)}, u32[]{:S(2)}, u32[]{:S(2)}) %collective-permute-start.2) | collective-permute-done | bytes 65568 | tf_op jit(solution)/shard_map/ppermute | solution.py:342
  26.2 0.0 collective-permute-done.1
  26.2 0.1 broadcast_multiply_fusion
  26.3 0.0 copy-done
  26.3 0.0 copy-done.1
  26.3 7.1 %col_pass.2 = f32[16,64,128]{2,1,0:T(8,128)S(1)} custom-call(s32[4,128]{1,0:T(4,128)S(1)} %bitcast.17, s32[128]{0:T(128)S(1)} %bitcast.21, bf16[128,128,128]{2,1,0:T(8,128)(2,1)S(1)} %get-tuple-element.42.refs_2_, bf16[64,131072]{1,0:T(8,128)(2,1)S(1)} %get-tuple-element.41.refs_3_, f32[128,128]{1,0:T(8,128)S(1)} %get-tuple-element.79.refs_4_, ...), custom_call_target="tpu_custom_call" | custom-call | tf_op jit(solution)/shard_map/col_pass/pallas_call | solution.py:278
  33.5 18.2 %all_to_all.20.refs_1_ = f32[16,64,128]{2,1,0:T(8,128)S(1)} all-to-all(f32[16,64,128]{2,1,0:T(8,128)S(1)} %col_pass.2), channel_id=1, replica_groups=mesh['row'=16,'col'=8] {'row'}, dimensions={0} | all-to-all | bytes 1048576 | tf_op jit(solution)/shard_map/all_to_all | solution.py:351
  51.6 0.1 combine.2
  51.8 13.4 %all_to_all.21 = f32[16,64,128]{2,1,0:T(8,128)S(1)} all-to-all(f32[16,64,128]{2,1,0:T(8,128)S(1)} %get-tuple-element.55), channel_id=1, replica_groups=mesh['row'=16,'col'=8] {'row'}, dimensions={0} | all-to-all | bytes 1048576 | tf_op jit(solution)/shard_map/all_to_all | solution.py:351
  65.2 7.3 %row_pass.1 = f32[144,128]{1,0:T(8,128)S(1)} custom-call(s32[4,128]{1,0:T(4,128)S(1)} %bitcast.18, s32[128]{0:T(128)S(1)} %bitcast.22, bf16[128,128,128]{2,1,0:T(8,128)(2,1)S(1)} %get-tuple-element.40.refs_2_, bf16[64,131072]{1,0:T(8,128)(2,1)S(1)} %get-tuple-element.41.refs_3_, f32[128,128]{1,0:T(8,128)S(1)} %get-tuple-element.58.refs_4_, ...), custom_call_target="tpu_custom_call" | custom-call | tf_op jit(solution)/shard_map/row_pass/pallas_call | solution.py:265
  72.5 0.1 collective-permute-start.4
  72.6 1.3 %collective-permute-done.4 = f32[144,128]{1,0:T(8,128)S(1)} collective-permute-done((f32[144,128]{1,0:T(8,128)S(1)}, f32[144,128]{1,0:T(8,128)S(1)}, u32[]{:S(2)}, u32[]{:S(2)}) %collective-permute-start.4) | collective-permute-done | bytes 73760 | tf_op jit(solution)/shard_map/ppermute | solution.py:342
  73.9 1.1 collective-permute-start.7
  75.1 1.0 collective-permute-start.6
  76.0 0.6 collective-permute-start.5
  76.6 1.7 %collective-permute-done.7 = f32[144,128]{1,0:T(8,128)S(1)} collective-permute-done((f32[144,128]{1,0:T(8,128)S(1)}, f32[144,128]{1,0:T(8,128)S(1)}, u32[]{:S(2)}, u32[]{:S(2)}) %collective-permute-start.7) | collective-permute-done | bytes 73760 | tf_op jit(solution)/shard_map/ppermute | solution.py:342
  78.3 3.7 %collective-permute-done.6 = f32[144,128]{1,0:T(8,128)S(1)} collective-permute-done((f32[144,128]{1,0:T(8,128)S(1)}, f32[144,128]{1,0:T(8,128)S(1)}, u32[]{:S(2)}, u32[]{:S(2)}) %collective-permute-start.6) | collective-permute-done | bytes 73760 | tf_op jit(solution)/shard_map/ppermute | solution.py:342
  82.1 0.0 collective-permute-done.5
  82.1 0.1 multiply_add_fusion
  82.2 0.7 multiply_add_fusion.2
  82.9 7.1 %col_pass.3 = f32[16,64,128]{2,1,0:T(8,128)S(1)} custom-call(s32[4,128]{1,0:T(4,128)S(1)} %bitcast.19, s32[128]{0:T(128)S(1)} %bitcast.23, bf16[128,128,128]{2,1,0:T(8,128)(2,1)S(1)} %get-tuple-element.40.refs_2_, bf16[64,131072]{1,0:T(8,128)(2,1)S(1)} %get-tuple-element.41.refs_3_, f32[128,128]{1,0:T(8,128)S(1)} %get-tuple-element.77.refs_4_, ...), custom_call_target="tpu_custom_call" | custom-call | tf_op jit(solution)/shard_map/col_pass/pallas_call | solution.py:278
  90.0 12.9 %all_to_all.22.refs_1_ = f32[16,64,128]{2,1,0:T(8,128)S(1)} all-to-all(f32[16,64,128]{2,1,0:T(8,128)S(1)} %col_pass.3), channel_id=1, replica_groups=mesh['row'=16,'col'=8] {'row'}, dimensions={0} | all-to-all | bytes 1048576 | tf_op jit(solution)/shard_map/all_to_all | solution.py:351
  102.9 0.1 combine.3
  103.1 13.1 %all_to_all.23 = f32[16,64,128]{2,1,0:T(8,128)S(1)} all-to-all(f32[16,64,128]{2,1,0:T(8,128)S(1)} %combine.3), channel_id=1, replica_groups=mesh['row'=16,'col'=8] {'row'}, dimensions={0} | all-to-all | bytes 1048576 | tf_op jit(solution)/shard_map/all_to_all | solution.py:351
  116.2 0.8 copy.9
  (4 shorter events, 0.1 us)
Async XLA Ops:
  0.6 25.7 %copy-start = (s32[128,1,4]{0,2,1:T(4,128)S(1)}, s32[128,1,4]{0,2,1:T(4,128)}, u32[]{:S(2)}) copy-start(s32[128,1,4]{0,2,1:T(4,128)} %param.10) | copy-start | bytes 6148
  0.6 25.7 %copy-start.1 = (s32[128,1]{0,1:T(1,128)S(1)}, s32[128,1]{0,1:T(1,128)}, u32[]{:S(2)}) copy-start(s32[128,1]{0,1:T(1,128)} %param.11) | copy-start | bytes 1540
  14.2 1.3 %collective-permute-start = (f32[128,128]{1,0:T(8,128)S(1)}, f32[128,128]{1,0:T(8,128)S(1)}, u32[]{:S(2)}, u32[]{:S(2)}) collective-permute-start(f32[128,128]{1,0:T(8,128)S(1)} %get-tuple-element.44), channel_id=1, source_target_pairs={{0,1},{1,0},{2,3},{3,2},{4,5},{5,4},{6,7},{7,6},{8,9},{9,8},{10,11... | collective-permute-start | bytes 196616 | tf_op jit(solution)/shard_map/ppermute | solution.py:342
  15.5 6.1 %collective-permute-start.3 = (f32[128,128]{1,0:T(8,128)S(1)}, f32[128,128]{1,0:T(8,128)S(1)}, u32[]{:S(2)}, u32[]{:S(2)}) collective-permute-start(f32[128,128]{1,0:T(8,128)S(1)} %multiply_add_fusion.3), channel_id=1, source_target_pairs={{0,6},{1,7},{2,0},{3,1},{4,2},{5,3},{6,4},{7,5},{8,14},{9,15},{10,... | collective-permute-start | bytes 196616 | tf_op jit(solution)/shard_map/ppermute | solution.py:342
  19.7 6.5 %collective-permute-start.2 = (f32[128,128]{1,0:T(8,128)S(1)}, f32[128,128]{1,0:T(8,128)S(1)}, u32[]{:S(2)}, u32[]{:S(2)}) collective-permute-start(f32[128,128]{1,0:T(8,128)S(1)} %multiply_add_fusion.3), channel_id=1, source_target_pairs={{0,2},{1,3},{2,4},{3,5},{4,6},{5,7},{6,0},{7,1},{8,10},{9,11},{10,... | collective-permute-start | bytes 196616 | tf_op jit(solution)/shard_map/ppermute | solution.py:342
  19.7 6.5 %collective-permute-start.1 = (f32[128,128]{1,0:T(8,128)S(1)}, f32[128,128]{1,0:T(8,128)S(1)}, u32[]{:S(2)}, u32[]{:S(2)}) collective-permute-start(f32[128,128]{1,0:T(8,128)S(1)} %multiply_add_fusion.3), channel_id=1, source_target_pairs={{0,4},{1,5},{2,6},{3,7},{4,0},{5,1},{6,2},{7,3},{8,12},{9,13},{10,... | collective-permute-start | bytes 196616 | tf_op jit(solution)/shard_map/ppermute | solution.py:342
  72.5 1.3 %collective-permute-start.4 = (f32[144,128]{1,0:T(8,128)S(1)}, f32[144,128]{1,0:T(8,128)S(1)}, u32[]{:S(2)}, u32[]{:S(2)}) collective-permute-start(f32[144,128]{1,0:T(8,128)S(1)} %row_pass.1), channel_id=1, source_target_pairs={{0,1},{1,0},{2,3},{3,2},{4,5},{5,4},{6,7},{7,6},{8,9},{9,8},{10,11... | collective-permute-start | bytes 221192 | tf_op jit(solution)/shard_map/ppermute | solution.py:342
  73.9 4.4 %collective-permute-start.7 = (f32[144,128]{1,0:T(8,128)S(1)}, f32[144,128]{1,0:T(8,128)S(1)}, u32[]{:S(2)}, u32[]{:S(2)}) collective-permute-start(f32[144,128]{1,0:T(8,128)S(1)} %multiply_add_fusion.1), channel_id=1, source_target_pairs={{0,6},{1,7},{2,0},{3,1},{4,2},{5,3},{6,4},{7,5},{8,14},{9,15},{10,... | collective-permute-start | bytes 221192 | tf_op jit(solution)/shard_map/ppermute | solution.py:342
  75.1 7.0 %collective-permute-start.6 = (f32[144,128]{1,0:T(8,128)S(1)}, f32[144,128]{1,0:T(8,128)S(1)}, u32[]{:S(2)}, u32[]{:S(2)}) collective-permute-start(f32[144,128]{1,0:T(8,128)S(1)} %multiply_add_fusion.1), channel_id=1, source_target_pairs={{0,2},{1,3},{2,4},{3,5},{4,6},{5,7},{6,0},{7,1},{8,10},{9,11},{10,... | collective-permute-start | bytes 221192 | tf_op jit(solution)/shard_map/ppermute | solution.py:342
  76.0 6.1 %collective-permute-start.5 = (f32[144,128]{1,0:T(8,128)S(1)}, f32[144,128]{1,0:T(8,128)S(1)}, u32[]{:S(2)}, u32[]{:S(2)}) collective-permute-start(f32[144,128]{1,0:T(8,128)S(1)} %multiply_add_fusion.1), channel_id=1, source_target_pairs={{0,4},{1,5},{2,6},{3,7},{4,0},{5,1},{6,2},{7,3},{8,12},{9,13},{10,... | collective-permute-start | bytes 221192 | tf_op jit(solution)/shard_map/ppermute | solution.py:342

commit v7 on v6

--- a/solution.py
+++ b/solution.py
@@ -15,7 +15,8 @@
 SMALLEST = 2.0**-100
 LARGEST = 2.0**120
 VMEM_LIMIT = 16 * 1024 * 1024
-UNROLL = 32
+ROW_UNROLL = 128
+COL_UNROLL = 64
 CHUNK = 64
 ROW_OFFSET = 64.0
 COL_OFFSET = 80.0
@@ -130,7 +131,7 @@
     blocks = total.shape[1]
     lane = lax.broadcasted_iota(jnp.int32, (TILE, TILE), 1)
 
-    @pl.loop(0, blocks, unroll=UNROLL)
+    @pl.loop(0, blocks, unroll=ROW_UNROLL)
     def _(r):
         scores = products(x_ref, y_ref, f_ref, cols, slots, r, offset)
         terms = None
@@ -186,7 +187,7 @@
         return least, most
 
     ones = jnp.ones((1, TILE), jnp.float32)
-    least, most = lax.fori_loop(0, blocks, visit, (ones, ones), unroll=UNROLL)
+    least, most = lax.fori_loop(0, blocks, visit, (ones, ones), unroll=COL_UNROLL)
     fine = jnp.logical_and(jnp.min(least) >= SMALLEST, jnp.max(most) <= LARGEST / blocks)
 
     @pl.when(fine)
@@ -397,7 +398,8 @@
     part = col_pass(cols, counts, x2, y, f_pot, g_pot, slots, row_devices)
     stack, (source, totals, first_own) = exchange(part, (source, totals, first_own))
     send = combine(first_own, stack, log_b, g_own, (g_first, totals, second, first + second))
-    target, source = exchange(send, source)
+    send, source = lax.optimization_barrier((send, source))
+    target = lax.all_to_all(send, "row", 0, 0)
     return (source.reshape(rows), target.reshape(target_cells))
 
 

time: 117 us -> 115 us (0.983)
  Pallas kernels: 35.3 us -> 33.4 us
    all_to_all x0 -> x1, blocking collectives: none -> 13.1 us  [body(): target = lax.all_to_all(send, 'row', 0, 0)]
    all_to_all x4 -> x3, blocking collectives: 57.7 us -> 44.7 us  [exchange(): return lax.optimization_barrier((lax.all_to_all(blocks, 'row', 0, 0), rest))]
where the time goes in v7:
time: 115 us
  blocking collectives  57.8 us (50%)
  Pallas kernels  33.4 us (29%)
  waiting for transfers between devices  12.7 us (11%)
  starting transfers between devices  8.78 us (8%)
    all_to_all x3, blocking collectives, exchange(): return lax.optimization_barrier((lax.all_to_all(blocks, 'row', 0, 0), rest))  44.7 us
    pallas_call x2, Pallas kernels, col_pass(): pl.pallas_call(functools.partial(col_pass_kernel, slots), out_shape=jax.S...  13.7 us
    all_to_all x1, blocking collectives, body(): target = lax.all_to_all(send, 'row', 0, 0)  13.1 us
    pallas_call x1, Pallas kernels, first_row_pass(): pl.pallas_call(functools.partial(row_pass_kernel, LOG2E / first_epsilon,...  12.7 us
    ppermute x8, waiting for transfers between devices, moved(): return lax.ppermute(value, 'col', pairs)  12.7 us
    ppermute x8, starting transfers between devices, moved(): return lax.ppermute(value, 'col', pairs)  8.78 us
    pallas_call x1, Pallas kernels, row_pass(): pl.pallas_call(functools.partial(row_pass_kernel, None, slots), out_shape...  6.76 us
  transfers between devices with their start and end apart: 8, of which 5 were waited for; matrix products, arithmetic and copies ran while one was open for 0% of the time, Pallas kernels for 0%

profile of v7, /device:TPU:0, one launch (start us, length us, event | category | flops | bytes accessed | tf_op | source)
XLA Modules:
  0.0 115.1 jit_solution(9330700627935573254)
XLA Ops:
  0.6 0.0 copy-start
  0.6 0.0 copy-start.1
  0.7 12.7 %row_pass_first.1 = (f32[128,128]{1,0:T(8,128)S(1)}, bf16[128,128,128]{2,1,0:T(8,128)(2,1)S(1)}, bf16[128,128,128]{2,1,0:T(8,128)(2,1)S(1)}, bf16[64,131072]{1,0...) custom-call(s32[4,128]{1,0:T(4,128)} %bitcast.16, ...), custom_call_target="tpu_custom_call" | custom-call | tf_op jit(solution)/shard_map/row_pass_first/pallas_call | solution.py:237
  13.3 0.1 collective-permute-start
  13.4 1.2 %collective-permute-done = f32[128,128]{1,0:T(8,128)S(1)} collective-permute-done((f32[128,128]{1,0:T(8,128)S(1)}, f32[128,128]{1,0:T(8,128)S(1)}, u32[]{:S(2)}, u32[]{:S(2)}) %collective-permute-start) | collective-permute-done | bytes 65568 | tf_op jit(solution)/shard_map/ppermute | solution.py:343
  14.7 4.2 %collective-permute-start.3 = (f32[128,128]{1,0:T(8,128)S(1)}, f32[128,128]{1,0:T(8,128)S(1)}, u32[]{:S(2)}, u32[]{:S(2)}) collective-permute-start(f32[128,128]{1,0:T(8,128)S(1)} %multiply_add_fusion.3), channel_id=1, source_target_pairs={{0,6},{1,7},{2,0},{3,1},{4,2},{5,3},{6,4},{7,5},{8,14},{9,15},{10,... | collective-permute-start | bytes 196616 | tf_op jit(solution)/shard_map/ppermute | solution.py:343
  18.9 0.0 collective-permute-start.2
  18.9 1.9 %collective-permute-start.1 = (f32[128,128]{1,0:T(8,128)S(1)}, f32[128,128]{1,0:T(8,128)S(1)}, u32[]{:S(2)}, u32[]{:S(2)}) collective-permute-start(f32[128,128]{1,0:T(8,128)S(1)} %multiply_add_fusion.3), channel_id=1, source_target_pairs={{0,4},{1,5},{2,6},{3,7},{4,0},{5,1},{6,2},{7,3},{8,12},{9,13},{10,... | collective-permute-start | bytes 196616 | tf_op jit(solution)/shard_map/ppermute | solution.py:343
  20.8 0.0 collective-permute-done.3
  20.8 4.6 %collective-permute-done.2 = f32[128,128]{1,0:T(8,128)S(1)} collective-permute-done((f32[128,128]{1,0:T(8,128)S(1)}, f32[128,128]{1,0:T(8,128)S(1)}, u32[]{:S(2)}, u32[]{:S(2)}) %collective-permute-start.2) | collective-permute-done | bytes 65568 | tf_op jit(solution)/shard_map/ppermute | solution.py:343
  25.4 0.0 collective-permute-done.1
  25.4 0.1 broadcast_multiply_fusion
  25.5 0.0 copy-done
  25.5 0.0 copy-done.1
  25.5 6.8 %col_pass.2 = f32[16,64,128]{2,1,0:T(8,128)S(1)} custom-call(s32[4,128]{1,0:T(4,128)S(1)} %bitcast.17, s32[128]{0:T(128)S(1)} %bitcast.21, bf16[128,128,128]{2,1,0:T(8,128)(2,1)S(1)} %get-tuple-element.40.refs_2_, bf16[64,131072]{1,0:T(8,128)(2,1)S(1)} %get-tuple-element.39.refs_3_, f32[128,128]{1,0:T(8,128)S(1)} %get-tuple-element.75.refs_4_, ...), custom_call_target="tpu_custom_call" | custom-call | tf_op jit(solution)/shard_map/col_pass/pallas_call | solution.py:279
  32.4 18.2 %all_to_all.20.refs_1_ = f32[16,64,128]{2,1,0:T(8,128)S(1)} all-to-all(f32[16,64,128]{2,1,0:T(8,128)S(1)} %col_pass.2), channel_id=1, replica_groups=mesh['row'=16,'col'=8] {'row'}, dimensions={0} | all-to-all | bytes 1048576 | tf_op jit(solution)/shard_map/all_to_all | solution.py:352
  50.6 0.1 combine.2
  50.7 13.4 %all_to_all.21 = f32[16,64,128]{2,1,0:T(8,128)S(1)} all-to-all(f32[16,64,128]{2,1,0:T(8,128)S(1)} %get-tuple-element.53), channel_id=1, replica_groups=mesh['row'=16,'col'=8] {'row'}, dimensions={0} | all-to-all | bytes 1048576 | tf_op jit(solution)/shard_map/all_to_all | solution.py:352
  64.2 6.8 %row_pass.1 = f32[144,128]{1,0:T(8,128)S(1)} custom-call(s32[4,128]{1,0:T(4,128)S(1)} %bitcast.18, s32[128]{0:T(128)S(1)} %bitcast.22, bf16[128,128,128]{2,1,0:T(8,128)(2,1)S(1)} %get-tuple-element.38.refs_2_, bf16[64,131072]{1,0:T(8,128)(2,1)S(1)} %get-tuple-element.39.refs_3_, f32[128,128]{1,0:T(8,128)S(1)} %get-tuple-element.56.refs_4_, ...), custom_call_target="tpu_custom_call" | custom-call | tf_op jit(solution)/shard_map/row_pass/pallas_call | solution.py:266
  70.9 0.0 collective-permute-start.4
  70.9 1.3 %collective-permute-done.4 = f32[144,128]{1,0:T(8,128)S(1)} collective-permute-done((f32[144,128]{1,0:T(8,128)S(1)}, f32[144,128]{1,0:T(8,128)S(1)}, u32[]{:S(2)}, u32[]{:S(2)}) %collective-permute-start.4) | collective-permute-done | bytes 73760 | tf_op jit(solution)/shard_map/ppermute | solution.py:343
  72.3 1.1 collective-permute-start.7
  73.3 1.0 collective-permute-start.6
  74.3 0.5 collective-permute-start.5
  74.9 1.8 %collective-permute-done.7 = f32[144,128]{1,0:T(8,128)S(1)} collective-permute-done((f32[144,128]{1,0:T(8,128)S(1)}, f32[144,128]{1,0:T(8,128)S(1)}, u32[]{:S(2)}, u32[]{:S(2)}) %collective-permute-start.7) | collective-permute-done | bytes 73760 | tf_op jit(solution)/shard_map/ppermute | solution.py:343
  76.7 3.7 %collective-permute-done.6 = f32[144,128]{1,0:T(8,128)S(1)} collective-permute-done((f32[144,128]{1,0:T(8,128)S(1)}, f32[144,128]{1,0:T(8,128)S(1)}, u32[]{:S(2)}, u32[]{:S(2)}) %collective-permute-start.6) | collective-permute-done | bytes 73760 | tf_op jit(solution)/shard_map/ppermute | solution.py:343
  80.4 0.0 collective-permute-done.5
  80.4 0.1 multiply_add_fusion
  80.5 0.7 multiply_add_fusion.2
  81.2 6.8 %col_pass.3 = f32[16,64,128]{2,1,0:T(8,128)S(1)} custom-call(s32[4,128]{1,0:T(4,128)S(1)} %bitcast.19, s32[128]{0:T(128)S(1)} %bitcast.23, bf16[128,128,128]{2,1,0:T(8,128)(2,1)S(1)} %get-tuple-element.38.refs_2_, bf16[64,131072]{1,0:T(8,128)(2,1)S(1)} %get-tuple-element.39.refs_3_, f32[128,128]{1,0:T(8,128)S(1)} %get-tuple-element.73.refs_4_, ...), custom_call_target="tpu_custom_call" | custom-call | tf_op jit(solution)/shard_map/col_pass/pallas_call | solution.py:279
  88.0 13.0 %all_to_all.22.refs_1_ = f32[16,64,128]{2,1,0:T(8,128)S(1)} all-to-all(f32[16,64,128]{2,1,0:T(8,128)S(1)} %col_pass.3), channel_id=1, replica_groups=mesh['row'=16,'col'=8] {'row'}, dimensions={0} | all-to-all | bytes 1048576 | tf_op jit(solution)/shard_map/all_to_all | solution.py:352
  101.0 0.1 combine.3
  101.2 13.1 %all_to_all.23 = f32[16,64,128]{2,1,0:T(8,128)S(1)} all-to-all(f32[16,64,128]{2,1,0:T(8,128)S(1)} %combine.3), channel_id=1, replica_groups=mesh['row'=16,'col'=8] {'row'}, dimensions={0} | all-to-all | bytes 1048576 | tf_op jit(solution)/shard_map/all_to_all | solution.py:402
  114.3 0.8 copy.9
  (4 shorter events, 0.1 us)
Async XLA Ops:
  0.6 24.8 %copy-start = (s32[128,1,4]{0,2,1:T(4,128)S(1)}, s32[128,1,4]{0,2,1:T(4,128)}, u32[]{:S(2)}) copy-start(s32[128,1,4]{0,2,1:T(4,128)} %param.10) | copy-start | bytes 6148
  0.6 24.8 %copy-start.1 = (s32[128,1]{0,1:T(1,128)S(1)}, s32[128,1]{0,1:T(1,128)}, u32[]{:S(2)}) copy-start(s32[128,1]{0,1:T(1,128)} %param.11) | copy-start | bytes 1540
  13.3 1.3 %collective-permute-start = (f32[128,128]{1,0:T(8,128)S(1)}, f32[128,128]{1,0:T(8,128)S(1)}, u32[]{:S(2)}, u32[]{:S(2)}) collective-permute-start(f32[128,128]{1,0:T(8,128)S(1)} %get-tuple-element.42), channel_id=1, source_target_pairs={{0,1},{1,0},{2,3},{3,2},{4,5},{5,4},{6,7},{7,6},{8,9},{9,8},{10,11... | collective-permute-start | bytes 196616 | tf_op jit(solution)/shard_map/ppermute | solution.py:343
  14.7 6.1 %collective-permute-start.3 = (f32[128,128]{1,0:T(8,128)S(1)}, f32[128,128]{1,0:T(8,128)S(1)}, u32[]{:S(2)}, u32[]{:S(2)}) collective-permute-start(f32[128,128]{1,0:T(8,128)S(1)} %multiply_add_fusion.3), channel_id=1, source_target_pairs={{0,6},{1,7},{2,0},{3,1},{4,2},{5,3},{6,4},{7,5},{8,14},{9,15},{10,... | collective-permute-start | bytes 196616 | tf_op jit(solution)/shard_map/ppermute | solution.py:343
  18.9 6.5 %collective-permute-start.2 = (f32[128,128]{1,0:T(8,128)S(1)}, f32[128,128]{1,0:T(8,128)S(1)}, u32[]{:S(2)}, u32[]{:S(2)}) collective-permute-start(f32[128,128]{1,0:T(8,128)S(1)} %multiply_add_fusion.3), channel_id=1, source_target_pairs={{0,2},{1,3},{2,4},{3,5},{4,6},{5,7},{6,0},{7,1},{8,10},{9,11},{10,... | collective-permute-start | bytes 196616 | tf_op jit(solution)/shard_map/ppermute | solution.py:343
  18.9 6.5 %collective-permute-start.1 = (f32[128,128]{1,0:T(8,128)S(1)}, f32[128,128]{1,0:T(8,128)S(1)}, u32[]{:S(2)}, u32[]{:S(2)}) collective-permute-start(f32[128,128]{1,0:T(8,128)S(1)} %multiply_add_fusion.3), channel_id=1, source_target_pairs={{0,4},{1,5},{2,6},{3,7},{4,0},{5,1},{6,2},{7,3},{8,12},{9,13},{10,... | collective-permute-start | bytes 196616 | tf_op jit(solution)/shard_map/ppermute | solution.py:343
  70.9 1.3 %collective-permute-start.4 = (f32[144,128]{1,0:T(8,128)S(1)}, f32[144,128]{1,0:T(8,128)S(1)}, u32[]{:S(2)}, u32[]{:S(2)}) collective-permute-start(f32[144,128]{1,0:T(8,128)S(1)} %row_pass.1), channel_id=1, source_target_pairs={{0,1},{1,0},{2,3},{3,2},{4,5},{5,4},{6,7},{7,6},{8,9},{9,8},{10,11... | collective-permute-start | bytes 221192 | tf_op jit(solution)/shard_map/ppermute | solution.py:343
  72.3 4.4 %collective-permute-start.7 = (f32[144,128]{1,0:T(8,128)S(1)}, f32[144,128]{1,0:T(8,128)S(1)}, u32[]{:S(2)}, u32[]{:S(2)}) collective-permute-start(f32[144,128]{1,0:T(8,128)S(1)} %multiply_add_fusion.1), channel_id=1, source_target_pairs={{0,6},{1,7},{2,0},{3,1},{4,2},{5,3},{6,4},{7,5},{8,14},{9,15},{10,... | collective-permute-start | bytes 221192 | tf_op jit(solution)/shard_map/ppermute | solution.py:343
  73.3 7.1 %collective-permute-start.6 = (f32[144,128]{1,0:T(8,128)S(1)}, f32[144,128]{1,0:T(8,128)S(1)}, u32[]{:S(2)}, u32[]{:S(2)}) collective-permute-start(f32[144,128]{1,0:T(8,128)S(1)} %multiply_add_fusion.1), channel_id=1, source_target_pairs={{0,2},{1,3},{2,4},{3,5},{4,6},{5,7},{6,0},{7,1},{8,10},{9,11},{10,... | collective-permute-start | bytes 221192 | tf_op jit(solution)/shard_map/ppermute | solution.py:343
  74.3 6.1 %collective-permute-start.5 = (f32[144,128]{1,0:T(8,128)S(1)}, f32[144,128]{1,0:T(8,128)S(1)}, u32[]{:S(2)}, u32[]{:S(2)}) collective-permute-start(f32[144,128]{1,0:T(8,128)S(1)} %multiply_add_fusion.1), channel_id=1, source_target_pairs={{0,4},{1,5},{2,6},{3,7},{4,0},{5,1},{6,2},{7,3},{8,12},{9,13},{10,... | collective-permute-start | bytes 221192 | tf_op jit(solution)/shard_map/ppermute | solution.py:343

commit v8 on v7

--- a/solution.py
+++ b/solution.py
@@ -169,8 +169,18 @@
         out_ref[:blocks, :] = (total[...] - offset).T
 
 
-def col_pass_kernel(slots, *refs):
-    cols, counts, x_ref, y_ref, f_ref, g_ref, out_ref, total = refs
+def col_pass_kernel(slots, last, *refs):
+    if last is None:
+        cols, counts, x_ref, y_ref, f_ref, g_ref, out_ref, total = refs
+    else:
+        (cols, counts, x_ref, y_ref, f_ref, g_ref, hx_ref, totals_ref, out_ref, source_hbm, total,
+         source, sem) = refs
+        second, first = last
+        total_b, total_a = totals_ref[:1, :], totals_ref[8:9, :]
+        shift = first * total_b - (second + first) * total_a
+        source[...] = hx_ref[...] + LN2 * (second * f_ref[...] + shift)
+        source_copy = pltpu.make_async_copy(source, source_hbm, sem)
+        source_copy.start()
     blocks = f_ref.shape[0]
     total[...] = jnp.zeros_like(total)
 
@@ -188,12 +198,10 @@
 
     ones = jnp.ones((1, TILE), jnp.float32)
     least, most = lax.fori_loop(0, blocks, visit, (ones, ones), unroll=COL_UNROLL)
+    sums = total[...]
+    result = jnp.where(sums > 0.0, jnp.log2(sums) - COL_OFFSET, very_negative)
+    out_ref[...] = result.reshape(out_ref.shape)
     fine = jnp.logical_and(jnp.min(least) >= SMALLEST, jnp.max(most) <= LARGEST / blocks)
-
-    @pl.when(fine)
-    def _():
-        sums = total[...]
-        total[...] = jnp.where(sums > 0.0, jnp.log2(sums) - COL_OFFSET, very_negative)
 
     @pl.when(jnp.logical_not(fine))
     def _():
@@ -216,7 +224,10 @@
                     peak = jnp.maximum(old, mine)
                     total[at, :] = peak + jnp.log2(jnp.exp2(old - peak) + jnp.exp2(mine - peak))
 
-    out_ref[...] = total[...].reshape(out_ref.shape)
+        out_ref[...] = total[...].reshape(out_ref.shape)
+
+    if last is not None:
+        source_copy.wait()
 
 
 SMEM = functools.partial(pl.BlockSpec, memory_space=pltpu.SMEM)
@@ -274,19 +285,24 @@
     )(cols, counts, x, y, f_pot, g_pot, g_first, log_b, mass)
 
 
-def col_pass(cols, counts, x, y, f_pot, g_pot, slots, devices):
+def col_pass(cols, counts, x, y, f_pot, g_pot, slots, devices, last=None):
     target_blocks = g_pot.shape[0]
+    out = jax.ShapeDtypeStruct((devices, target_blocks // devices, TILE), jnp.float32)
+    scratch = [pltpu.VMEM((target_blocks, TILE), jnp.float32)]
+    more, scales, out_specs = (), None, VMEM()
+    if last is not None:
+        more, scales = last[:2], last[2:]
+        out, out_specs = (out, pltpu.HBM(f_pot.shape, jnp.float32)), (VMEM(), ANY())
+        scratch += [pltpu.VMEM(f_pot.shape, jnp.float32), pltpu.SemaphoreType.DMA]
     return pl.pallas_call(
-        functools.partial(col_pass_kernel, slots),
-        out_shape=jax.ShapeDtypeStruct(
-            (devices, target_blocks // devices, TILE), jnp.float32
-        ),
-        in_specs=[SMEM(), SMEM()] + [VMEM()] * 4,
-        out_specs=VMEM(),
-        scratch_shapes=[pltpu.VMEM((target_blocks, TILE), jnp.float32)],
+        functools.partial(col_pass_kernel, slots, scales),
+        out_shape=out,
+        in_specs=[SMEM(), SMEM()] + [VMEM()] * (4 + len(more)),
+        out_specs=out_specs,
+        scratch_shapes=scratch,
         name="col_pass",
         compiler_params=pltpu.CompilerParams(vmem_limit_bytes=VMEM_LIMIT),
-    )(cols, counts, x, y, f_pot, g_pot)
+    )(cols, counts, x, y, f_pot, g_pot, *more)
 
 
 def combine_kernel(epsilon, both_eps, *refs):
@@ -343,8 +359,8 @@
         return lax.ppermute(value, "col", pairs)
 
     part = lse_of([part, moved(part, [(i, i ^ 1) for i in range(cols)])])
-    away = sorted(range(2, cols, 2), key=lambda by: -min(by, cols - by))
-    return lse_of([part] + [moved(part, [(i, (i + by) % cols) for i in range(cols)]) for by in away])
+    masks = range(2, cols, 2)
+    return lse_of([part] + [moved(part, [(i, i ^ mask) for i in range(cols)]) for mask in masks])
 
 
 def exchange(blocks, rest):
@@ -391,14 +407,11 @@
     both = over_cols(part, col_devices)
     part, totals = both[:row_blocks], both[row_blocks:]
     f_pot = f_pot + (log_a - part)
-    total_b, total_a = totals[:1], totals[8:9]
-    source = half_x + LN2 * (
-        second * f_pot - (second + first) * total_a + first * total_b
+    part, source = col_pass(
+        cols, counts, x2, y, f_pot, g_pot, slots, row_devices, (half_x, totals, second, first)
     )
-    part = col_pass(cols, counts, x2, y, f_pot, g_pot, slots, row_devices)
-    stack, (source, totals, first_own) = exchange(part, (source, totals, first_own))
+    stack, (totals, first_own) = exchange(part, (totals, first_own))
     send = combine(first_own, stack, log_b, g_own, (g_first, totals, second, first + second))
-    send, source = lax.optimization_barrier((send, source))
     target = lax.all_to_all(send, "row", 0, 0)
     return (source.reshape(rows), target.reshape(target_cells))
 

time: 115 us -> 113 us (0.983)
  blocking collectives: 57.8 us -> 56.3 us
    all_to_all x3, blocking collectives: 44.7 us -> 43.2 us  [exchange(): return lax.optimization_barrier((lax.all_to_all(blocks, 'row', 0, 0), rest))]
  transfers between devices with their start and end apart: 8 -> 8, of which waited for: 5 -> 6; matrix products, arithmetic and copies ran while one was open for 0% -> 0% of each run, Pallas kernels for 0% -> 0%
where the time goes in v8:
time: 113 us; the launch traced here: 112 us
  blocking collectives  56.3 us (50%)
  Pallas kernels  33.2 us (29%)
  waiting for transfers between devices  11.6 us (10%)
  starting transfers between devices  9.43 us (8%)
    all_to_all x3, blocking collectives, exchange(): return lax.optimization_barrier((lax.all_to_all(blocks, 'row', 0, 0), rest))  43.2 us
    pallas_call x2, Pallas kernels, col_pass(): pl.pallas_call(functools.partial(col_pass_kernel, slots, scales), out_sha...  13.5 us
    all_to_all x1, blocking collectives, body(): target = lax.all_to_all(send, 'row', 0, 0)  13.1 us
    pallas_call x1, Pallas kernels, first_row_pass(): pl.pallas_call(functools.partial(row_pass_kernel, LOG2E / first_epsilon,...  12.7 us
    ppermute x8, waiting for transfers between devices, moved(): return lax.ppermute(value, 'col', pairs)  11.6 us
    ppermute x8, starting transfers between devices, moved(): return lax.ppermute(value, 'col', pairs)  9.43 us
    pallas_call x1, Pallas kernels, row_pass(): pl.pallas_call(functools.partial(row_pass_kernel, None, slots), out_shape...  6.79 us
  transfers between devices with their start and end apart: 8, of which 6 were waited for; matrix products, arithmetic and copies ran while one was open for 0% of the time, Pallas kernels for 0%

profile of v8, /device:TPU:0, one launch (start us, length us, event | category | flops | bytes accessed | tf_op | source)
XLA Modules:
  0.0 112.5 jit_solution(11794236707131686718)
XLA Ops:
  0.6 0.0 copy-start
  0.6 0.0 copy-start.1
  0.7 12.7 %row_pass_first.1 = (f32[128,128]{1,0:T(8,128)S(1)}, bf16[128,128,128]{2,1,0:T(8,128)(2,1)S(1)}, bf16[128,128,128]{2,1,0:T(8,128)(2,1)S(1)}, bf16[64,131072]{1,0...) custom-call(s32[4,128]{1,0:T(4,128)} %bitcast.12, ...), custom_call_target="tpu_custom_call" | custom-call | tf_op jit(solution)/shard_map/row_pass_first/pallas_call | solution.py:248
  13.3 0.1 collective-permute-start
  13.4 1.2 %collective-permute-done = f32[128,128]{1,0:T(8,128)S(1)} collective-permute-done((f32[128,128]{1,0:T(8,128)S(1)}, f32[128,128]{1,0:T(8,128)S(1)}, u32[]{:S(2)}, u32[]{:S(2)}) %collective-permute-start) | collective-permute-done | bytes 65568 | tf_op jit(solution)/shard_map/ppermute | solution.py:359
  14.7 4.2 %collective-permute-start.3 = (f32[128,128]{1,0:T(8,128)S(1)}, f32[128,128]{1,0:T(8,128)S(1)}, u32[]{:S(2)}, u32[]{:S(2)}) collective-permute-start(f32[128,128]{1,0:T(8,128)S(1)} %multiply_add_fusion.2), channel_id=1, source_target_pairs={{0,6},{1,7},{2,4},{3,5},{4,2},{5,3},{6,0},{7,1},{8,14},{9,15},{10,... | collective-permute-start | bytes 196616 | tf_op jit(solution)/shard_map/ppermute | solution.py:359
  18.9 0.0 collective-permute-start.2
  18.9 0.9 collective-permute-start.1
  19.9 2.2 %collective-permute-done.3 = f32[128,128]{1,0:T(8,128)S(1)} collective-permute-done((f32[128,128]{1,0:T(8,128)S(1)}, f32[128,128]{1,0:T(8,128)S(1)}, u32[]{:S(2)}, u32[]{:S(2)}) %collective-permute-start.3) | collective-permute-done | bytes 65568 | tf_op jit(solution)/shard_map/ppermute | solution.py:359
  22.0 3.0 %collective-permute-done.2 = f32[128,128]{1,0:T(8,128)S(1)} collective-permute-done((f32[128,128]{1,0:T(8,128)S(1)}, f32[128,128]{1,0:T(8,128)S(1)}, u32[]{:S(2)}, u32[]{:S(2)}) %collective-permute-start.2) | collective-permute-done | bytes 65568 | tf_op jit(solution)/shard_map/ppermute | solution.py:359
  25.0 0.0 collective-permute-done.1
  25.0 0.1 broadcast_multiply_fusion
  25.1 0.0 copy-done
  25.1 0.0 copy-done.1
  25.1 6.7 %col_pass.2 = f32[16,64,128]{2,1,0:T(8,128)S(1)} custom-call(s32[4,128]{1,0:T(4,128)S(1)} %bitcast.13, s32[128]{0:T(128)S(1)} %bitcast.17, bf16[128,128,128]{2,1,0:T(8,128)(2,1)S(1)} %get-tuple-element.38.refs_2_, bf16[64,131072]{1,0:T(8,128)(2,1)S(1)} %get-tuple-element.37.refs_3_, f32[128,128]{1,0:T(8,128)S(1)} %get-tuple-element.69.refs_4_, ...), custom_call_target="tpu_custom_call" | custom-call | tf_op jit(solution)/shard_map/col_pass/pallas_call | solution.py:297
  31.9 17.0 %all_to_all.20.refs_1_ = f32[16,64,128]{2,1,0:T(8,128)S(1)} all-to-all(f32[16,64,128]{2,1,0:T(8,128)S(1)} %col_pass.2), channel_id=1, replica_groups=mesh['row'=16,'col'=8] {'row'}, dimensions={0} | all-to-all | bytes 1048576 | tf_op jit(solution)/shard_map/all_to_all | solution.py:368
  48.8 0.1 combine.2
  49.0 13.1 %all_to_all.21 = f32[16,64,128]{2,1,0:T(8,128)S(1)} all-to-all(f32[16,64,128]{2,1,0:T(8,128)S(1)} %get-tuple-element.51), channel_id=1, replica_groups=mesh['row'=16,'col'=8] {'row'}, dimensions={0} | all-to-all | bytes 1048576 | tf_op jit(solution)/shard_map/all_to_all | solution.py:368
  62.1 6.8 %row_pass.1 = f32[144,128]{1,0:T(8,128)S(1)} custom-call(s32[4,128]{1,0:T(4,128)S(1)} %bitcast.14, s32[128]{0:T(128)S(1)} %bitcast.18, bf16[128,128,128]{2,1,0:T(8,128)(2,1)S(1)} %get-tuple-element.36.refs_2_, bf16[64,131072]{1,0:T(8,128)(2,1)S(1)} %get-tuple-element.37.refs_3_, f32[128,128]{1,0:T(8,128)S(1)} %get-tuple-element.54.refs_4_, ...), custom_call_target="tpu_custom_call" | custom-call | tf_op jit(solution)/shard_map/row_pass/pallas_call | solution.py:277
  68.9 0.0 collective-permute-start.4
  68.9 1.3 %collective-permute-done.4 = f32[144,128]{1,0:T(8,128)S(1)} collective-permute-done((f32[144,128]{1,0:T(8,128)S(1)}, f32[144,128]{1,0:T(8,128)S(1)}, u32[]{:S(2)}, u32[]{:S(2)}) %collective-permute-start.4) | collective-permute-done | bytes 73760 | tf_op jit(solution)/shard_map/ppermute | solution.py:359
  70.2 1.8 %collective-permute-start.7 = (f32[144,128]{1,0:T(8,128)S(1)}, f32[144,128]{1,0:T(8,128)S(1)}, u32[]{:S(2)}, u32[]{:S(2)}) collective-permute-start(f32[144,128]{1,0:T(8,128)S(1)} %multiply_add_fusion.1), channel_id=1, source_target_pairs={{0,6},{1,7},{2,4},{3,5},{4,2},{5,3},{6,0},{7,1},{8,14},{9,15},{10,... | collective-permute-start | bytes 221192 | tf_op jit(solution)/shard_map/ppermute | solution.py:359
  72.1 0.5 collective-permute-start.6
  72.5 1.9 %collective-permute-start.5 = (f32[144,128]{1,0:T(8,128)S(1)}, f32[144,128]{1,0:T(8,128)S(1)}, u32[]{:S(2)}, u32[]{:S(2)}) collective-permute-start(f32[144,128]{1,0:T(8,128)S(1)} %multiply_add_fusion.1), channel_id=1, source_target_pairs={{0,2},{1,3},{2,0},{3,1},{4,6},{5,7},{6,4},{7,5},{8,10},{9,11},{10,... | collective-permute-start | bytes 221192 | tf_op jit(solution)/shard_map/ppermute | solution.py:359
  74.4 1.5 %collective-permute-done.7 = f32[144,128]{1,0:T(8,128)S(1)} collective-permute-done((f32[144,128]{1,0:T(8,128)S(1)}, f32[144,128]{1,0:T(8,128)S(1)}, u32[]{:S(2)}, u32[]{:S(2)}) %collective-permute-start.7) | collective-permute-done | bytes 73760 | tf_op jit(solution)/shard_map/ppermute | solution.py:359
  75.9 2.5 %collective-permute-done.6 = f32[144,128]{1,0:T(8,128)S(1)} collective-permute-done((f32[144,128]{1,0:T(8,128)S(1)}, f32[144,128]{1,0:T(8,128)S(1)}, u32[]{:S(2)}, u32[]{:S(2)}) %collective-permute-start.6) | collective-permute-done | bytes 73760 | tf_op jit(solution)/shard_map/ppermute | solution.py:359
  78.4 0.0 collective-permute-done.5
  78.4 0.1 multiply_add_fusion
  78.5 6.8 %col_pass.3 = (f32[16,64,128]{2,1,0:T(8,128)S(1)}, f32[128,128]{1,0:T(8,128)}) custom-call(s32[4,128]{1,0:T(4,128)S(1)} %bitcast.15, s32[128]{0:T(128)S(1)} %bitcast.19, bf16[128,128,128]{2,1,0:T(8,128)(2,1)S(1)} %get-tuple-element.36.refs_2_, bf16[64,131072]{1,0:T(8,128)(2,1)S(1)} %get-tuple-element.37.refs_3_, f32[128,128]{1,0:T(8,128)S(1)} %fusion.2.refs_4_, ...), custom_call_target="tpu_custom_call" | custom-call | tf_op jit(solution)/shard_map/col_pass/pallas_call | solution.py:297
  85.3 13.1 %all_to_all.22.refs_1_ = f32[16,64,128]{2,1,0:T(8,128)S(1)} all-to-all(f32[16,64,128]{2,1,0:T(8,128)S(1)} %get-tuple-element.61), channel_id=1, replica_groups=mesh['row'=16,'col'=8] {'row'}, dimensions={0} | all-to-all | bytes 1048576 | tf_op jit(solution)/shard_map/all_to_all | solution.py:368
  98.4 0.1 combine.3
  98.5 13.1 %all_to_all.23 = f32[16,64,128]{2,1,0:T(8,128)S(1)} all-to-all(f32[16,64,128]{2,1,0:T(8,128)S(1)} %combine.3), channel_id=1, replica_groups=mesh['row'=16,'col'=8] {'row'}, dimensions={0} | all-to-all | bytes 1048576 | tf_op jit(solution)/shard_map/all_to_all | solution.py:415
  111.7 0.8 copy.9
  (4 shorter events, 0.1 us)
Async XLA Ops:
  0.6 24.5 %copy-start = (s32[128,1,4]{0,2,1:T(4,128)S(1)}, s32[128,1,4]{0,2,1:T(4,128)}, u32[]{:S(2)}) copy-start(s32[128,1,4]{0,2,1:T(4,128)} %param.10) | copy-start | bytes 6148
  0.6 24.5 %copy-start.1 = (s32[128,1]{0,1:T(1,128)S(1)}, s32[128,1]{0,1:T(1,128)}, u32[]{:S(2)}) copy-start(s32[128,1]{0,1:T(1,128)} %param.11) | copy-start | bytes 1540
  13.3 1.3 %collective-permute-start = (f32[128,128]{1,0:T(8,128)S(1)}, f32[128,128]{1,0:T(8,128)S(1)}, u32[]{:S(2)}, u32[]{:S(2)}) collective-permute-start(f32[128,128]{1,0:T(8,128)S(1)} %get-tuple-element.40), channel_id=1, source_target_pairs={{0,1},{1,0},{2,3},{3,2},{4,5},{5,4},{6,7},{7,6},{8,9},{9,8},{10,11... | collective-permute-start | bytes 196616 | tf_op jit(solution)/shard_map/ppermute | solution.py:359
  14.7 7.3 %collective-permute-start.3 = (f32[128,128]{1,0:T(8,128)S(1)}, f32[128,128]{1,0:T(8,128)S(1)}, u32[]{:S(2)}, u32[]{:S(2)}) collective-permute-start(f32[128,128]{1,0:T(8,128)S(1)} %multiply_add_fusion.2), channel_id=1, source_target_pairs={{0,6},{1,7},{2,4},{3,5},{4,2},{5,3},{6,0},{7,1},{8,14},{9,15},{10,... | collective-permute-start | bytes 196616 | tf_op jit(solution)/shard_map/ppermute | solution.py:359
  18.9 6.1 %collective-permute-start.2 = (f32[128,128]{1,0:T(8,128)S(1)}, f32[128,128]{1,0:T(8,128)S(1)}, u32[]{:S(2)}, u32[]{:S(2)}) collective-permute-start(f32[128,128]{1,0:T(8,128)S(1)} %multiply_add_fusion.2), channel_id=1, source_target_pairs={{0,4},{1,5},{2,6},{3,7},{4,0},{5,1},{6,2},{7,3},{8,12},{9,13},{10,... | collective-permute-start | bytes 196616 | tf_op jit(solution)/shard_map/ppermute | solution.py:359
  18.9 6.1 %collective-permute-start.1 = (f32[128,128]{1,0:T(8,128)S(1)}, f32[128,128]{1,0:T(8,128)S(1)}, u32[]{:S(2)}, u32[]{:S(2)}) collective-permute-start(f32[128,128]{1,0:T(8,128)S(1)} %multiply_add_fusion.2), channel_id=1, source_target_pairs={{0,2},{1,3},{2,0},{3,1},{4,6},{5,7},{6,4},{7,5},{8,10},{9,11},{10,... | collective-permute-start | bytes 196616 | tf_op jit(solution)/shard_map/ppermute | solution.py:359
  68.9 1.3 %collective-permute-start.4 = (f32[144,128]{1,0:T(8,128)S(1)}, f32[144,128]{1,0:T(8,128)S(1)}, u32[]{:S(2)}, u32[]{:S(2)}) collective-permute-start(f32[144,128]{1,0:T(8,128)S(1)} %row_pass.1), channel_id=1, source_target_pairs={{0,1},{1,0},{2,3},{3,2},{4,5},{5,4},{6,7},{7,6},{8,9},{9,8},{10,11... | collective-permute-start | bytes 221192 | tf_op jit(solution)/shard_map/ppermute | solution.py:359
  70.2 5.6 %collective-permute-start.7 = (f32[144,128]{1,0:T(8,128)S(1)}, f32[144,128]{1,0:T(8,128)S(1)}, u32[]{:S(2)}, u32[]{:S(2)}) collective-permute-start(f32[144,128]{1,0:T(8,128)S(1)} %multiply_add_fusion.1), channel_id=1, source_target_pairs={{0,6},{1,7},{2,4},{3,5},{4,2},{5,3},{6,0},{7,1},{8,14},{9,15},{10,... | collective-permute-start | bytes 221192 | tf_op jit(solution)/shard_map/ppermute | solution.py:359
  72.1 6.3 %collective-permute-start.6 = (f32[144,128]{1,0:T(8,128)S(1)}, f32[144,128]{1,0:T(8,128)S(1)}, u32[]{:S(2)}, u32[]{:S(2)}) collective-permute-start(f32[144,128]{1,0:T(8,128)S(1)} %multiply_add_fusion.1), channel_id=1, source_target_pairs={{0,4},{1,5},{2,6},{3,7},{4,0},{5,1},{6,2},{7,3},{8,12},{9,13},{10,... | collective-permute-start | bytes 221192 | tf_op jit(solution)/shard_map/ppermute | solution.py:359
  72.5 5.9 %collective-permute-start.5 = (f32[144,128]{1,0:T(8,128)S(1)}, f32[144,128]{1,0:T(8,128)S(1)}, u32[]{:S(2)}, u32[]{:S(2)}) collective-permute-start(f32[144,128]{1,0:T(8,128)S(1)} %multiply_add_fusion.1), channel_id=1, source_target_pairs={{0,2},{1,3},{2,0},{3,1},{4,6},{5,7},{6,4},{7,5},{8,10},{9,11},{10,... | collective-permute-start | bytes 221192 | tf_op jit(solution)/shard_map/ppermute | solution.py:359

commit v9 on v8

--- a/solution.py
+++ b/solution.py
@@ -15,8 +15,9 @@
 SMALLEST = 2.0**-100
 LARGEST = 2.0**120
 VMEM_LIMIT = 16 * 1024 * 1024
-ROW_UNROLL = 128
-COL_UNROLL = 64
+TAIL = 32
+ROW_UNROLL = 96
+COL_UNROLL = 48
 CHUNK = 64
 ROW_OFFSET = 64.0
 COL_OFFSET = 80.0
@@ -57,34 +58,51 @@
     ]
 
 
+def make_order(order, counts, blocks, slots):
+    def place(r, found):
+        full, half = found
+        is_full = counts[r] > slots // 2
+        order[jnp.where(is_full, full, blocks - 1 - half)] = r
+        return jnp.where(is_full, full + 1, full), jnp.where(is_full, half, half + 1)
+
+    order[blocks] = lax.fori_loop(0, blocks, place, (0, 0), unroll=4)[1]
+
+
+def over_rows(order, blocks, slots, unroll, visit):
+    short = order[blocks] >= TAIL
+
+    def run(first, last, width, unroll):
+        visit(first, last, unroll, lambda at: (order[at], width))
+
+    run(0, blocks - TAIL, slots, unroll)
+
+    @pl.when(short)
+    def _():
+        run(blocks - TAIL, blocks, slots // 2, TAIL)
+
+    @pl.when(jnp.logical_not(short))
+    def _():
+        run(blocks - TAIL, blocks, slots, 8)
+
+
 def log2_sum(values):
     summed = jnp.sum(jnp.sum(values, axis=0, keepdims=True), axis=1, keepdims=True)
     return jnp.broadcast_to(jnp.log2(summed), (8, TILE))
 
 
-def prepare(kappa, x_hbm, y_hbm, x_ref, x2_ref, y_ref, g_ref, hx_ref, x_in, x_sem, y_sem, others):
+def prepare(kappa, x_hbm, y_hbm, x_ref, x2_ref, y_ref, g_ref, hx_ref, x_in, x_sem, y_sem, others, then):
     width = y_ref.shape[0]
     blocks = hx_ref.shape[0]
     target_blocks = g_ref.shape[0]
     chunks = target_blocks // CHUNK
     x_copy = pltpu.make_async_copy(x_hbm, x_in, x_sem)
-    x_copy.start()
+    beside = blocks * 8 // target_blocks
 
     def y_copy(c):
         at = pl.ds(pl.multiple_of(c * (CHUNK * TILE), CHUNK * TILE), CHUNK * TILE)
         return pltpu.make_async_copy(y_hbm.at[:, at], y_ref.at[:, at], y_sem.at[c])
 
-    for other in others:
-        other.start()
-
-    @pl.loop(0, chunks)
-    def _(c):
-        y_copy(c).start()
-
-    x_copy.wait()
-
-    @pl.loop(0, blocks, unroll=4)
-    def _(r):
+    def source_block(r):
         xf = x_in[:, pl.ds(pl.multiple_of(r * TILE, TILE), TILE)].astype(jnp.float32)
         hx_ref[pl.ds(r, 1), :] = 0.5 * jnp.sum(xf * xf, axis=0, keepdims=True)
         scaled = xf * kappa
@@ -94,27 +112,40 @@
         x_ref[r] = turned
         x2_ref[r] = turned + turned
 
+    for other in others:
+        other.start()
+    x_copy.start()
+
+    @pl.loop(0, chunks)
+    def _(c):
+        y_copy(c).start()
+
+    for other in others:
+        other.wait()
+    then()
+    x_copy.wait()
+
     @pl.loop(0, chunks)
     def _(c):
         y_copy(c).wait()
 
-        @pl.loop(0, CHUNK // 8, unroll=2)
+        @pl.loop(0, CHUNK // 8, unroll=4)
         def _(q):
-            first = c * CHUNK + q * 8
-            at = pl.ds(pl.multiple_of(first * TILE, 8 * TILE), 8 * TILE)
+            group = c * (CHUNK // 8) + q
+            at = pl.ds(pl.multiple_of(group * (8 * TILE), 8 * TILE), 8 * TILE)
             yf = y_ref[:, at].astype(jnp.float32)
             half = (-0.5 * kappa) * jnp.sum(yf * yf, axis=0, keepdims=True)
             for k in range(8):
-                g_ref[pl.ds(first + k, 1), :] = half[:, k * TILE : (k + 1) * TILE]
-
-    for other in others:
-        other.wait()
+                g_ref[pl.ds(group * 8 + k, 1), :] = half[:, k * TILE : (k + 1) * TILE]
+            for k in range(beside):
+                source_block(group * beside + k)
 
 
 def row_pass_kernel(kappa, slots, *refs):
     if kappa is not None:
         (cols_hbm, counts_hbm, a_hbm, b_hbm, x_hbm, y_hbm, out_ref, x_ref, x2_ref,
-         y_ref, g_ref, hx_ref, a_ref, b_ref, mass_ref, total, x_in, cols, counts, sems, y_sem) = refs
+         y_ref, g_ref, hx_ref, a_ref, b_ref, mass_ref, order, total, x_in, cols, counts, sems,
+         y_sem) = refs
         f_ref = None
         small = ((a_hbm, a_ref), (b_hbm, b_ref), (cols_hbm, cols), (counts_hbm, counts))
         others = [
@@ -122,24 +153,28 @@
             for i, (source, target) in enumerate(small)
         ]
         prepare(kappa, x_hbm, y_hbm, x_ref, x2_ref, y_ref, g_ref, hx_ref, x_in, sems.at[0],
-                y_sem, others)
+                y_sem, others, lambda: make_order(order, counts, total.shape[1], slots))
         offset = 0.0
     else:
-        (cols, counts, x_ref, y_ref, f_ref, g_ref, g_first_ref, b_ref, mass_ref, out_ref,
+        (cols, counts, order, x_ref, y_ref, f_ref, g_ref, g_first_ref, b_ref, mass_ref, out_ref,
          total) = refs
         offset = ROW_OFFSET
     blocks = total.shape[1]
     lane = lax.broadcasted_iota(jnp.int32, (TILE, TILE), 1)
 
-    @pl.loop(0, blocks, unroll=ROW_UNROLL)
-    def _(r):
-        scores = products(x_ref, y_ref, f_ref, cols, slots, r, offset)
-        terms = None
-        for k, row in enumerate(shifts(cols, counts, g_ref, slots, r)):
-            term = jnp.exp2(scores[:, k * TILE : (k + 1) * TILE] + row)
-            terms = term if terms is None else terms + term
-        summed = jnp.sum(terms, axis=1, keepdims=True)
-        total[...] = jnp.where(lane == r, summed, total[...])
+    def visit(first, last, unroll, place):
+        @pl.loop(first, last, unroll=unroll)
+        def _(at):
+            r, width = place(at)
+            scores = products(x_ref, y_ref, f_ref, cols, width, r, offset)
+            terms = None
+            for k, row in enumerate(shifts(cols, counts, g_ref, width, r)):
+                term = jnp.exp2(scores[:, k * TILE : (k + 1) * TILE] + row)
+                terms = term if terms is None else terms + term
+            summed = jnp.sum(terms, axis=1, keepdims=True)
+            total[...] = jnp.where(lane == r, summed, total[...])
+
+    over_rows(order, blocks, slots, ROW_UNROLL, visit)
 
     sums = total[...]
     out_ref[:blocks, :] = (jnp.log2(sums) - offset).T
@@ -171,10 +206,10 @@
 
 def col_pass_kernel(slots, last, *refs):
     if last is None:
-        cols, counts, x_ref, y_ref, f_ref, g_ref, out_ref, total = refs
-    else:
-        (cols, counts, x_ref, y_ref, f_ref, g_ref, hx_ref, totals_ref, out_ref, source_hbm, total,
-         source, sem) = refs
+        cols, counts, order, x_ref, y_ref, f_ref, g_ref, out_ref, total, bounds = refs
+    else:
+        (cols, counts, order, x_ref, y_ref, f_ref, g_ref, hx_ref, totals_ref, out_ref, source_hbm,
+         total, bounds, source, sem) = refs
         second, first = last
         total_b, total_a = totals_ref[:1, :], totals_ref[8:9, :]
         shift = first * total_b - (second + first) * total_a
@@ -184,20 +219,29 @@
     blocks = f_ref.shape[0]
     total[...] = jnp.zeros_like(total)
 
-    def visit(r, carry):
-        least, most = carry
-        scores = products(x_ref, y_ref, f_ref, cols, slots, r, COL_OFFSET)
-        live = counts[r]
-        for k, row in enumerate(shifts(cols, counts, g_ref, slots, r)):
-            terms = jnp.exp2(scores[:, k * TILE : (k + 1) * TILE] + row)
-            summed = jnp.sum(terms, axis=0, keepdims=True)
-            total[pl.ds(cols[k, r], 1), :] += summed
-            least = jnp.minimum(least, jnp.where(k < live, summed, 1.0))
-            most = jnp.maximum(most, summed)
-        return least, most
-
-    ones = jnp.ones((1, TILE), jnp.float32)
-    least, most = lax.fori_loop(0, blocks, visit, (ones, ones), unroll=COL_UNROLL)
+    bounds[...] = jnp.ones_like(bounds)
+
+    def visit(first, last, unroll, place):
+        def one(at, carry):
+            least, most = carry
+            r, width = place(at)
+            scores = products(x_ref, y_ref, f_ref, cols, width, r, COL_OFFSET)
+            live = counts[r]
+            for k, row in enumerate(shifts(cols, counts, g_ref, width, r)):
+                terms = jnp.exp2(scores[:, k * TILE : (k + 1) * TILE] + row)
+                summed = jnp.sum(terms, axis=0, keepdims=True)
+                total[pl.ds(cols[k, r], 1), :] += summed
+                least = jnp.minimum(least, jnp.where(k < live, summed, 1.0))
+                most = jnp.maximum(most, summed)
+            return least, most
+
+        carry = (bounds[:1, :], bounds[1:2, :])
+        least, most = lax.fori_loop(first, last, one, carry, unroll=unroll)
+        bounds[:1, :] = least
+        bounds[1:2, :] = most
+
+    over_rows(order, blocks, slots, COL_UNROLL, visit)
+    least, most = bounds[:1, :], bounds[1:2, :]
     sums = total[...]
     result = jnp.where(sums > 0.0, jnp.log2(sums) - COL_OFFSET, very_negative)
     out_ref[...] = result.reshape(out_ref.shape)
@@ -257,9 +301,10 @@
             shape((blocks, TILE), f32),
             shape((target_blocks, TILE), f32),
             shape((8, TILE), f32),
+            shape((blocks + 1,), jnp.int32),
         ),
         in_specs=[ANY()] * 6,
-        out_specs=(VMEM(),) * 9,
+        out_specs=(VMEM(),) * 9 + (SMEM(),),
         scratch_shapes=[
             pltpu.VMEM((TILE, blocks), f32),
             pltpu.VMEM(source_points.shape, bf16),
@@ -273,22 +318,22 @@
     )(*in_hbm)
 
 
-def row_pass(cols, counts, x, y, f_pot, g_pot, g_first, log_b, mass, slots):
+def row_pass(lists, x, y, f_pot, g_pot, g_first, log_b, mass, slots):
     return pl.pallas_call(
         functools.partial(row_pass_kernel, None, slots),
         out_shape=jax.ShapeDtypeStruct((f_pot.shape[0] + 16, TILE), jnp.float32),
-        in_specs=[SMEM(), SMEM()] + [VMEM()] * 7,
+        in_specs=[SMEM()] * 3 + [VMEM()] * 7,
         out_specs=VMEM(),
         scratch_shapes=[pltpu.VMEM((TILE, f_pot.shape[0]), jnp.float32)],
         name="row_pass",
         compiler_params=pltpu.CompilerParams(vmem_limit_bytes=VMEM_LIMIT),
-    )(cols, counts, x, y, f_pot, g_pot, g_first, log_b, mass)
-
-
-def col_pass(cols, counts, x, y, f_pot, g_pot, slots, devices, last=None):
+    )(*lists, x, y, f_pot, g_pot, g_first, log_b, mass)
+
+
+def col_pass(lists, x, y, f_pot, g_pot, slots, devices, last=None):
     target_blocks = g_pot.shape[0]
     out = jax.ShapeDtypeStruct((devices, target_blocks // devices, TILE), jnp.float32)
-    scratch = [pltpu.VMEM((target_blocks, TILE), jnp.float32)]
+    scratch = [pltpu.VMEM((target_blocks, TILE), jnp.float32), pltpu.VMEM((8, TILE), jnp.float32)]
     more, scales, out_specs = (), None, VMEM()
     if last is not None:
         more, scales = last[:2], last[2:]
@@ -297,12 +342,12 @@
     return pl.pallas_call(
         functools.partial(col_pass_kernel, slots, scales),
         out_shape=out,
-        in_specs=[SMEM(), SMEM()] + [VMEM()] * (4 + len(more)),
+        in_specs=[SMEM()] * 3 + [VMEM()] * (4 + len(more)),
         out_specs=out_specs,
         scratch_shapes=scratch,
         name="col_pass",
         compiler_params=pltpu.CompilerParams(vmem_limit_bytes=VMEM_LIMIT),
-    )(cols, counts, x, y, f_pot, g_pot, *more)
+    )(*lists, x, y, f_pot, g_pot, *more)
 
 
 def combine_kernel(epsilon, both_eps, *refs):
@@ -384,7 +429,7 @@
     first_own = (lax.axis_index("row") * own_blocks).reshape(1)
     counts, first_own = lax.optimization_barrier((counts, first_own))
 
-    part, x1, x2, y, g_first, half_x, log_a, log_b, mass = first_row_pass(
+    part, x1, x2, y, g_first, half_x, log_a, log_b, mass, order = first_row_pass(
         cols,
         counts,
         mass_a,
@@ -393,22 +438,23 @@
         target_points,
         slots,
     )
+    lists = (cols, counts, order)
     x1, x2, y = (pltpu.with_memory_space_constraint(v, pltpu.VMEM) for v in (x1, x2, y))
 
     f_pot = log_a - over_cols(part, col_devices)
-    part = col_pass(cols, counts, x1, y, f_pot, g_first, slots, row_devices)
+    part = col_pass(lists, x1, y, f_pot, g_first, slots, row_devices)
     stack, (f_pot, first_own) = exchange(part, (2.0 * f_pot, first_own))
     send, g_own = combine(first_own, stack, log_b, g_first, None)
     g_pot, (f_pot, first_own) = exchange(send, (f_pot, first_own))
     g_pot = g_pot.reshape(target_blocks, TILE)
 
     first, second = first_epsilon, 0.5 * first_epsilon
-    part = row_pass(cols, counts, x2, y, f_pot, g_pot, g_first, log_b, mass, slots)
+    part = row_pass(lists, x2, y, f_pot, g_pot, g_first, log_b, mass, slots)
     both = over_cols(part, col_devices)
     part, totals = both[:row_blocks], both[row_blocks:]
     f_pot = f_pot + (log_a - part)
     part, source = col_pass(
-        cols, counts, x2, y, f_pot, g_pot, slots, row_devices, (half_x, totals, second, first)
+        lists, x2, y, f_pot, g_pot, slots, row_devices, (half_x, totals, second, first)
     )
     stack, (totals, first_own) = exchange(part, (totals, first_own))
     send = combine(first_own, stack, log_b, g_own, (g_first, totals, second, first + second))

time: 113 us -> 112 us (level)
  Pallas kernels: 33.2 us -> 32 us
where the time goes in v9:
time: 112 us; the launch traced here: 111 us
  blocking collectives  56.3 us (50%)
  Pallas kernels  32 us (29%)
  waiting for transfers between devices  11.6 us (10%)
  starting transfers between devices  9.51 us (8%)
    all_to_all x3, blocking collectives, exchange(): return lax.optimization_barrier((lax.all_to_all(blocks, 'row', 0, 0), rest))  43.2 us
    all_to_all x1, blocking collectives, body(): target = lax.all_to_all(send, 'row', 0, 0)  13.1 us
    pallas_call x1, Pallas kernels, first_row_pass(): pl.pallas_call(functools.partial(row_pass_kernel, LOG2E / first_epsilon,...  12.8 us
    pallas_call x2, Pallas kernels, col_pass(): pl.pallas_call(functools.partial(col_pass_kernel, slots, scales), out_sha...  12.5 us
    ppermute x8, waiting for transfers between devices, moved(): return lax.ppermute(value, 'col', pairs)  11.6 us
    ppermute x8, starting transfers between devices, moved(): return lax.ppermute(value, 'col', pairs)  9.51 us
    pallas_call x1, Pallas kernels, row_pass(): pl.pallas_call(functools.partial(row_pass_kernel, None, slots), out_shape...  6.43 us
  transfers between devices with their start and end apart: 8, of which 6 were waited for; matrix products, arithmetic and copies ran while one was open for 0% of the time, Pallas kernels for 0%

profile of v9, /device:TPU:0, one launch (start us, length us, event | category | flops | bytes accessed | tf_op | source)
XLA Modules:
  0.0 111.3 jit_solution(12607272088080805669)
XLA Ops:
  0.6 0.0 copy-start
  0.6 0.0 copy-start.1
  0.7 12.8 %row_pass_first.1 = (f32[128,128]{1,0:T(8,128)S(1)}, bf16[128,128,128]{2,1,0:T(8,128)(2,1)S(1)}, bf16[128,128,128]{2,1,0:T(8,128)(2,1)S(1)}, bf16[64,131072]{1,0...) custom-call(s32[4,128]{1,0:T(4,128)} %bitcast.12, ...), custom_call_target="tpu_custom_call" | custom-call | tf_op jit(solution)/shard_map/row_pass_first/pallas_call | solution.py:292
  13.5 0.1 collective-permute-start
  13.6 1.2 %collective-permute-done = f32[128,128]{1,0:T(8,128)S(1)} collective-permute-done((f32[128,128]{1,0:T(8,128)S(1)}, f32[128,128]{1,0:T(8,128)S(1)}, u32[]{:S(2)}, u32[]{:S(2)}) %collective-permute-start) | collective-permute-done | bytes 65568 | tf_op jit(solution)/shard_map/ppermute | solution.py:404
  14.9 4.2 %collective-permute-start.3 = (f32[128,128]{1,0:T(8,128)S(1)}, f32[128,128]{1,0:T(8,128)S(1)}, u32[]{:S(2)}, u32[]{:S(2)}) collective-permute-start(f32[128,128]{1,0:T(8,128)S(1)} %multiply_add_fusion.2), channel_id=1, source_target_pairs={{0,6},{1,7},{2,4},{3,5},{4,2},{5,3},{6,0},{7,1},{8,14},{9,15},{10,... | collective-permute-start | bytes 196616 | tf_op jit(solution)/shard_map/ppermute | solution.py:404
  19.1 0.0 collective-permute-start.2
  19.1 0.9 collective-permute-start.1
  20.0 2.2 %collective-permute-done.3 = f32[128,128]{1,0:T(8,128)S(1)} collective-permute-done((f32[128,128]{1,0:T(8,128)S(1)}, f32[128,128]{1,0:T(8,128)S(1)}, u32[]{:S(2)}, u32[]{:S(2)}) %collective-permute-start.3) | collective-permute-done | bytes 65568 | tf_op jit(solution)/shard_map/ppermute | solution.py:404
  22.2 3.0 %collective-permute-done.2 = f32[128,128]{1,0:T(8,128)S(1)} collective-permute-done((f32[128,128]{1,0:T(8,128)S(1)}, f32[128,128]{1,0:T(8,128)S(1)}, u32[]{:S(2)}, u32[]{:S(2)}) %collective-permute-start.2) | collective-permute-done | bytes 65568 | tf_op jit(solution)/shard_map/ppermute | solution.py:404
  25.2 0.0 collective-permute-done.1
  25.2 0.1 broadcast_multiply_fusion
  25.2 0.0 copy-done
  25.2 0.0 copy-done.1
  25.3 6.2 %col_pass.2 = f32[16,64,128]{2,1,0:T(8,128)S(1)} custom-call(s32[4,128]{1,0:T(4,128)S(1)} %bitcast.13, s32[128]{0:T(128)S(1)} %bitcast.17, s32[129]{0:T(256)S(1)} %get-tuple-element.37.refs_2_, bf16[128,128,128]{2,1,0:T(8,128)(2,1)S(1)} %get-tuple-element.40.refs_3_, bf16[64,131072]{1,0:T(8,128)(2,1)S(1)} %get-tuple-element.39.refs_4_, ...), custom_call_target="tpu_custom_call" | custom-call | tf_op jit(solution)/shard_map/col_pass/pallas_call | solution.py:342
  31.5 16.9 %all_to_all.20.refs_1_ = f32[16,64,128]{2,1,0:T(8,128)S(1)} all-to-all(f32[16,64,128]{2,1,0:T(8,128)S(1)} %col_pass.2), channel_id=1, replica_groups=mesh['row'=16,'col'=8] {'row'}, dimensions={0} | all-to-all | bytes 1048576 | tf_op jit(solution)/shard_map/all_to_all | solution.py:413
  48.4 0.1 combine.2
  48.6 13.1 %all_to_all.21 = f32[16,64,128]{2,1,0:T(8,128)S(1)} all-to-all(f32[16,64,128]{2,1,0:T(8,128)S(1)} %get-tuple-element.53), channel_id=1, replica_groups=mesh['row'=16,'col'=8] {'row'}, dimensions={0} | all-to-all | bytes 1048576 | tf_op jit(solution)/shard_map/all_to_all | solution.py:413
  61.7 6.4 %row_pass.1 = f32[144,128]{1,0:T(8,128)S(1)} custom-call(s32[4,128]{1,0:T(4,128)S(1)} %bitcast.14, s32[128]{0:T(128)S(1)} %bitcast.18, s32[129]{0:T(256)S(1)} %get-tuple-element.37.refs_2_, bf16[128,128,128]{2,1,0:T(8,128)(2,1)S(1)} %get-tuple-element.38.refs_3_, bf16[64,131072]{1,0:T(8,128)(2,1)S(1)} %get-tuple-element.39.refs_4_, ...), custom_call_target="tpu_custom_call" | custom-call | tf_op jit(solution)/shard_map/row_pass/pallas_call | solution.py:322
  68.2 0.1 collective-permute-start.4
  68.2 1.3 %collective-permute-done.4 = f32[144,128]{1,0:T(8,128)S(1)} collective-permute-done((f32[144,128]{1,0:T(8,128)S(1)}, f32[144,128]{1,0:T(8,128)S(1)}, u32[]{:S(2)}, u32[]{:S(2)}) %collective-permute-start.4) | collective-permute-done | bytes 73760 | tf_op jit(solution)/shard_map/ppermute | solution.py:404
  69.6 1.9 %collective-permute-start.7 = (f32[144,128]{1,0:T(8,128)S(1)}, f32[144,128]{1,0:T(8,128)S(1)}, u32[]{:S(2)}, u32[]{:S(2)}) collective-permute-start(f32[144,128]{1,0:T(8,128)S(1)} %multiply_add_fusion.1), channel_id=1, source_target_pairs={{0,6},{1,7},{2,4},{3,5},{4,2},{5,3},{6,0},{7,1},{8,14},{9,15},{10,... | collective-permute-start | bytes 221192 | tf_op jit(solution)/shard_map/ppermute | solution.py:404
  71.4 0.4 collective-permute-start.6
  71.8 1.9 %collective-permute-start.5 = (f32[144,128]{1,0:T(8,128)S(1)}, f32[144,128]{1,0:T(8,128)S(1)}, u32[]{:S(2)}, u32[]{:S(2)}) collective-permute-start(f32[144,128]{1,0:T(8,128)S(1)} %multiply_add_fusion.1), channel_id=1, source_target_pairs={{0,2},{1,3},{2,0},{3,1},{4,6},{5,7},{6,4},{7,5},{8,10},{9,11},{10,... | collective-permute-start | bytes 221192 | tf_op jit(solution)/shard_map/ppermute | solution.py:404
  73.7 1.5 %collective-permute-done.7 = f32[144,128]{1,0:T(8,128)S(1)} collective-permute-done((f32[144,128]{1,0:T(8,128)S(1)}, f32[144,128]{1,0:T(8,128)S(1)}, u32[]{:S(2)}, u32[]{:S(2)}) %collective-permute-start.7) | collective-permute-done | bytes 73760 | tf_op jit(solution)/shard_map/ppermute | solution.py:404
  75.2 2.6 %collective-permute-done.6 = f32[144,128]{1,0:T(8,128)S(1)} collective-permute-done((f32[144,128]{1,0:T(8,128)S(1)}, f32[144,128]{1,0:T(8,128)S(1)}, u32[]{:S(2)}, u32[]{:S(2)}) %collective-permute-start.6) | collective-permute-done | bytes 73760 | tf_op jit(solution)/shard_map/ppermute | solution.py:404
  77.7 0.0 collective-permute-done.5
  77.8 0.1 multiply_add_fusion
  77.9 6.2 %col_pass.3 = (f32[16,64,128]{2,1,0:T(8,128)S(1)}, f32[128,128]{1,0:T(8,128)}) custom-call(s32[4,128]{1,0:T(4,128)S(1)} %bitcast.15, s32[128]{0:T(128)S(1)} %bitcast.19, s32[129]{0:T(256)S(1)} %get-tuple-element.37.refs_2_, bf16[128,128,128]{2,1,0:T(8,128)(2,1)S(1)} %get-tuple-element.38.refs_3_, bf16[64,131072]{1,0:T(8,128)(2,1)S(1)} %get-tuple-element.39.refs_4_, ...), custom_call_target="tpu_custom_call" | custom-call | tf_op jit(solution)/shard_map/col_pass/pallas_call | solution.py:342
  84.1 13.1 %all_to_all.22.refs_1_ = f32[16,64,128]{2,1,0:T(8,128)S(1)} all-to-all(f32[16,64,128]{2,1,0:T(8,128)S(1)} %get-tuple-element.63), channel_id=1, replica_groups=mesh['row'=16,'col'=8] {'row'}, dimensions={0} | all-to-all | bytes 1048576 | tf_op jit(solution)/shard_map/all_to_all | solution.py:413
  97.2 0.1 combine.3
  97.3 13.1 %all_to_all.23 = f32[16,64,128]{2,1,0:T(8,128)S(1)} all-to-all(f32[16,64,128]{2,1,0:T(8,128)S(1)} %combine.3), channel_id=1, replica_groups=mesh['row'=16,'col'=8] {'row'}, dimensions={0} | all-to-all | bytes 1048576 | tf_op jit(solution)/shard_map/all_to_all | solution.py:461
  110.5 0.8 copy.9
  (4 shorter events, 0.1 us)
Async XLA Ops:
  0.6 24.6 %copy-start = (s32[128,1,4]{0,2,1:T(4,128)S(1)}, s32[128,1,4]{0,2,1:T(4,128)}, u32[]{:S(2)}) copy-start(s32[128,1,4]{0,2,1:T(4,128)} %param.10) | copy-start | bytes 6148
  0.6 24.6 %copy-start.1 = (s32[128,1]{0,1:T(1,128)S(1)}, s32[128,1]{0,1:T(1,128)}, u32[]{:S(2)}) copy-start(s32[128,1]{0,1:T(1,128)} %param.11) | copy-start | bytes 1540
  13.5 1.3 %collective-permute-start = (f32[128,128]{1,0:T(8,128)S(1)}, f32[128,128]{1,0:T(8,128)S(1)}, u32[]{:S(2)}, u32[]{:S(2)}) collective-permute-start(f32[128,128]{1,0:T(8,128)S(1)} %get-tuple-element.42), channel_id=1, source_target_pairs={{0,1},{1,0},{2,3},{3,2},{4,5},{5,4},{6,7},{7,6},{8,9},{9,8},{10,11... | collective-permute-start | bytes 196616 | tf_op jit(solution)/shard_map/ppermute | solution.py:404
  14.9 7.3 %collective-permute-start.3 = (f32[128,128]{1,0:T(8,128)S(1)}, f32[128,128]{1,0:T(8,128)S(1)}, u32[]{:S(2)}, u32[]{:S(2)}) collective-permute-start(f32[128,128]{1,0:T(8,128)S(1)} %multiply_add_fusion.2), channel_id=1, source_target_pairs={{0,6},{1,7},{2,4},{3,5},{4,2},{5,3},{6,0},{7,1},{8,14},{9,15},{10,... | collective-permute-start | bytes 196616 | tf_op jit(solution)/shard_map/ppermute | solution.py:404
  19.1 6.1 %collective-permute-start.2 = (f32[128,128]{1,0:T(8,128)S(1)}, f32[128,128]{1,0:T(8,128)S(1)}, u32[]{:S(2)}, u32[]{:S(2)}) collective-permute-start(f32[128,128]{1,0:T(8,128)S(1)} %multiply_add_fusion.2), channel_id=1, source_target_pairs={{0,4},{1,5},{2,6},{3,7},{4,0},{5,1},{6,2},{7,3},{8,12},{9,13},{10,... | collective-permute-start | bytes 196616 | tf_op jit(solution)/shard_map/ppermute | solution.py:404
  19.1 6.1 %collective-permute-start.1 = (f32[128,128]{1,0:T(8,128)S(1)}, f32[128,128]{1,0:T(8,128)S(1)}, u32[]{:S(2)}, u32[]{:S(2)}) collective-permute-start(f32[128,128]{1,0:T(8,128)S(1)} %multiply_add_fusion.2), channel_id=1, source_target_pairs={{0,2},{1,3},{2,0},{3,1},{4,6},{5,7},{6,4},{7,5},{8,10},{9,11},{10,... | collective-permute-start | bytes 196616 | tf_op jit(solution)/shard_map/ppermute | solution.py:404
  68.2 1.3 %collective-permute-start.4 = (f32[144,128]{1,0:T(8,128)S(1)}, f32[144,128]{1,0:T(8,128)S(1)}, u32[]{:S(2)}, u32[]{:S(2)}) collective-permute-start(f32[144,128]{1,0:T(8,128)S(1)} %row_pass.1), channel_id=1, source_target_pairs={{0,1},{1,0},{2,3},{3,2},{4,5},{5,4},{6,7},{7,6},{8,9},{9,8},{10,11... | collective-permute-start | bytes 221192 | tf_op jit(solution)/shard_map/ppermute | solution.py:404
  69.6 5.6 %collective-permute-start.7 = (f32[144,128]{1,0:T(8,128)S(1)}, f32[144,128]{1,0:T(8,128)S(1)}, u32[]{:S(2)}, u32[]{:S(2)}) collective-permute-start(f32[144,128]{1,0:T(8,128)S(1)} %multiply_add_fusion.1), channel_id=1, source_target_pairs={{0,6},{1,7},{2,4},{3,5},{4,2},{5,3},{6,0},{7,1},{8,14},{9,15},{10,... | collective-permute-start | bytes 221192 | tf_op jit(solution)/shard_map/ppermute | solution.py:404
  71.4 6.3 %collective-permute-start.6 = (f32[144,128]{1,0:T(8,128)S(1)}, f32[144,128]{1,0:T(8,128)S(1)}, u32[]{:S(2)}, u32[]{:S(2)}) collective-permute-start(f32[144,128]{1,0:T(8,128)S(1)} %multiply_add_fusion.1), channel_id=1, source_target_pairs={{0,4},{1,5},{2,6},{3,7},{4,0},{5,1},{6,2},{7,3},{8,12},{9,13},{10,... | collective-permute-start | bytes 221192 | tf_op jit(solution)/shard_map/ppermute | solution.py:404
  71.8 5.9 %collective-permute-start.5 = (f32[144,128]{1,0:T(8,128)S(1)}, f32[144,128]{1,0:T(8,128)S(1)}, u32[]{:S(2)}, u32[]{:S(2)}) collective-permute-start(f32[144,128]{1,0:T(8,128)S(1)} %multiply_add_fusion.1), channel_id=1, source_target_pairs={{0,2},{1,3},{2,0},{3,1},{4,6},{5,7},{6,4},{7,5},{8,10},{9,11},{10,... | collective-permute-start | bytes 221192 | tf_op jit(solution)/shard_map/ppermute | solution.py:404

commit v10 on v9

--- a/solution.py
+++ b/solution.py
@@ -15,9 +15,9 @@
 SMALLEST = 2.0**-100
 LARGEST = 2.0**120
 VMEM_LIMIT = 16 * 1024 * 1024
-TAIL = 32
-ROW_UNROLL = 96
-COL_UNROLL = 48
+LESS = 56
+HALF = 32
+UNROLL = 8
 CHUNK = 64
 ROW_OFFSET = 64.0
 COL_OFFSET = 80.0
@@ -59,30 +59,46 @@
 
 
 def make_order(order, counts, blocks, slots):
+    def count(r, found):
+        return found + jnp.where(counts[r] == slots, 1, 0)
+
+    whole = lax.fori_loop(0, blocks, count, 0, unroll=8)
+
     def place(r, found):
-        full, half = found
-        is_full = counts[r] > slots // 2
-        order[jnp.where(is_full, full, blocks - 1 - half)] = r
-        return jnp.where(is_full, full + 1, full), jnp.where(is_full, half, half + 1)
-
-    order[blocks] = lax.fori_loop(0, blocks, place, (0, 0), unroll=4)[1]
-
-
-def over_rows(order, blocks, slots, unroll, visit):
-    short = order[blocks] >= TAIL
-
-    def run(first, last, width, unroll):
-        visit(first, last, unroll, lambda at: (order[at], width))
-
-    run(0, blocks - TAIL, slots, unroll)
+        full, less, half = found
+        is_full, is_half = counts[r] == slots, counts[r] <= slots // 2
+        at = jnp.where(is_full, full, jnp.where(is_half, blocks - 1 - half, less))
+        order[at] = r
+        one = jnp.where(is_half, 0, 1)
+        return (
+            full + jnp.where(is_full, 1, 0),
+            less + jnp.where(is_full, 0, one),
+            half + 1 - one,
+        )
+
+    half = lax.fori_loop(0, blocks, place, (0, whole, 0), unroll=4)[2]
+    short = jnp.logical_and(blocks - whole >= LESS, half >= HALF)
+    order[blocks] = jnp.where(short, 1, 0)
+
+
+def over_rows(order, blocks, slots, visit, load, store):
+    short = order[blocks] == 1
 
     @pl.when(short)
     def _():
-        run(blocks - TAIL, blocks, slots // 2, TAIL)
+        carry = load()
+        for at in range(blocks):
+            width = slots if at < blocks - LESS else slots - 1
+            width = width if at < blocks - HALF else slots // 2
+            carry = visit(order[at], width, carry)
+        store(carry)
 
     @pl.when(jnp.logical_not(short))
     def _():
-        run(blocks - TAIL, blocks, slots, 8)
+        def one(at, carry):
+            return visit(order[at], slots, carry)
+
+        store(lax.fori_loop(0, blocks, one, load(), unroll=UNROLL))
 
 
 def log2_sum(values):
@@ -90,7 +106,7 @@
     return jnp.broadcast_to(jnp.log2(summed), (8, TILE))
 
 
-def prepare(kappa, x_hbm, y_hbm, x_ref, x2_ref, y_ref, g_ref, hx_ref, x_in, x_sem, y_sem, others, then):
+def prepare(kappa, x_hbm, y_hbm, x_ref, x2_ref, y_ref, g_ref, hx_ref, x_in, x_sem, y_sem, others, masses, then):
     width = y_ref.shape[0]
     blocks = hx_ref.shape[0]
     target_blocks = g_ref.shape[0]
@@ -120,6 +136,8 @@
     def _(c):
         y_copy(c).start()
 
+    for other in masses:
+        other.start()
     for other in others:
         other.wait()
     then()
@@ -147,13 +165,14 @@
          y_ref, g_ref, hx_ref, a_ref, b_ref, mass_ref, order, total, x_in, cols, counts, sems,
          y_sem) = refs
         f_ref = None
-        small = ((a_hbm, a_ref), (b_hbm, b_ref), (cols_hbm, cols), (counts_hbm, counts))
-        others = [
+        small = ((cols_hbm, cols), (counts_hbm, counts), (a_hbm, a_ref), (b_hbm, b_ref))
+        copies = [
             pltpu.make_async_copy(source, target, sems.at[1 + i])
             for i, (source, target) in enumerate(small)
         ]
+        others, masses = copies[:2], copies[2:]
         prepare(kappa, x_hbm, y_hbm, x_ref, x2_ref, y_ref, g_ref, hx_ref, x_in, sems.at[0],
-                y_sem, others, lambda: make_order(order, counts, total.shape[1], slots))
+                y_sem, others, masses, lambda: make_order(order, counts, total.shape[1], slots))
         offset = 0.0
     else:
         (cols, counts, order, x_ref, y_ref, f_ref, g_ref, g_first_ref, b_ref, mass_ref, out_ref,
@@ -162,23 +181,23 @@
     blocks = total.shape[1]
     lane = lax.broadcasted_iota(jnp.int32, (TILE, TILE), 1)
 
-    def visit(first, last, unroll, place):
-        @pl.loop(first, last, unroll=unroll)
-        def _(at):
-            r, width = place(at)
-            scores = products(x_ref, y_ref, f_ref, cols, width, r, offset)
-            terms = None
-            for k, row in enumerate(shifts(cols, counts, g_ref, width, r)):
-                term = jnp.exp2(scores[:, k * TILE : (k + 1) * TILE] + row)
-                terms = term if terms is None else terms + term
-            summed = jnp.sum(terms, axis=1, keepdims=True)
-            total[...] = jnp.where(lane == r, summed, total[...])
-
-    over_rows(order, blocks, slots, ROW_UNROLL, visit)
+    def visit(r, width, carry):
+        scores = products(x_ref, y_ref, f_ref, cols, width, r, offset)
+        terms = None
+        for k, row in enumerate(shifts(cols, counts, g_ref, width, r)):
+            term = jnp.exp2(scores[:, k * TILE : (k + 1) * TILE] + row)
+            terms = term if terms is None else terms + term
+        summed = jnp.sum(terms, axis=1, keepdims=True)
+        total[...] = jnp.where(lane == r, summed, total[...])
+        return carry
+
+    over_rows(order, blocks, slots, visit, lambda: 0, lambda carry: None)
 
     sums = total[...]
     out_ref[:blocks, :] = (jnp.log2(sums) - offset).T
     if kappa is not None:
+        for other in masses:
+            other.wait()
         mass_ref[...] = log2_sum(b_ref[...])
         a_ref[...] = jnp.log2(a_ref[...])
         b_ref[...] = jnp.log2(b_ref[...])
@@ -221,26 +240,25 @@
 
     bounds[...] = jnp.ones_like(bounds)
 
-    def visit(first, last, unroll, place):
-        def one(at, carry):
-            least, most = carry
-            r, width = place(at)
-            scores = products(x_ref, y_ref, f_ref, cols, width, r, COL_OFFSET)
-            live = counts[r]
-            for k, row in enumerate(shifts(cols, counts, g_ref, width, r)):
-                terms = jnp.exp2(scores[:, k * TILE : (k + 1) * TILE] + row)
-                summed = jnp.sum(terms, axis=0, keepdims=True)
-                total[pl.ds(cols[k, r], 1), :] += summed
-                least = jnp.minimum(least, jnp.where(k < live, summed, 1.0))
-                most = jnp.maximum(most, summed)
-            return least, most
-
-        carry = (bounds[:1, :], bounds[1:2, :])
-        least, most = lax.fori_loop(first, last, one, carry, unroll=unroll)
-        bounds[:1, :] = least
-        bounds[1:2, :] = most
-
-    over_rows(order, blocks, slots, COL_UNROLL, visit)
+    def visit(r, width, carry):
+        least, most = carry
+        scores = products(x_ref, y_ref, f_ref, cols, width, r, COL_OFFSET)
+        live = counts[r]
+        for k, row in enumerate(shifts(cols, counts, g_ref, width, r)):
+            terms = jnp.exp2(scores[:, k * TILE : (k + 1) * TILE] + row)
+            summed = jnp.sum(terms, axis=0, keepdims=True)
+            total[pl.ds(cols[k, r], 1), :] += summed
+            least = jnp.minimum(least, jnp.where(k < live, summed, 1.0))
+            most = jnp.maximum(most, summed)
+        return least, most
+
+    def load():
+        return bounds[:1, :], bounds[1:2, :]
+
+    def store(carry):
+        bounds[:1, :], bounds[1:2, :] = carry
+
+    over_rows(order, blocks, slots, visit, load, store)
     least, most = bounds[:1, :], bounds[1:2, :]
     sums = total[...]
     result = jnp.where(sums > 0.0, jnp.log2(sums) - COL_OFFSET, very_negative)

time: 112 us -> 110 us (0.982)
  Pallas kernels: 32 us -> 30.4 us
where the time goes in v10:
time: 110 us
  blocking collectives  56.3 us (51%)
  Pallas kernels  30.4 us (28%)
  waiting for transfers between devices  11.7 us (11%)
  starting transfers between devices  9.49 us (9%)
    all_to_all x3, blocking collectives, exchange(): return lax.optimization_barrier((lax.all_to_all(blocks, 'row', 0, 0), rest))  43.2 us
    all_to_all x1, blocking collectives, body(): target = lax.all_to_all(send, 'row', 0, 0)  13.1 us
    pallas_call x1, Pallas kernels, first_row_pass(): pl.pallas_call(functools.partial(row_pass_kernel, LOG2E / first_epsilon,...  12.3 us
    pallas_call x2, Pallas kernels, col_pass(): pl.pallas_call(functools.partial(col_pass_kernel, slots, scales), out_sha...  11.7 us
    ppermute x8, waiting for transfers between devices, moved(): return lax.ppermute(value, 'col', pairs)  11.7 us
    ppermute x8, starting transfers between devices, moved(): return lax.ppermute(value, 'col', pairs)  9.49 us
    pallas_call x1, Pallas kernels, row_pass(): pl.pallas_call(functools.partial(row_pass_kernel, None, slots), out_shape...  6.11 us
  transfers between devices with their start and end apart: 8, of which 6 were waited for; matrix products, arithmetic and copies ran while one was open for 0% of the time, Pallas kernels for 0%

profile of v10, /device:TPU:0, one launch (start us, length us, event | category | flops | bytes accessed | tf_op | source)
XLA Modules:
  0.0 109.7 jit_solution(10348912972090653662)
XLA Ops:
  0.6 0.0 copy-start
  0.6 0.0 copy-start.1
  0.7 12.3 %row_pass_first.1 = (f32[128,128]{1,0:T(8,128)S(1)}, bf16[128,128,128]{2,1,0:T(8,128)(2,1)S(1)}, bf16[128,128,128]{2,1,0:T(8,128)(2,1)S(1)}, bf16[64,131072]{1,0...) custom-call(s32[4,128]{1,0:T(4,128)} %bitcast.12, ...), custom_call_target="tpu_custom_call" | custom-call | tf_op jit(solution)/shard_map/row_pass_first/pallas_call | solution.py:310
  13.0 0.1 collective-permute-start
  13.0 1.2 %collective-permute-done = f32[128,128]{1,0:T(8,128)S(1)} collective-permute-done((f32[128,128]{1,0:T(8,128)S(1)}, f32[128,128]{1,0:T(8,128)S(1)}, u32[]{:S(2)}, u32[]{:S(2)}) %collective-permute-start) | collective-permute-done | bytes 65568 | tf_op jit(solution)/shard_map/ppermute | solution.py:422
  14.3 4.2 %collective-permute-start.3 = (f32[128,128]{1,0:T(8,128)S(1)}, f32[128,128]{1,0:T(8,128)S(1)}, u32[]{:S(2)}, u32[]{:S(2)}) collective-permute-start(f32[128,128]{1,0:T(8,128)S(1)} %multiply_add_fusion.2), channel_id=1, source_target_pairs={{0,6},{1,7},{2,4},{3,5},{4,2},{5,3},{6,0},{7,1},{8,14},{9,15},{10,... | collective-permute-start | bytes 196616 | tf_op jit(solution)/shard_map/ppermute | solution.py:422
  18.5 0.0 collective-permute-start.2
  18.5 0.9 collective-permute-start.1
  19.5 2.2 %collective-permute-done.3 = f32[128,128]{1,0:T(8,128)S(1)} collective-permute-done((f32[128,128]{1,0:T(8,128)S(1)}, f32[128,128]{1,0:T(8,128)S(1)}, u32[]{:S(2)}, u32[]{:S(2)}) %collective-permute-start.3) | collective-permute-done | bytes 65568 | tf_op jit(solution)/shard_map/ppermute | solution.py:422
  21.6 3.0 %collective-permute-done.2 = f32[128,128]{1,0:T(8,128)S(1)} collective-permute-done((f32[128,128]{1,0:T(8,128)S(1)}, f32[128,128]{1,0:T(8,128)S(1)}, u32[]{:S(2)}, u32[]{:S(2)}) %collective-permute-start.2) | collective-permute-done | bytes 65568 | tf_op jit(solution)/shard_map/ppermute | solution.py:422
  24.6 0.0 collective-permute-done.1
  24.6 0.1 broadcast_multiply_fusion
  24.7 0.0 copy-done
  24.7 0.0 copy-done.1
  24.7 5.8 %col_pass.2 = f32[16,64,128]{2,1,0:T(8,128)S(1)} custom-call(s32[4,128]{1,0:T(4,128)S(1)} %bitcast.13, s32[128]{0:T(128)S(1)} %bitcast.17, s32[129]{0:T(256)S(1)} %get-tuple-element.37.refs_2_, bf16[128,128,128]{2,1,0:T(8,128)(2,1)S(1)} %get-tuple-element.40.refs_3_, bf16[64,131072]{1,0:T(8,128)(2,1)S(1)} %get-tuple-element.39.refs_4_, ...), custom_call_target="tpu_custom_call" | custom-call | tf_op jit(solution)/shard_map/col_pass/pallas_call | solution.py:360
  30.6 17.0 %all_to_all.20.refs_1_ = f32[16,64,128]{2,1,0:T(8,128)S(1)} all-to-all(f32[16,64,128]{2,1,0:T(8,128)S(1)} %col_pass.2), channel_id=1, replica_groups=mesh['row'=16,'col'=8] {'row'}, dimensions={0} | all-to-all | bytes 1048576 | tf_op jit(solution)/shard_map/all_to_all | solution.py:431
  47.5 0.1 combine.2
  47.7 13.1 %all_to_all.21 = f32[16,64,128]{2,1,0:T(8,128)S(1)} all-to-all(f32[16,64,128]{2,1,0:T(8,128)S(1)} %get-tuple-element.53), channel_id=1, replica_groups=mesh['row'=16,'col'=8] {'row'}, dimensions={0} | all-to-all | bytes 1048576 | tf_op jit(solution)/shard_map/all_to_all | solution.py:431
  60.8 6.1 %row_pass.1 = f32[144,128]{1,0:T(8,128)S(1)} custom-call(s32[4,128]{1,0:T(4,128)S(1)} %bitcast.14, s32[128]{0:T(128)S(1)} %bitcast.18, s32[129]{0:T(256)S(1)} %get-tuple-element.37.refs_2_, bf16[128,128,128]{2,1,0:T(8,128)(2,1)S(1)} %get-tuple-element.38.refs_3_, bf16[64,131072]{1,0:T(8,128)(2,1)S(1)} %get-tuple-element.39.refs_4_, ...), custom_call_target="tpu_custom_call" | custom-call | tf_op jit(solution)/shard_map/row_pass/pallas_call | solution.py:340
  66.9 0.1 collective-permute-start.4
  67.0 1.3 %collective-permute-done.4 = f32[144,128]{1,0:T(8,128)S(1)} collective-permute-done((f32[144,128]{1,0:T(8,128)S(1)}, f32[144,128]{1,0:T(8,128)S(1)}, u32[]{:S(2)}, u32[]{:S(2)}) %collective-permute-start.4) | collective-permute-done | bytes 73760 | tf_op jit(solution)/shard_map/ppermute | solution.py:422
  68.3 1.9 %collective-permute-start.7 = (f32[144,128]{1,0:T(8,128)S(1)}, f32[144,128]{1,0:T(8,128)S(1)}, u32[]{:S(2)}, u32[]{:S(2)}) collective-permute-start(f32[144,128]{1,0:T(8,128)S(1)} %multiply_add_fusion.1), channel_id=1, source_target_pairs={{0,6},{1,7},{2,4},{3,5},{4,2},{5,3},{6,0},{7,1},{8,14},{9,15},{10,... | collective-permute-start | bytes 221192 | tf_op jit(solution)/shard_map/ppermute | solution.py:422
  70.2 0.5 collective-permute-start.6
  70.6 1.9 %collective-permute-start.5 = (f32[144,128]{1,0:T(8,128)S(1)}, f32[144,128]{1,0:T(8,128)S(1)}, u32[]{:S(2)}, u32[]{:S(2)}) collective-permute-start(f32[144,128]{1,0:T(8,128)S(1)} %multiply_add_fusion.1), channel_id=1, source_target_pairs={{0,2},{1,3},{2,0},{3,1},{4,6},{5,7},{6,4},{7,5},{8,10},{9,11},{10,... | collective-permute-start | bytes 221192 | tf_op jit(solution)/shard_map/ppermute | solution.py:422
  72.5 1.5 %collective-permute-done.7 = f32[144,128]{1,0:T(8,128)S(1)} collective-permute-done((f32[144,128]{1,0:T(8,128)S(1)}, f32[144,128]{1,0:T(8,128)S(1)}, u32[]{:S(2)}, u32[]{:S(2)}) %collective-permute-start.7) | collective-permute-done | bytes 73760 | tf_op jit(solution)/shard_map/ppermute | solution.py:422
  74.0 2.6 %collective-permute-done.6 = f32[144,128]{1,0:T(8,128)S(1)} collective-permute-done((f32[144,128]{1,0:T(8,128)S(1)}, f32[144,128]{1,0:T(8,128)S(1)}, u32[]{:S(2)}, u32[]{:S(2)}) %collective-permute-start.6) | collective-permute-done | bytes 73760 | tf_op jit(solution)/shard_map/ppermute | solution.py:422
  76.5 0.0 collective-permute-done.5
  76.5 0.1 multiply_add_fusion
  76.6 5.9 %col_pass.3 = (f32[16,64,128]{2,1,0:T(8,128)S(1)}, f32[128,128]{1,0:T(8,128)}) custom-call(s32[4,128]{1,0:T(4,128)S(1)} %bitcast.15, s32[128]{0:T(128)S(1)} %bitcast.19, s32[129]{0:T(256)S(1)} %get-tuple-element.37.refs_2_, bf16[128,128,128]{2,1,0:T(8,128)(2,1)S(1)} %get-tuple-element.38.refs_3_, bf16[64,131072]{1,0:T(8,128)(2,1)S(1)} %get-tuple-element.39.refs_4_, ...), custom_call_target="tpu_custom_call" | custom-call | tf_op jit(solution)/shard_map/col_pass/pallas_call | solution.py:360
  82.5 13.1 %all_to_all.22.refs_1_ = f32[16,64,128]{2,1,0:T(8,128)S(1)} all-to-all(f32[16,64,128]{2,1,0:T(8,128)S(1)} %get-tuple-element.63), channel_id=1, replica_groups=mesh['row'=16,'col'=8] {'row'}, dimensions={0} | all-to-all | bytes 1048576 | tf_op jit(solution)/shard_map/all_to_all | solution.py:431
  95.6 0.1 combine.3
  95.8 13.1 %all_to_all.23 = f32[16,64,128]{2,1,0:T(8,128)S(1)} all-to-all(f32[16,64,128]{2,1,0:T(8,128)S(1)} %combine.3), channel_id=1, replica_groups=mesh['row'=16,'col'=8] {'row'}, dimensions={0} | all-to-all | bytes 1048576 | tf_op jit(solution)/shard_map/all_to_all | solution.py:479
  108.9 0.8 copy.9
  (4 shorter events, 0.1 us)
Async XLA Ops:
  0.6 24.1 %copy-start = (s32[128,1,4]{0,2,1:T(4,128)S(1)}, s32[128,1,4]{0,2,1:T(4,128)}, u32[]{:S(2)}) copy-start(s32[128,1,4]{0,2,1:T(4,128)} %param.10) | copy-start | bytes 6148
  0.6 24.1 %copy-start.1 = (s32[128,1]{0,1:T(1,128)S(1)}, s32[128,1]{0,1:T(1,128)}, u32[]{:S(2)}) copy-start(s32[128,1]{0,1:T(1,128)} %param.11) | copy-start | bytes 1540
  13.0 1.3 %collective-permute-start = (f32[128,128]{1,0:T(8,128)S(1)}, f32[128,128]{1,0:T(8,128)S(1)}, u32[]{:S(2)}, u32[]{:S(2)}) collective-permute-start(f32[128,128]{1,0:T(8,128)S(1)} %get-tuple-element.42), channel_id=1, source_target_pairs={{0,1},{1,0},{2,3},{3,2},{4,5},{5,4},{6,7},{7,6},{8,9},{9,8},{10,11... | collective-permute-start | bytes 196616 | tf_op jit(solution)/shard_map/ppermute | solution.py:422
  14.3 7.3 %collective-permute-start.3 = (f32[128,128]{1,0:T(8,128)S(1)}, f32[128,128]{1,0:T(8,128)S(1)}, u32[]{:S(2)}, u32[]{:S(2)}) collective-permute-start(f32[128,128]{1,0:T(8,128)S(1)} %multiply_add_fusion.2), channel_id=1, source_target_pairs={{0,6},{1,7},{2,4},{3,5},{4,2},{5,3},{6,0},{7,1},{8,14},{9,15},{10,... | collective-permute-start | bytes 196616 | tf_op jit(solution)/shard_map/ppermute | solution.py:422
  18.5 6.1 %collective-permute-start.2 = (f32[128,128]{1,0:T(8,128)S(1)}, f32[128,128]{1,0:T(8,128)S(1)}, u32[]{:S(2)}, u32[]{:S(2)}) collective-permute-start(f32[128,128]{1,0:T(8,128)S(1)} %multiply_add_fusion.2), channel_id=1, source_target_pairs={{0,4},{1,5},{2,6},{3,7},{4,0},{5,1},{6,2},{7,3},{8,12},{9,13},{10,... | collective-permute-start | bytes 196616 | tf_op jit(solution)/shard_map/ppermute | solution.py:422
  18.5 6.1 %collective-permute-start.1 = (f32[128,128]{1,0:T(8,128)S(1)}, f32[128,128]{1,0:T(8,128)S(1)}, u32[]{:S(2)}, u32[]{:S(2)}) collective-permute-start(f32[128,128]{1,0:T(8,128)S(1)} %multiply_add_fusion.2), channel_id=1, source_target_pairs={{0,2},{1,3},{2,0},{3,1},{4,6},{5,7},{6,4},{7,5},{8,10},{9,11},{10,... | collective-permute-start | bytes 196616 | tf_op jit(solution)/shard_map/ppermute | solution.py:422
  66.9 1.3 %collective-permute-start.4 = (f32[144,128]{1,0:T(8,128)S(1)}, f32[144,128]{1,0:T(8,128)S(1)}, u32[]{:S(2)}, u32[]{:S(2)}) collective-permute-start(f32[144,128]{1,0:T(8,128)S(1)} %row_pass.1), channel_id=1, source_target_pairs={{0,1},{1,0},{2,3},{3,2},{4,5},{5,4},{6,7},{7,6},{8,9},{9,8},{10,11... | collective-permute-start | bytes 221192 | tf_op jit(solution)/shard_map/ppermute | solution.py:422
  68.3 5.6 %collective-permute-start.7 = (f32[144,128]{1,0:T(8,128)S(1)}, f32[144,128]{1,0:T(8,128)S(1)}, u32[]{:S(2)}, u32[]{:S(2)}) collective-permute-start(f32[144,128]{1,0:T(8,128)S(1)} %multiply_add_fusion.1), channel_id=1, source_target_pairs={{0,6},{1,7},{2,4},{3,5},{4,2},{5,3},{6,0},{7,1},{8,14},{9,15},{10,... | collective-permute-start | bytes 221192 | tf_op jit(solution)/shard_map/ppermute | solution.py:422
  70.2 6.3 %collective-permute-start.6 = (f32[144,128]{1,0:T(8,128)S(1)}, f32[144,128]{1,0:T(8,128)S(1)}, u32[]{:S(2)}, u32[]{:S(2)}) collective-permute-start(f32[144,128]{1,0:T(8,128)S(1)} %multiply_add_fusion.1), channel_id=1, source_target_pairs={{0,4},{1,5},{2,6},{3,7},{4,0},{5,1},{6,2},{7,3},{8,12},{9,13},{10,... | collective-permute-start | bytes 221192 | tf_op jit(solution)/shard_map/ppermute | solution.py:422
  70.6 5.9 %collective-permute-start.5 = (f32[144,128]{1,0:T(8,128)S(1)}, f32[144,128]{1,0:T(8,128)S(1)}, u32[]{:S(2)}, u32[]{:S(2)}) collective-permute-start(f32[144,128]{1,0:T(8,128)S(1)} %multiply_add_fusion.1), channel_id=1, source_target_pairs={{0,2},{1,3},{2,0},{3,1},{4,6},{5,7},{6,4},{7,5},{8,10},{9,11},{10,... | collective-permute-start | bytes 221192 | tf_op jit(solution)/shard_map/ppermute | solution.py:422

commit v11 on v10

--- a/solution.py
+++ b/solution.py
@@ -159,6 +159,22 @@
                 source_block(group * beside + k)
 
 
+def start_lists(sources, targets, sems):
+    copies = [
+        pltpu.make_async_copy(source, target, sems.at[i])
+        for i, (source, target) in enumerate(zip(sources, targets))
+    ]
+    for copy in copies:
+        copy.start()
+    return copies
+
+
+def list_scratch(lists):
+    return [pltpu.SMEM(v.shape, v.dtype) for v in lists] + [
+        pltpu.SemaphoreType.DMA((len(lists),))
+    ]
+
+
 def row_pass_kernel(kappa, slots, *refs):
     if kappa is not None:
         (cols_hbm, counts_hbm, a_hbm, b_hbm, x_hbm, y_hbm, out_ref, x_ref, x2_ref,
@@ -175,8 +191,15 @@
                 y_sem, others, masses, lambda: make_order(order, counts, total.shape[1], slots))
         offset = 0.0
     else:
-        (cols, counts, order, x_ref, y_ref, f_ref, g_ref, g_first_ref, b_ref, mass_ref, out_ref,
-         total) = refs
+        (*lists, x_ref, y_ref, f_ref, g_ref, g_first_ref, b_ref, mass_ref, out_ref, total, cols,
+         counts, order, list_sems) = refs
+        lists = start_lists(lists, (cols, counts, order), list_sems)
+        blocks = total.shape[1]
+        out_ref[blocks : blocks + 8, :] = mass_ref[...]
+        last = g_first_ref[...] + b_ref[...] - 0.5 * g_ref[...]
+        out_ref[blocks + 8 :, :] = log2_sum(jnp.exp2(last))
+        for copy in lists:
+            copy.wait()
         offset = ROW_OFFSET
     blocks = total.shape[1]
     lane = lax.broadcasted_iota(jnp.int32, (TILE, TILE), 1)
@@ -201,10 +224,6 @@
         mass_ref[...] = log2_sum(b_ref[...])
         a_ref[...] = jnp.log2(a_ref[...])
         b_ref[...] = jnp.log2(b_ref[...])
-    else:
-        out_ref[blocks : blocks + 8, :] = mass_ref[...]
-        last = g_first_ref[...] + b_ref[...] - 0.5 * g_ref[...]
-        out_ref[blocks + 8 :, :] = log2_sum(jnp.exp2(last))
     fine = jnp.logical_and(jnp.min(sums) >= SMALLEST, jnp.max(sums) <= LARGEST)
 
     @pl.when(jnp.logical_not(fine))
@@ -319,7 +338,7 @@
             shape((blocks, TILE), f32),
             shape((target_blocks, TILE), f32),
             shape((8, TILE), f32),
-            shape((blocks + 1,), jnp.int32),
+            shape((2 * blocks,), jnp.int32),
         ),
         in_specs=[ANY()] * 6,
         out_specs=(VMEM(),) * 9 + (SMEM(),),
@@ -340,9 +359,9 @@
     return pl.pallas_call(
         functools.partial(row_pass_kernel, None, slots),
         out_shape=jax.ShapeDtypeStruct((f_pot.shape[0] + 16, TILE), jnp.float32),
-        in_specs=[SMEM()] * 3 + [VMEM()] * 7,
+        in_specs=[ANY()] * 3 + [VMEM()] * 7,
         out_specs=VMEM(),
-        scratch_shapes=[pltpu.VMEM((TILE, f_pot.shape[0]), jnp.float32)],
+        scratch_shapes=[pltpu.VMEM((TILE, f_pot.shape[0]), jnp.float32), *list_scratch(lists)],
         name="row_pass",
         compiler_params=pltpu.CompilerParams(vmem_limit_bytes=VMEM_LIMIT),
     )(*lists, x, y, f_pot, g_pot, g_first, log_b, mass)

time: 110 us -> 110 us (level)
  no operation moved by 1% of the time
where the time goes in v11:
time: 110 us
  blocking collectives  56.4 us (51%)
  Pallas kernels  30.4 us (28%)
  waiting for transfers between devices  11.7 us (11%)
  starting transfers between devices  9.47 us (9%)
    all_to_all x3, blocking collectives, exchange(): return lax.optimization_barrier((lax.all_to_all(blocks, 'row', 0, 0), rest))  43.2 us
    all_to_all x1, blocking collectives, body(): target = lax.all_to_all(send, 'row', 0, 0)  13.1 us
    pallas_call x1, Pallas kernels, first_row_pass(): pl.pallas_call(functools.partial(row_pass_kernel, LOG2E / first_epsilon,...  12.3 us
    pallas_call x2, Pallas kernels, col_pass(): pl.pallas_call(functools.partial(col_pass_kernel, slots, scales), out_sha...  11.7 us
    ppermute x8, waiting for transfers between devices, moved(): return lax.ppermute(value, 'col', pairs)  11.7 us
    ppermute x8, starting transfers between devices, moved(): return lax.ppermute(value, 'col', pairs)  9.47 us
    pallas_call x1, Pallas kernels, row_pass(): pl.pallas_call(functools.partial(row_pass_kernel, None, slots), out_shape...  6.18 us
  transfers between devices with their start and end apart: 8, of which 6 were waited for; matrix products, arithmetic and copies ran while one was open for 0% of the time, Pallas kernels for 0%

profile of v11, /device:TPU:0, one launch (start us, length us, event | category | flops | bytes accessed | tf_op | source)
XLA Modules:
  0.0 109.8 jit_solution(2834576159223679793)
XLA Ops:
  0.6 0.0 copy-start
  0.6 0.0 copy-start.1
  0.7 12.3 %row_pass_first.1 = (f32[128,128]{1,0:T(8,128)S(1)}, bf16[128,128,128]{2,1,0:T(8,128)(2,1)S(1)}, bf16[128,128,128]{2,1,0:T(8,128)(2,1)S(1)}, bf16[64,131072]{1,0...) custom-call(s32[4,128]{1,0:T(4,128)} %bitcast.12, ...), custom_call_target="tpu_custom_call" | custom-call | tf_op jit(solution)/shard_map/row_pass_first/pallas_call | solution.py:329
  12.9 0.1 collective-permute-start
  13.0 1.2 %collective-permute-done = f32[128,128]{1,0:T(8,128)S(1)} collective-permute-done((f32[128,128]{1,0:T(8,128)S(1)}, f32[128,128]{1,0:T(8,128)S(1)}, u32[]{:S(2)}, u32[]{:S(2)}) %collective-permute-start) | collective-permute-done | bytes 65568 | tf_op jit(solution)/shard_map/ppermute | solution.py:441
  14.3 4.2 %collective-permute-start.3 = (f32[128,128]{1,0:T(8,128)S(1)}, f32[128,128]{1,0:T(8,128)S(1)}, u32[]{:S(2)}, u32[]{:S(2)}) collective-permute-start(f32[128,128]{1,0:T(8,128)S(1)} %multiply_add_fusion.2), channel_id=1, source_target_pairs={{0,6},{1,7},{2,4},{3,5},{4,2},{5,3},{6,0},{7,1},{8,14},{9,15},{10,... | collective-permute-start | bytes 196616 | tf_op jit(solution)/shard_map/ppermute | solution.py:441
  18.5 0.0 collective-permute-start.2
  18.5 0.9 collective-permute-start.1
  19.5 2.2 %collective-permute-done.3 = f32[128,128]{1,0:T(8,128)S(1)} collective-permute-done((f32[128,128]{1,0:T(8,128)S(1)}, f32[128,128]{1,0:T(8,128)S(1)}, u32[]{:S(2)}, u32[]{:S(2)}) %collective-permute-start.3) | collective-permute-done | bytes 65568 | tf_op jit(solution)/shard_map/ppermute | solution.py:441
  21.6 3.0 %collective-permute-done.2 = f32[128,128]{1,0:T(8,128)S(1)} collective-permute-done((f32[128,128]{1,0:T(8,128)S(1)}, f32[128,128]{1,0:T(8,128)S(1)}, u32[]{:S(2)}, u32[]{:S(2)}) %collective-permute-start.2) | collective-permute-done | bytes 65568 | tf_op jit(solution)/shard_map/ppermute | solution.py:441
  24.6 0.0 collective-permute-done.1
  24.6 0.1 broadcast_multiply_fusion
  24.7 0.0 copy-done
  24.7 0.0 copy-done.1
  24.7 5.8 %col_pass.2 = f32[16,64,128]{2,1,0:T(8,128)S(1)} custom-call(s32[4,128]{1,0:T(4,128)S(1)} %bitcast.13, s32[128]{0:T(128)S(1)} %bitcast.17, s32[256]{0:T(256)S(1)} %get-tuple-element.37.refs_2_, bf16[128,128,128]{2,1,0:T(8,128)(2,1)S(1)} %get-tuple-element.40.refs_3_, bf16[64,131072]{1,0:T(8,128)(2,1)S(1)} %get-tuple-element.39.refs_4_, ...), custom_call_target="tpu_custom_call" | custom-call | tf_op jit(solution)/shard_map/col_pass/pallas_call | solution.py:379
  30.5 17.0 %all_to_all.20.refs_1_ = f32[16,64,128]{2,1,0:T(8,128)S(1)} all-to-all(f32[16,64,128]{2,1,0:T(8,128)S(1)} %col_pass.2), channel_id=1, replica_groups=mesh['row'=16,'col'=8] {'row'}, dimensions={0} | all-to-all | bytes 1048576 | tf_op jit(solution)/shard_map/all_to_all | solution.py:450
  47.5 0.1 combine.2
  47.7 13.1 %all_to_all.21 = f32[16,64,128]{2,1,0:T(8,128)S(1)} all-to-all(f32[16,64,128]{2,1,0:T(8,128)S(1)} %get-tuple-element.53), channel_id=1, replica_groups=mesh['row'=16,'col'=8] {'row'}, dimensions={0} | all-to-all | bytes 1048576 | tf_op jit(solution)/shard_map/all_to_all | solution.py:450
  60.8 6.2 %row_pass.1 = f32[144,128]{1,0:T(8,128)S(1)} custom-call(s32[4,128]{1,0:T(4,128)S(1)} %bitcast.14, s32[128]{0:T(128)S(1)} %bitcast.18, s32[256]{0:T(256)S(1)} %get-tuple-element.37.refs_2_, bf16[128,128,128]{2,1,0:T(8,128)(2,1)S(1)} %get-tuple-element.38.refs_3_, bf16[64,131072]{1,0:T(8,128)(2,1)S(1)} %get-tuple-element.39.refs_4_, ...), custom_call_target="tpu_custom_call" | custom-call | tf_op jit(solution)/shard_map/row_pass/pallas_call | solution.py:359
  67.0 0.1 collective-permute-start.4
  67.1 1.3 %collective-permute-done.4 = f32[144,128]{1,0:T(8,128)S(1)} collective-permute-done((f32[144,128]{1,0:T(8,128)S(1)}, f32[144,128]{1,0:T(8,128)S(1)}, u32[]{:S(2)}, u32[]{:S(2)}) %collective-permute-start.4) | collective-permute-done | bytes 73760 | tf_op jit(solution)/shard_map/ppermute | solution.py:441
  68.4 1.9 %collective-permute-start.7 = (f32[144,128]{1,0:T(8,128)S(1)}, f32[144,128]{1,0:T(8,128)S(1)}, u32[]{:S(2)}, u32[]{:S(2)}) collective-permute-start(f32[144,128]{1,0:T(8,128)S(1)} %multiply_add_fusion.1), channel_id=1, source_target_pairs={{0,6},{1,7},{2,4},{3,5},{4,2},{5,3},{6,0},{7,1},{8,14},{9,15},{10,... | collective-permute-start | bytes 221192 | tf_op jit(solution)/shard_map/ppermute | solution.py:441
  70.3 0.5 collective-permute-start.6
  70.7 1.9 %collective-permute-start.5 = (f32[144,128]{1,0:T(8,128)S(1)}, f32[144,128]{1,0:T(8,128)S(1)}, u32[]{:S(2)}, u32[]{:S(2)}) collective-permute-start(f32[144,128]{1,0:T(8,128)S(1)} %multiply_add_fusion.1), channel_id=1, source_target_pairs={{0,2},{1,3},{2,0},{3,1},{4,6},{5,7},{6,4},{7,5},{8,10},{9,11},{10,... | collective-permute-start | bytes 221192 | tf_op jit(solution)/shard_map/ppermute | solution.py:441
  72.6 1.5 %collective-permute-done.7 = f32[144,128]{1,0:T(8,128)S(1)} collective-permute-done((f32[144,128]{1,0:T(8,128)S(1)}, f32[144,128]{1,0:T(8,128)S(1)}, u32[]{:S(2)}, u32[]{:S(2)}) %collective-permute-start.7) | collective-permute-done | bytes 73760 | tf_op jit(solution)/shard_map/ppermute | solution.py:441
  74.0 2.6 %collective-permute-done.6 = f32[144,128]{1,0:T(8,128)S(1)} collective-permute-done((f32[144,128]{1,0:T(8,128)S(1)}, f32[144,128]{1,0:T(8,128)S(1)}, u32[]{:S(2)}, u32[]{:S(2)}) %collective-permute-start.6) | collective-permute-done | bytes 73760 | tf_op jit(solution)/shard_map/ppermute | solution.py:441
  76.6 0.0 collective-permute-done.5
  76.6 0.1 multiply_add_fusion
  76.7 5.9 %col_pass.3 = (f32[16,64,128]{2,1,0:T(8,128)S(1)}, f32[128,128]{1,0:T(8,128)}) custom-call(s32[4,128]{1,0:T(4,128)S(1)} %bitcast.15, s32[128]{0:T(128)S(1)} %bitcast.19, s32[256]{0:T(256)S(1)} %get-tuple-element.37.refs_2_, bf16[128,128,128]{2,1,0:T(8,128)(2,1)S(1)} %get-tuple-element.38.refs_3_, bf16[64,131072]{1,0:T(8,128)(2,1)S(1)} %get-tuple-element.39.refs_4_, ...), custom_call_target="tpu_custom_call" | custom-call | tf_op jit(solution)/shard_map/col_pass/pallas_call | solution.py:379
  82.6 13.1 %all_to_all.22.refs_1_ = f32[16,64,128]{2,1,0:T(8,128)S(1)} all-to-all(f32[16,64,128]{2,1,0:T(8,128)S(1)} %get-tuple-element.63), channel_id=1, replica_groups=mesh['row'=16,'col'=8] {'row'}, dimensions={0} | all-to-all | bytes 1048576 | tf_op jit(solution)/shard_map/all_to_all | solution.py:450
  95.7 0.1 combine.3
  95.8 13.1 %all_to_all.23 = f32[16,64,128]{2,1,0:T(8,128)S(1)} all-to-all(f32[16,64,128]{2,1,0:T(8,128)S(1)} %combine.3), channel_id=1, replica_groups=mesh['row'=16,'col'=8] {'row'}, dimensions={0} | all-to-all | bytes 1048576 | tf_op jit(solution)/shard_map/all_to_all | solution.py:498
  109.0 0.8 copy.9
  (4 shorter events, 0.1 us)
Async XLA Ops:
  0.6 24.0 %copy-start = (s32[128,1,4]{0,2,1:T(4,128)S(1)}, s32[128,1,4]{0,2,1:T(4,128)}, u32[]{:S(2)}) copy-start(s32[128,1,4]{0,2,1:T(4,128)} %param.10) | copy-start | bytes 6148
  0.6 24.0 %copy-start.1 = (s32[128,1]{0,1:T(1,128)S(1)}, s32[128,1]{0,1:T(1,128)}, u32[]{:S(2)}) copy-start(s32[128,1]{0,1:T(1,128)} %param.11) | copy-start | bytes 1540
  12.9 1.3 %collective-permute-start = (f32[128,128]{1,0:T(8,128)S(1)}, f32[128,128]{1,0:T(8,128)S(1)}, u32[]{:S(2)}, u32[]{:S(2)}) collective-permute-start(f32[128,128]{1,0:T(8,128)S(1)} %get-tuple-element.42), channel_id=1, source_target_pairs={{0,1},{1,0},{2,3},{3,2},{4,5},{5,4},{6,7},{7,6},{8,9},{9,8},{10,11... | collective-permute-start | bytes 196616 | tf_op jit(solution)/shard_map/ppermute | solution.py:441
  14.3 7.3 %collective-permute-start.3 = (f32[128,128]{1,0:T(8,128)S(1)}, f32[128,128]{1,0:T(8,128)S(1)}, u32[]{:S(2)}, u32[]{:S(2)}) collective-permute-start(f32[128,128]{1,0:T(8,128)S(1)} %multiply_add_fusion.2), channel_id=1, source_target_pairs={{0,6},{1,7},{2,4},{3,5},{4,2},{5,3},{6,0},{7,1},{8,14},{9,15},{10,... | collective-permute-start | bytes 196616 | tf_op jit(solution)/shard_map/ppermute | solution.py:441
  18.5 6.1 %collective-permute-start.2 = (f32[128,128]{1,0:T(8,128)S(1)}, f32[128,128]{1,0:T(8,128)S(1)}, u32[]{:S(2)}, u32[]{:S(2)}) collective-permute-start(f32[128,128]{1,0:T(8,128)S(1)} %multiply_add_fusion.2), channel_id=1, source_target_pairs={{0,4},{1,5},{2,6},{3,7},{4,0},{5,1},{6,2},{7,3},{8,12},{9,13},{10,... | collective-permute-start | bytes 196616 | tf_op jit(solution)/shard_map/ppermute | solution.py:441
  18.5 6.1 %collective-permute-start.1 = (f32[128,128]{1,0:T(8,128)S(1)}, f32[128,128]{1,0:T(8,128)S(1)}, u32[]{:S(2)}, u32[]{:S(2)}) collective-permute-start(f32[128,128]{1,0:T(8,128)S(1)} %multiply_add_fusion.2), channel_id=1, source_target_pairs={{0,2},{1,3},{2,0},{3,1},{4,6},{5,7},{6,4},{7,5},{8,10},{9,11},{10,... | collective-permute-start | bytes 196616 | tf_op jit(solution)/shard_map/ppermute | solution.py:441
  67.0 1.3 %collective-permute-start.4 = (f32[144,128]{1,0:T(8,128)S(1)}, f32[144,128]{1,0:T(8,128)S(1)}, u32[]{:S(2)}, u32[]{:S(2)}) collective-permute-start(f32[144,128]{1,0:T(8,128)S(1)} %row_pass.1), channel_id=1, source_target_pairs={{0,1},{1,0},{2,3},{3,2},{4,5},{5,4},{6,7},{7,6},{8,9},{9,8},{10,11... | collective-permute-start | bytes 221192 | tf_op jit(solution)/shard_map/ppermute | solution.py:441
  68.4 5.6 %collective-permute-start.7 = (f32[144,128]{1,0:T(8,128)S(1)}, f32[144,128]{1,0:T(8,128)S(1)}, u32[]{:S(2)}, u32[]{:S(2)}) collective-permute-start(f32[144,128]{1,0:T(8,128)S(1)} %multiply_add_fusion.1), channel_id=1, source_target_pairs={{0,6},{1,7},{2,4},{3,5},{4,2},{5,3},{6,0},{7,1},{8,14},{9,15},{10,... | collective-permute-start | bytes 221192 | tf_op jit(solution)/shard_map/ppermute | solution.py:441
  70.3 6.3 %collective-permute-start.6 = (f32[144,128]{1,0:T(8,128)S(1)}, f32[144,128]{1,0:T(8,128)S(1)}, u32[]{:S(2)}, u32[]{:S(2)}) collective-permute-start(f32[144,128]{1,0:T(8,128)S(1)} %multiply_add_fusion.1), channel_id=1, source_target_pairs={{0,4},{1,5},{2,6},{3,7},{4,0},{5,1},{6,2},{7,3},{8,12},{9,13},{10,... | collective-permute-start | bytes 221192 | tf_op jit(solution)/shard_map/ppermute | solution.py:441
  70.7 5.9 %collective-permute-start.5 = (f32[144,128]{1,0:T(8,128)S(1)}, f32[144,128]{1,0:T(8,128)S(1)}, u32[]{:S(2)}, u32[]{:S(2)}) collective-permute-start(f32[144,128]{1,0:T(8,128)S(1)} %multiply_add_fusion.1), channel_id=1, source_target_pairs={{0,2},{1,3},{2,0},{3,1},{4,6},{5,7},{6,4},{7,5},{8,10},{9,11},{10,... | collective-permute-start | bytes 221192 | tf_op jit(solution)/shard_map/ppermute | solution.py:441
